TPU v7x, 32 devices: a whole 2x2x4 slice. The times are simulated.
32 devices in a mesh: lat: 4 (over y, core), lon: 8 (over z, x).
Axes of the slice: x: 2, y: 2, z: 4, core: 2. Of those that a mesh axis runs over, the one named last changes fastest.
Arguments:
- features: bfloat16 [128, 64, 1024], P('lat', 'lon'), may hold values from -18 to 18
- depth_kernel: bfloat16 [7, 7, 1024], replicated, may hold values from -0.875 to 0.875
- depth_bias: float32 [1024], replicated, may hold values from -3 to 3
- norm_gain: float32 [1024], replicated, may hold values from 0.1 to 1.9
- norm_bias: float32 [1024], replicated, may hold values from -3 to 3
- up_weight: bfloat16 [1024, 4096], P('lon', 'lat'), may hold values from -0.1875 to 0.1875
- up_bias: float32 [4096], P('lat'), may hold values from -3 to 3
- down_weight: bfloat16 [1024, 4096], P('lon', 'lat'), may hold values from -0.09375 to 0.09375
- down_bias: float32 [1024], replicated, may hold values from -3 to 3
- layer_scale: float32 [1024], replicated, may hold values from 0.3 to 2
Outputs:
- updated: bfloat16 [128, 64, 1024], P('lat', 'lon')
All inputs are finite; a program needn't handle non-finite values.
Results may differ from a plain program's by a relative error of at most 0.0085.
Values may be sent and summed in bfloat16 or wider, within the bound.
No kernel may reach another device: no remote copies, remote signals or barrier semaphores. Data moves between devices by JAX's collectives and lax.ppermute only.
A program may use at most 64 MiB of HBM per device.

v0:
```python
import jax
import jax.numpy as jnp
from jax import lax
from jax.sharding import PartitionSpec as P


def with_halo(block, sides, width, periodic):
    for axis, dim in sides:
        count = lax.axis_size(axis)
        forward = [(i, i + 1) for i in range(count - 1)]
        if periodic:
            forward.append((count - 1, 0))
        backward = [(target, source) for source, target in forward]
        low = lax.ppermute(
            lax.slice_in_dim(block, block.shape[dim] - width, None, axis=dim), axis, forward
        )
        high = lax.ppermute(lax.slice_in_dim(block, 0, width, axis=dim), axis, backward)
        block = jnp.concatenate([low, block, high], axis=dim)
    return block


def local(
    features,
    depth_kernel,
    depth_bias,
    norm_gain,
    norm_bias,
    up_weight,
    up_bias,
    down_weight,
    down_bias,
    layer_scale,
):
    row_count, col_count, chan_count = features.shape
    circled = with_halo(features, (("lon", 1),), 3, True)
    padded = with_halo(circled, (("lat", 0),), 3, False)
    kernel = depth_kernel.astype(jnp.float32)
    total = jnp.zeros((row_count, col_count, chan_count), jnp.float32) + depth_bias
    for row_off in range(7):
        for col_off in range(7):
            window = padded[row_off : row_off + row_count, col_off : col_off + col_count].astype(
                jnp.float32
            )
            total = total + window * kernel[row_off, col_off]
    centre = jnp.mean(total, axis=-1, keepdims=True)
    spread = jnp.mean((total - centre) ** 2, axis=-1, keepdims=True)
    normed = ((total - centre) * lax.rsqrt(spread + 1e-06) * norm_gain + norm_bias).astype(
        jnp.bfloat16
    )
    normed = normed.reshape(row_count * col_count, chan_count)
    gathered = lax.all_gather(normed, "lat", axis=0, tiled=True)
    pre = (
        jnp.dot(
            gathered,
            lax.all_gather(up_weight, "lon", axis=0, tiled=True),
            preferred_element_type=jnp.float32,
        )
        + up_bias
    )
    hidden = jax.nn.gelu(pre, approximate=False).astype(jnp.bfloat16)
    partial_out = lax.dot_general(
        hidden,
        lax.all_gather(down_weight, "lon", axis=0, tiled=True),
        (((1,), (1,)), ((), ())),
        preferred_element_type=jnp.float32,
    )
    branch = lax.psum_scatter(
        partial_out.astype(jnp.bfloat16), "lat", scatter_dimension=0, tiled=True
    ).astype(jnp.float32)
    branch = branch.reshape(row_count, col_count, chan_count)
    updated = features.astype(jnp.float32) + layer_scale * (branch + down_bias)
    return updated.astype(jnp.bfloat16)


def solution(mesh):
    placed = (
        P("lat", "lon", None),
        P(),
        P(),
        P(),
        P(),
        P("lon", "lat"),
        P("lat"),
        P("lon", "lat"),
        P(),
        P(),
    )
    return jax.shard_map(
        local, mesh=mesh, in_specs=placed, out_specs=P("lat", "lon", None), check_vma=False
    )
```

profile of v0, /device:TPU:0, one launch (start us, length us, event | category | flops | bytes accessed | tf_op | source)
XLA Modules:
  0.0 223.2 jit_solution(2848432043768450)
XLA Ops:
  6.5 0.0 copy-start
  6.5 0.0 all-gather.4.cloned.1.call-start
  6.5 1.5 fusion.79
  8.0 3.0 %collective-permute-start = (bf16[32,3,1024]{2,1,0:T(4,128)(2,1)S(1)}, bf16[32,3,1024]{2,1,0:T(4,128)(2,1)S(1)}, u32[]{:S(2)}, u32[]{:S(2)}) collective-permute-start(bf16[32,3,1024]{2,1,0:T(4,128)(2,1)S(1)} %get-tuple-element.11), channel_id=1, source_target_pairs={{0,1},{1,2},{2,3},{3,4},{4,5},{5,6},{6,7},{7,0},{8,9},{9,10},{10,1... | collective-permute-start | bytes 589832 | tf_op jit(solution)/shard_map/ppermute | solution.py:14
  11.0 3.1 %collective-permute-start.1 = (bf16[32,3,1024]{2,1,0:T(4,128)(2,1)S(1)}, bf16[32,3,1024]{2,1,0:T(4,128)(2,1)S(1)}, u32[]{:S(2)}, u32[]{:S(2)}) collective-permute-start(bf16[32,3,1024]{2,1,0:T(4,128)(2,1)S(1)} %get-tuple-element.12), channel_id=1, source_target_pairs={{1,0},{2,1},{3,2},{4,3},{5,4},{6,5},{7,6},{0,7},{9,8},{10,9},{11,1... | collective-permute-start | bytes 589832 | tf_op jit(solution)/shard_map/ppermute | solution.py:17
  14.1 1.1 fusion.80
  15.2 1.2 fusion.81
  16.5 1.1 constant_dynamic-update-slice_fusion.1
  17.6 1.1 fusion.82
  18.7 3.5 %collective-permute-done = bf16[32,3,1024]{2,1,0:T(4,128)(2,1)S(1)} collective-permute-done((bf16[32,3,1024]{2,1,0:T(4,128)(2,1)S(1)}, bf16[32,3,1024]{2,1,0:T(4,128)(2,1)S(1)}, u32[]{:S(2)}, u32[]{:S(2)}) %collective-permute-start) | collective-permute-done | bytes 196640 | tf_op jit(solution)/shard_map/ppermute | solution.py:14
  22.2 2.2 collective-permute-done.1
  24.4 0.0 copy-done
  24.4 0.1 pad_maximum_fusion.4
  24.5 1.3 collective-permute-start.2
  25.8 0.0 copy-start.1
  25.8 1.3 collective-permute-start.3
  27.1 0.2 constant_dynamic-update-slice_fusion
  27.3 0.0 collective-permute-done.2
  27.3 3.4 %collective-permute-done.3 = bf16[3,14,1024]{2,1,0:T(8,128)(2,1)S(1)} collective-permute-done((bf16[3,14,1024]{2,1,0:T(8,128)(2,1)S(1)}, bf16[3,14,1024]{2,1,0:T(8,128)(2,1)S(1)}, u32[]{:S(2)}, u32[]{:S(2)}) %collective-permute-start.3) | collective-permute-done | bytes 86048 | tf_op jit(solution)/shard_map/ppermute | solution.py:17
  30.7 0.7 maximum_maximum_fusion
  31.4 0.0 copy-done.1
  31.4 0.0 copy-start.2
  31.4 0.0 copy-start.3
  31.4 9.4 %fusion.77 = (f32[32,8]{1,0:T(8,128)S(1)}, f32[32,8,1024]{2,1,0:T(8,128)S(1)}) fusion(f32[1024]{0:T(1024)S(1)} %bitcast.105, bf16[35,14,1024]{2,1,0:T(8,128)(2,1)S(1)} %get-tuple-element.8, f32[1024]{0:T(1024)S(1)} %bitcast.104, f32[1024]{0:T(1024)S(1)} %bitcast.103, f32[1024]{0:T(1024)S(1)} %bitcast.102, f32[1024]{0:T(1024)S(1)} %bitcast.101, ...), kind=kLoop, calls=%fused_computation.101 | loop fusion | flops 41156352 | bytes 25568256 | tf_op jit(solution)/shard_map/reduce_sum | solution.py:45
  40.9 0.0 copy-start.6
  40.9 0.3 multiply_reduce_fusion
  41.2 0.0 copy-done.2
  41.2 0.0 copy-done.3
  41.2 1.0 fusion.44
  42.2 0.0 all-gather.4.cloned.1.call-update
  42.2 0.0 all-gather.6.cloned.1.call-start
  42.3 0.7 all-gather.6.cloned.1.call-update
  43.0 0.0 all-gather.8.cloned.1.call-start
  43.0 0.7 all-gather.8.cloned.1.call-update
  43.7 0.0 reduce-scatter.2.cloned.1.call-start
  43.8 23.2 %all-gather.4.cloned.1.call-done = bf16[1024,1024]{1,0:T(8,128)(2,1)} async-done(((bf16[256,1024]{1,0:T(8,128)(2,1)}), bf16[1024,1024]{1,0:T(8,128)(2,1)}) %all-gather.4.cloned.1.call-update) | async-done | bytes 2097168 | tf_op jit(solution)/shard_map/all_gather | solution.py:51
  67.0 51.4 %all-gather.6.cloned.1.call-done = bf16[1024,1024]{1,0:T(8,128)(2,1)} async-done(((bf16[128,1024]{1,0:T(8,128)(2,1)}), bf16[1024,1024]{1,0:T(8,128)(2,1)}) %all-gather.6.cloned.1.call-update) | async-done | bytes 2097168 | tf_op jit(solution)/shard_map/all_gather | solution.py:55
  118.4 49.9 %all-gather.8.cloned.1.call-done = bf16[1024,1024]{1,0:T(8,128)(2,1)} async-done(((bf16[128,1024]{1,0:T(8,128)(2,1)}), bf16[1024,1024]{1,0:T(8,128)(2,1)}) %all-gather.8.cloned.1.call-update) | async-done | bytes 2097168 | tf_op jit(solution)/shard_map/all_gather | solution.py:63
  168.3 0.0 copy-done.6
  168.4 16.2 %fusion.14 = bf16[1024,1024]{1,0:T(8,128)(2,1)} fusion(bf16[1024,1024]{1,0:T(8,128)(2,1)} %all-gather.8.cloned.1.call-done, f32[1024]{0:T(1024)S(1)} %copy-done.6, bf16[1024,1024]{1,0:T(8,128)(2,1)} %all-gather.4.cloned.1.call-done, bf16[1024,1024]{1,0:T(8,128)(2,1)} %all-gather.6.cloned.1.call-done), kind=kOutput, calls=%fused_computation.21 | convolution fusion | flops 4365221888 | bytes 8392704 | tf_op jit(solution)/shard_map/dot_general | solution.py:61
  184.5 0.0 copy-start.4
  184.5 0.0 copy-start.5
  184.5 0.0 reduce-scatter.2.cloned.1.call-update
  184.5 30.1 %reduce-scatter.2.cloned.1.call-done = bf16[256,1024]{1,0:T(8,128)(2,1)} async-done(((bf16[1024,1024]{1,0:T(8,128)(2,1)}), bf16[256,1024]{1,0:T(8,128)(2,1)}) %reduce-scatter.2.cloned.1.call-update) | async-done | bytes 524304 | tf_op jit(solution)/shard_map/reduce_scatter | solution.py:67
  214.6 0.0 copy-done.4
  214.6 0.0 copy-done.5
  214.6 2.0 fusion.42
  (2 shorter events, 0.0 us)
Async XLA Ops:
  6.5 17.9 %copy-start = (bf16[32,8,1024]{2,1,0:T(8,128)(2,1)S(1)}, bf16[32,8,1024]{2,1,0:T(8,128)(2,1)}, u32[]{:S(2)}) copy-start(bf16[32,8,1024]{2,1,0:T(8,128)(2,1)} %param.10) | copy-start | bytes 1572868
  6.5 60.4 %all-gather.4.cloned.1.call-start = ((), (), s32[]{:S(2)}) async-start(), calls=%async_computation.1 | async-start | bytes 2621440 | tf_op jit(solution)/shard_map/all_gather | solution.py:51
  8.0 14.2 %collective-permute-start = (bf16[32,3,1024]{2,1,0:T(4,128)(2,1)S(1)}, bf16[32,3,1024]{2,1,0:T(4,128)(2,1)S(1)}, u32[]{:S(2)}, u32[]{:S(2)}) collective-permute-start(bf16[32,3,1024]{2,1,0:T(4,128)(2,1)S(1)} %get-tuple-element.11), channel_id=1, source_target_pairs={{0,1},{1,2},{2,3},{3,4},{4,5},{5,6},{6,7},{7,0},{8,9},{9,10},{10,1... | collective-permute-start | bytes 589832 | tf_op jit(solution)/shard_map/ppermute | solution.py:14
  11.0 13.4 %collective-permute-start.1 = (bf16[32,3,1024]{2,1,0:T(4,128)(2,1)S(1)}, bf16[32,3,1024]{2,1,0:T(4,128)(2,1)S(1)}, u32[]{:S(2)}, u32[]{:S(2)}) collective-permute-start(bf16[32,3,1024]{2,1,0:T(4,128)(2,1)S(1)} %get-tuple-element.12), channel_id=1, source_target_pairs={{1,0},{2,1},{3,2},{4,3},{5,4},{6,5},{7,6},{0,7},{9,8},{10,9},{11,1... | collective-permute-start | bytes 589832 | tf_op jit(solution)/shard_map/ppermute | solution.py:17
  24.5 2.8 %collective-permute-start.2 = (bf16[3,14,1024]{2,1,0:T(8,128)(2,1)S(1)}, bf16[3,14,1024]{2,1,0:T(8,128)(2,1)S(1)}, u32[]{:S(2)}, u32[]{:S(2)}) collective-permute-start(bf16[3,14,1024]{2,1,0:T(8,128)(2,1)S(1)} %get-tuple-element.9), channel_id=1, source_target_pairs={{0,8},{8,16},{16,24},{1,9},{9,17},{17,25},{2,10},{10,18},{18,26},{... | collective-permute-start | bytes 258056 | tf_op jit(solution)/shard_map/ppermute | solution.py:14
  25.8 5.6 %copy-start.1 = (f32[1024]{0:T(1024)S(1)}, f32[1024]{0:T(1024)}, u32[]{:S(2)}) copy-start(f32[1024]{0:T(1024)} %param.12) | copy-start | bytes 12292
  25.8 4.9 %collective-permute-start.3 = (bf16[3,14,1024]{2,1,0:T(8,128)(2,1)S(1)}, bf16[3,14,1024]{2,1,0:T(8,128)(2,1)S(1)}, u32[]{:S(2)}, u32[]{:S(2)}) collective-permute-start(bf16[3,14,1024]{2,1,0:T(8,128)(2,1)S(1)} %get-tuple-element.10), channel_id=1, source_target_pairs={{8,0},{16,8},{24,16},{9,1},{17,9},{25,17},{10,2},{18,10},{26,18},{... | collective-permute-start | bytes 258056 | tf_op jit(solution)/shard_map/ppermute | solution.py:17
  31.4 9.7 %copy-start.2 = (f32[1024]{0:T(1024)S(1)}, f32[1024]{0:T(1024)}, u32[]{:S(2)}) copy-start(f32[1024]{0:T(1024)} %param.14) | copy-start | bytes 12292
  31.4 9.7 %copy-start.3 = (f32[1024]{0:T(1024)S(1)}, f32[1024]{0:T(1024)}, u32[]{:S(2)}) copy-start(f32[1024]{0:T(1024)} %param.13) | copy-start | bytes 12292
  40.9 127.5 %copy-start.6 = (f32[1024]{0:T(1024)S(1)}, f32[1024]{0:T(1024)}, u32[]{:S(2)}) copy-start(f32[1024]{0:T(1024)} %param.16) | copy-start | bytes 12292
  42.2 76.2 %all-gather.6.cloned.1.call-start = ((), (), s32[]{:S(2)}) async-start(), calls=%async_computation.2 | async-start | bytes 2359296 | tf_op jit(solution)/shard_map/all_gather | solution.py:55
  43.0 125.4 %all-gather.8.cloned.1.call-start = ((), (), s32[]{:S(2)}) async-start(), calls=%async_computation.3 | async-start | bytes 2359296 | tf_op jit(solution)/shard_map/all_gather | solution.py:63
  43.7 170.9 %reduce-scatter.2.cloned.1.call-start = ((), (), s32[]{:S(2)}) async-start(), calls=%async_computation.4 | async-start | bytes 2621440 | tf_op jit(solution)/shard_map/reduce_scatter | solution.py:67
  184.5 30.1 %copy-start.4 = (f32[1024]{0:T(1024)S(1)}, f32[1024]{0:T(1024)}, u32[]{:S(2)}) copy-start(f32[1024]{0:T(1024)} %param.18) | copy-start | bytes 12292
  184.5 30.1 %copy-start.5 = (f32[1024]{0:T(1024)S(1)}, f32[1024]{0:T(1024)}, u32[]{:S(2)}) copy-start(f32[1024]{0:T(1024)} %param.19) | copy-start | bytes 12292
Sparse Core Ops, SparseCore 0:
  42.4 24.5 all-gather.3
  69.1 49.2 all-gather.5
  120.5 47.7 all-gather.7
  184.7 29.9 reduce-scatter.1
where the time goes:
time: 224 us; the launch traced here: 223 us
  waiting for transfers between devices  165 us (74%)
  matrix products  16.2 us (7%)
  other arithmetic  13.5 us (6%)
  between operations  13.2 us (6%)
  starting transfers between devices  8.8 us (4%)
  local copies, waits for them, and re-layouts  6.22 us (3%)
    all_gather x1, waiting for transfers between devices, local(): lax.all_gather(up_weight, 'lon', axis=0, tiled=True)  51.4 us
    all_gather x1, waiting for transfers between devices, local(): lax.all_gather(down_weight, 'lon', axis=0, tiled=True)  49.9 us
    reduce_scatter x1, waiting for transfers between devices, local(): lax.psum_scatter(partial_out.astype(jnp.bfloat16), 'lat', scatter_dimensi...  30.1 us
    all_gather x1, waiting for transfers between devices, local(): gathered = lax.all_gather(normed, 'lat', axis=0, tiled=True)  23.2 us
    dot_general x1, matrix products, local(): lax.dot_general(hidden, lax.all_gather(down_weight, 'lon', axis=0, tiled=...  16.2 us
    reduce_sum x1, other arithmetic, local(): centre = jnp.mean(total, axis=-1, keepdims=True)  9.43 us
    ppermute x2, waiting for transfers between devices, with_halo(): lax.ppermute(lax.slice_in_dim(block, 0, width, axis=dim), axis, backward)  5.64 us
  transfers between devices with their start and end apart: 8, of which 7 were waited for; matrix products, arithmetic and copies ran while one was open for 2% of the time, Pallas kernels for 0%

commit v1 on v0

v1 whole, which is shorter than its diff:
```python
import functools

import jax
import jax.numpy as jnp
from jax import lax
from jax.experimental import pallas as pl
from jax.experimental.pallas import tpu as pltpu
from jax.sharding import PartitionSpec as P

F32 = jnp.float32
BF16 = jnp.bfloat16
LANES = 128
VMEM = pl.BlockSpec(memory_space=pltpu.VMEM)
SMEM = pl.BlockSpec(memory_space=pltpu.SMEM)
PARAMS = pltpu.CompilerParams(vmem_limit_bytes=40 * 1024 * 1024)


def shift(value, axis, step, inner):
    count = lax.axis_size(axis)
    return lax.ppermute(value, axis, [(i, (i + step * inner) % count) for i in range(count)])


def swap(value, axis, bit):
    count = lax.axis_size(axis)
    return lax.ppermute(value, axis, [(i, i ^ bit) for i in range(count)])


def edges_kernel(low_ref, mid_ref, high_ref, first_ref, last_ref, slab):
    rows, cols, chans = mid_ref.shape

    @pl.loop(0, chans // LANES)
    def _(chunk):
        lanes = pl.ds(pl.multiple_of(chunk * LANES, LANES), LANES)
        slab[pl.ds(0, 3 * cols), :] = low_ref[:, :, lanes].astype(F32).reshape(3 * cols, LANES)
        slab[pl.ds(3 * cols, rows * cols), :] = mid_ref[:, :, lanes].astype(F32).reshape(rows * cols, LANES)
        slab[pl.ds((3 + rows) * cols, 3 * cols), :] = high_ref[:, :, lanes].astype(F32).reshape(3 * cols, LANES)
        for col in range(3):
            first_ref[col, :, lanes] = slab[pl.ds(col, rows + 6, stride=cols), :].astype(BF16)
            last_ref[col, :, lanes] = slab[pl.ds(cols - 3 + col, rows + 6, stride=cols), :].astype(BF16)


def edges(low, mid, high):
    rows, cols, chans = mid.shape
    shape = jax.ShapeDtypeStruct((3, rows + 6, chans), BF16)
    return pl.pallas_call(
        edges_kernel,
        out_shape=(shape, shape),
        in_specs=[VMEM] * 3,
        out_specs=(VMEM, VMEM),
        scratch_shapes=[pltpu.VMEM(((rows + 6) * cols, LANES), F32)],
        compiler_params=PARAMS,
    )(low, mid, high)


def conv_kernel(
    order_ref, mid_ref, low_ref, high_ref, left_ref, right_ref, taps_ref, bias_ref, gain_ref, shift_ref,
    out_ref, slab, taps, total,
):
    rows, cols, chans = mid_ref.shape
    wide = 16
    block = 16
    taps[pl.ds(0, 49), :] = taps_ref[...].astype(F32)

    def chunk_step(chunk, carry):
        lanes = pl.ds(pl.multiple_of(chunk * LANES, LANES), LANES)
        for row in range(3):
            slab[pl.ds(row * wide + 3, cols), :] = low_ref[row, :, lanes].astype(F32)
            slab[pl.ds((rows + 3 + row) * wide + 3, cols), :] = high_ref[row, :, lanes].astype(F32)
        for row in range(rows):
            slab[pl.ds((row + 3) * wide + 3, cols), :] = mid_ref[row, :, lanes].astype(F32)
        for col in range(3):
            slab[pl.ds(col, rows + 6, stride=wide), :] = left_ref[col, :, lanes].astype(F32)
            slab[pl.ds(cols + 3 + col, rows + 6, stride=wide), :] = right_ref[col, :, lanes].astype(F32)
        for base in range(0, rows, block):
            start = jnp.broadcast_to(bias_ref[:, lanes], (cols, LANES))
            sums = [start] * block
            for b in range(7):
                weights = [jnp.broadcast_to(taps[pl.ds(7 * a + b, 1), lanes], (cols, LANES)) for a in range(7)]
                for row in range(block + 6):
                    window = slab[pl.ds((base + row) * wide + b, cols), :]
                    for a in range(7):
                        if 0 <= row - a < block:
                            sums[row - a] = sums[row - a] + window * weights[a]
            for row in range(block):
                total[pl.ds((base + row) * cols, cols), lanes] = sums[row]
        return carry

    lax.fori_loop(0, chans // LANES, chunk_step, 0)

    step = 64
    for base in range(0, rows * cols, step):
        part = pl.ds(base, step)
        values = total[part, :]
        centre = jnp.mean(values, axis=-1, keepdims=True)
        values = values - centre
        spread = jnp.mean(values * values, axis=-1, keepdims=True)
        total[part, :] = values * lax.rsqrt(spread + 1e-06)
    for place in range(chans // LANES):
        lanes = pl.ds(pl.multiple_of(order_ref[place] * LANES, LANES), LANES)
        out_ref[:, pl.ds(place * LANES, LANES)] = (
            total[:, lanes] * gain_ref[:, lanes] + shift_ref[:, lanes]
        ).astype(BF16)


def conv_norm(order, mid, low, high, left, right, taps, bias, gain, offset):
    rows, cols, chans = mid.shape
    return pl.pallas_call(
        conv_kernel,
        out_shape=jax.ShapeDtypeStruct((rows * cols, chans), BF16),
        in_specs=[SMEM] + [VMEM] * 9,
        out_specs=VMEM,
        scratch_shapes=[
            pltpu.VMEM(((rows + 6) * 16, LANES), F32),
            pltpu.VMEM((56, chans), F32),
            pltpu.VMEM((rows * cols, chans), F32),
        ],
        compiler_params=PARAMS,
        cost_estimate=pl.CostEstimate(flops=100 * rows * cols * chans, bytes_accessed=2 << 20, transcendentals=0),
    )(order, mid, low, high, left, right, taps, bias, gain, offset)


def up_kernel(parts, *refs):
    pixels, shards, bias_ref = refs[:parts], refs[parts:-parts - 2], refs[-parts - 2]
    outs, weight = refs[-parts - 1:-1], refs[-1]
    at = 0
    for shard in shards:
        weight[pl.ds(at, shard.shape[0]), :] = shard[...]
        at += shard.shape[0]
    hidden = weight.shape[1]
    for pixel, out in zip(pixels, outs):
        for n in range(0, hidden, 256):
            cols = pl.ds(n, 256)
            pre = jnp.dot(pixel[...], weight[:, cols], preferred_element_type=F32) + bias_ref[:, cols]
            out[:, cols] = (0.5 * pre * (1.0 + lax.erf(pre * 0.7071067811865476))).astype(BF16)


def up(pixels, shards, bias):
    depth = sum(s.shape[0] for s in shards)
    hidden = shards[0].shape[1]
    outs = tuple(jax.ShapeDtypeStruct((p.shape[0], hidden), BF16) for p in pixels)
    return pl.pallas_call(
        functools.partial(up_kernel, len(pixels)),
        out_shape=outs,
        in_specs=[VMEM] * (len(pixels) + len(shards) + 1),
        out_specs=tuple(VMEM for _ in outs),
        scratch_shapes=[pltpu.VMEM((depth, hidden), BF16)],
        compiler_params=PARAMS,
        cost_estimate=pl.CostEstimate(
            flops=2 * depth * hidden * sum(p.shape[0] for p in pixels), bytes_accessed=6 << 20, transcendentals=0
        ),
    )(*pixels, *shards, bias)


def down_kernel(parts, *refs):
    hidden, shards, outs = refs[:parts], refs[parts:-parts], refs[-parts:]
    for act, out in zip(hidden, outs):
        at = 0
        for shard in shards:
            count = shard.shape[0]
            out[:, pl.ds(at, count)] = lax.dot_general(
                act[...], shard[...], (((1,), (1,)), ((), ())), preferred_element_type=F32
            ).astype(BF16)
            at += count


def down(hidden, shards):
    chans = sum(s.shape[0] for s in shards)
    outs = tuple(jax.ShapeDtypeStruct((h.shape[0], chans), BF16) for h in hidden)
    return pl.pallas_call(
        functools.partial(down_kernel, len(hidden)),
        out_shape=outs,
        in_specs=[VMEM] * (len(hidden) + len(shards)),
        out_specs=tuple(VMEM for _ in outs),
        compiler_params=PARAMS,
        cost_estimate=pl.CostEstimate(
            flops=2 * chans * hidden[0].shape[1] * sum(h.shape[0] for h in hidden), bytes_accessed=6 << 20,
            transcendentals=0,
        ),
    )(*hidden, *shards)


def add_kernel(one_ref, two_ref, out_ref):
    out_ref[...] = (one_ref[...].astype(F32) + two_ref[...].astype(F32)).astype(BF16)


def add(one, two):
    return pl.pallas_call(
        add_kernel,
        out_shape=jax.ShapeDtypeStruct(one.shape, BF16),
        in_specs=[VMEM, VMEM],
        out_specs=VMEM,
        compiler_params=PARAMS,
    )(one, two)


def finish_kernel(order_ref, feature_ref, one_ref, two_ref, three_ref, bias_ref, scale_ref, out_ref):
    for place in range(feature_ref.shape[1] // LANES):
        lanes = pl.ds(pl.multiple_of(order_ref[place] * LANES, LANES), LANES)
        held = pl.ds(place * LANES, LANES)
        branch = (one_ref[:, held].astype(F32) + two_ref[:, held].astype(F32)) + three_ref[:, held].astype(F32)
        out_ref[:, lanes] = (
            feature_ref[:, lanes].astype(F32) + scale_ref[:, lanes] * (branch + bias_ref[:, lanes])
        ).astype(BF16)


def finish(order, features, one, two, three, bias, scale):
    return pl.pallas_call(
        finish_kernel,
        out_shape=jax.ShapeDtypeStruct(features.shape, BF16),
        in_specs=[SMEM] + [VMEM] * 6,
        out_specs=VMEM,
        compiler_params=PARAMS,
    )(order, features, one, two, three, bias, scale)


def spread(weight):
    count = lax.axis_size("lon")
    if weight.shape[0] != LANES:
        whole = lax.all_gather(weight, "lon", axis=0, tiled=True)
        return [whole]
    held = []
    for step in range(count // 2):
        mine = weight if step == 0 else shift(weight, "lon", step, 2)
        held += [mine, swap(mine, "lon", 1)]
    return held


def chunk_order(weight):
    count = lax.axis_size("lon")
    if weight.shape[0] != LANES:
        return jnp.arange(count * weight.shape[0] // LANES, dtype=jnp.int32)
    me = lax.axis_index("lon").astype(jnp.int32)
    group, side = me // 2, me % 2
    return jnp.stack(
        [((group - step) % (count // 2)) * 2 + (side ^ flip) for step in range(count // 2) for flip in range(2)]
    ).astype(jnp.int32)


def local(
    features,
    depth_kernel,
    depth_bias,
    norm_gain,
    norm_bias,
    up_weight,
    up_bias,
    down_weight,
    down_bias,
    layer_scale,
):
    rows, cols, chans = features.shape
    lats, lons = lax.axis_size("lat"), lax.axis_size("lon")
    line = lambda v: v.reshape(1, -1)

    forward = [(i, i + 1) for i in range(lats - 1)]
    low = lax.ppermute(features[rows - 3:], "lat", forward)
    high = lax.ppermute(features[:3], "lat", [(b, a) for a, b in forward])
    first, last = edges(low, features, high)
    left = lax.ppermute(last, "lon", [(i, (i + 1) % lons) for i in range(lons)])
    right = lax.ppermute(first, "lon", [((i + 1) % lons, i) for i in range(lons)])

    up_shards = spread(up_weight)
    down_shards = spread(down_weight)
    order = chunk_order(up_weight)

    normed = conv_norm(
        order, features, low, high, left, right, depth_kernel.reshape(49, chans),
        line(depth_bias), line(norm_gain), line(norm_bias),
    )
    across = swap(normed, "lat", 2)
    beside = swap(normed, "lat", 1)
    opposite = swap(across, "lat", 1)
    hid_opposite, hid_across, hid_beside, hid_own = up(
        [opposite, across, beside, normed], up_shards, line(up_bias)
    )
    far_opposite, far_across = down([hid_opposite, hid_across], down_shards)
    far = add(far_across, swap(far_opposite, "lat", 1))
    arrived = swap(far, "lat", 2)
    near_beside, near_own = down([hid_beside, hid_own], down_shards)
    near = swap(near_beside, "lat", 1)
    updated = finish(
        order, features.reshape(rows * cols, chans), near_own, near, arrived, line(down_bias), line(layer_scale)
    )
    return updated.reshape(rows, cols, chans)


def solution(mesh):
    placed = (
        P("lat", "lon", None),
        P(),
        P(),
        P(),
        P(),
        P("lon", "lat"),
        P("lat"),
        P("lon", "lat"),
        P(),
        P(),
    )
    return jax.shard_map(
        local, mesh=mesh, in_specs=placed, out_specs=P("lat", "lon", None), check_vma=False
    )
```

time: 224 us -> 135 us (0.60)
  the two profiles are of different devices: /device:TPU:0 before, /device:TPU:28 now
where the time goes in v1:
time: 135 us
  waiting for transfers between devices  85.8 us (64%)
  starting transfers between devices  32.2 us (24%)
  Pallas kernels  14.8 us (11%)
  local copies, waits for them, and re-layouts  2.06 us (2%)
    ppermute x14, waiting for transfers between devices, swap(): return lax.ppermute(value, axis, [(i, i ^ bit) for i in range(count)])  42.3 us
    ppermute x6, waiting for transfers between devices, shift(): lax.ppermute(value, axis, [(i, (i + step * inner) % count) for i in range...  33 us
    ppermute x6, starting transfers between devices, shift(): lax.ppermute(value, axis, [(i, (i + step * inner) % count) for i in range...  15.1 us
    ppermute x14, starting transfers between devices, swap(): return lax.ppermute(value, axis, [(i, i ^ bit) for i in range(count)])  8.49 us
    ppermute x1, waiting for transfers between devices, local(): left = lax.ppermute(last, 'lon', [(i, (i + 1) % lons) for i in range(lons)])  7.07 us
    pallas_call x1, Pallas kernels, conv_norm(): pl.pallas_call(conv_kernel, out_shape=jax.ShapeDtypeStruct((rows * cols,...  5.03 us
    pallas_call x2, Pallas kernels, down(): pl.pallas_call(functools.partial(down_kernel, len(hidden)), out_shape=out...  4.67 us
    ppermute x1, starting transfers between devices, local(): high = lax.ppermute(features[:3], 'lat', [(b, a) for a, b in forward])  3.64 us
  transfers between devices with their start and end apart: 24, of which 13 were waited for; matrix products, arithmetic and copies ran while one was open for 0% of the time, Pallas kernels for 4%

profile of v1, /device:TPU:28, one launch (start us, length us, event | category | flops | bytes accessed | tf_op | source)
XLA Modules:
  0.0 135.1 jit_solution(11796931758797120831)
XLA Ops:
  0.0 0.8 fusion
  0.8 1.9 %collective-permute-start = (bf16[3,8,1024]{2,1,0:T(8,128)(2,1)S(1)}, bf16[3,8,1024]{2,1,0:T(8,128)(2,1)S(1)}, u32[]{:S(2)}, u32[]{:S(2)}) collective-permute-start(bf16[3,8,1024]{2,1,0:T(8,128)(2,1)S(1)} %get-tuple-element.26), channel_id=1, source_target_pairs={{0,8},{8,16},{16,24},{1,9},{9,17},{17,25},{2,10},{10,18},{18,26},{... | collective-permute-start | bytes 147464 | tf_op jit(solution)/shard_map/ppermute | solution.py:256
  2.7 3.6 %collective-permute-start.1 = (bf16[3,8,1024]{2,1,0:T(8,128)(2,1)S(1)}, bf16[3,8,1024]{2,1,0:T(8,128)(2,1)S(1)}, u32[]{:S(2)}, u32[]{:S(2)}) collective-permute-start(bf16[3,8,1024]{2,1,0:T(8,128)(2,1)S(1)} %get-tuple-element.25), channel_id=1, source_target_pairs={{8,0},{16,8},{24,16},{9,1},{17,9},{25,17},{10,2},{18,10},{26,18},{... | collective-permute-start | bytes 147464 | tf_op jit(solution)/shard_map/ppermute | solution.py:257
  6.4 1.7 %collective-permute-done.1.high_ref = bf16[3,8,1024]{2,1,0:T(8,128)(2,1)S(1)} collective-permute-done((bf16[3,8,1024]{2,1,0:T(8,128)(2,1)S(1)}, bf16[3,8,1024]{2,1,0:T(8,128)(2,1)S(1)}, u32[]{:S(2)}, u32[]{:S(2)}) %collective-permute-start.1) | collective-permute-done | bytes 49184 | tf_op jit(solution)/shard_map/ppermute | solution.py:257
  8.1 1.0 copy-done
  9.2 0.4 shard_map.100
  9.6 0.0 copy-start.10
  9.6 1.5 %collective-permute-start.2 = (bf16[3,38,1024]{2,1,0:T(8,128)(2,1)S(1)}, bf16[3,38,1024]{2,1,0:T(8,128)(2,1)S(1)}, u32[]{:S(2)}, u32[]{:S(2)}) collective-permute-start(bf16[3,38,1024]{2,1,0:T(8,128)(2,1)S(1)} %get-tuple-element.15), channel_id=1, source_target_pairs={{0,1},{1,2},{2,3},{3,4},{4,5},{5,6},{6,7},{7,0},{8,9},{9,10},{10,1... | collective-permute-start | bytes 700424 | tf_op jit(solution)/shard_map/ppermute | solution.py:259
  11.2 1.4 %collective-permute-start.3 = (bf16[3,38,1024]{2,1,0:T(8,128)(2,1)S(1)}, bf16[3,38,1024]{2,1,0:T(8,128)(2,1)S(1)}, u32[]{:S(2)}, u32[]{:S(2)}) collective-permute-start(bf16[3,38,1024]{2,1,0:T(8,128)(2,1)S(1)} %get-tuple-element.16), channel_id=1, source_target_pairs={{1,0},{2,1},{3,2},{4,3},{5,4},{6,5},{7,6},{0,7},{9,8},{10,9},{11,1... | collective-permute-start | bytes 700424 | tf_op jit(solution)/shard_map/ppermute | solution.py:260
  12.6 0.0 copy-start.4
  12.7 0.0 copy-start.2
  12.7 0.1 stack.35.order_ref
  12.8 7.1 %collective-permute-done.2.left_ref = bf16[3,38,1024]{2,1,0:T(8,128)(2,1)S(1)} collective-permute-done((bf16[3,38,1024]{2,1,0:T(8,128)(2,1)S(1)}, bf16[3,38,1024]{2,1,0:T(8,128)(2,1)S(1)}, u32[]{:S(2)}, u32[]{:S(2)}) %collective-permute-start.2) | collective-permute-done | bytes 233504 | tf_op jit(solution)/shard_map/ppermute | solution.py:259
  19.8 1.8 %collective-permute-done.3.right_ref = bf16[3,38,1024]{2,1,0:T(8,128)(2,1)S(1)} collective-permute-done((bf16[3,38,1024]{2,1,0:T(8,128)(2,1)S(1)}, bf16[3,38,1024]{2,1,0:T(8,128)(2,1)S(1)}, u32[]{:S(2)}, u32[]{:S(2)}) %collective-permute-start.3) | collective-permute-done | bytes 233504 | tf_op jit(solution)/shard_map/ppermute | solution.py:260
  21.6 0.0 copy-start.8
  21.6 0.0 copy-start.9
  21.7 5.0 %shard_map.101.refs_3_ = bf16[256,1024]{1,0:T(8,128)(2,1)S(1)} custom-call(s32[8]{0:T(128)S(1)} %stack.35.order_ref, bf16[32,8,1024]{2,1,0:T(8,128)(2,1)S(1)} %copy-done.1, bf16[3,8,1024]{2,1,0:T(8,128)(2,1)S(1)} %collective-permute-done.low_ref, bf16[3,8,1024]{2,1,0:T(8,128)(2,1)S(1)} %collective-permute-done.1.high_ref, ...), custom_call_target="tpu_custom_call" | custom-call | flops 26214400 | bytes 2097152 | tf_op jit(solution)/shard_map/pallas_call | solution.py:107
  26.7 2.4 %collective-permute-start.4 = (bf16[256,1024]{1,0:T(8,128)(2,1)S(1)}, bf16[256,1024]{1,0:T(8,128)(2,1)S(1)}, u32[]{:S(2)}, u32[]{:S(2)}) collective-permute-start(bf16[256,1024]{1,0:T(8,128)(2,1)S(1)} %shard_map.101.refs_3_), channel_id=1, source_target_pairs={{0,16},{8,24},{16,0},{24,8},{1,17},{9,25},{17,1},{25,9},{2,18},{10... | collective-permute-start | bytes 1572872 | tf_op jit(solution)/shard_map/ppermute | solution.py:25
  29.1 0.3 collective-permute-start.10
  29.4 0.1 collective-permute-start.12
  29.6 3.7 %collective-permute-start.8 = (bf16[128,1024]{1,0:T(8,128)(2,1)S(1)}, bf16[128,1024]{1,0:T(8,128)(2,1)S(1)}, u32[]{:S(2)}, u32[]{:S(2)}) collective-permute-start(bf16[128,1024]{1,0:T(8,128)(2,1)S(1)} %copy-done.7), channel_id=1, source_target_pairs={{0,2},{1,3},{2,4},{3,5},{4,6},{5,7},{6,0},{7,1},{8,10},{9,11},{10,... | collective-permute-start | bytes 786440 | tf_op jit(solution)/shard_map/ppermute | solution.py:20
  33.3 16.0 %collective-permute-done.10.refs_8_ = bf16[128,1024]{1,0:T(8,128)(2,1)S(1)} collective-permute-done((bf16[128,1024]{1,0:T(8,128)(2,1)S(1)}, bf16[128,1024]{1,0:T(8,128)(2,1)S(1)}, u32[]{:S(2)}, u32[]{:S(2)}) %collective-permute-start.10) | collective-permute-done | bytes 262176 | tf_op jit(solution)/shard_map/ppermute | solution.py:20
  49.3 11.0 %collective-permute-start.17 = (bf16[128,1024]{1,0:T(8,128)(2,1)S(1)}, bf16[128,1024]{1,0:T(8,128)(2,1)S(1)}, u32[]{:S(2)}, u32[]{:S(2)}) collective-permute-start(bf16[128,1024]{1,0:T(8,128)(2,1)S(1)} %copy-done.8), channel_id=1, source_target_pairs={{0,4},{1,5},{2,6},{3,7},{4,0},{5,1},{6,2},{7,3},{8,12},{9,13},{10,... | collective-permute-start | bytes 786440 | tf_op jit(solution)/shard_map/ppermute | solution.py:20
  60.3 0.1 collective-permute-start.6
  60.4 0.5 collective-permute-start.5
  60.9 16.9 %collective-permute-done.17.refs_6_ = bf16[128,1024]{1,0:T(8,128)(2,1)S(1)} collective-permute-done((bf16[128,1024]{1,0:T(8,128)(2,1)S(1)}, bf16[128,1024]{1,0:T(8,128)(2,1)S(1)}, u32[]{:S(2)}, u32[]{:S(2)}) %collective-permute-start.17) | collective-permute-done | bytes 262176 | tf_op jit(solution)/shard_map/ppermute | solution.py:20
  77.8 0.2 collective-permute-start.13
  78.0 1.8 %collective-permute-start.9 = (bf16[128,1024]{1,0:T(8,128)(2,1)S(1)}, bf16[128,1024]{1,0:T(8,128)(2,1)S(1)}, u32[]{:S(2)}, u32[]{:S(2)}) collective-permute-start(bf16[128,1024]{1,0:T(8,128)(2,1)S(1)} %collective-permute-done.8.refs_6_), channel_id=1, source_target_pairs={{0,1},{1,0},{2,3},{3,2},{4,5},{5,4},{6,7},{7,6},{8,9},{9,8},{10,11... | collective-permute-start | bytes 786440 | tf_op jit(solution)/shard_map/ppermute | solution.py:25
  79.8 0.2 collective-permute-start.14
  80.0 7.0 %collective-permute-done.13.refs_11_ = bf16[128,1024]{1,0:T(8,128)(2,1)S(1)} collective-permute-done((bf16[128,1024]{1,0:T(8,128)(2,1)S(1)}, bf16[128,1024]{1,0:T(8,128)(2,1)S(1)}, u32[]{:S(2)}, u32[]{:S(2)}) %collective-permute-start.13) | collective-permute-done | bytes 262176 | tf_op jit(solution)/shard_map/ppermute | solution.py:25
  87.0 0.2 collective-permute-start.16
  87.2 5.4 %collective-permute-done.9.refs_7_ = bf16[128,1024]{1,0:T(8,128)(2,1)S(1)} collective-permute-done((bf16[128,1024]{1,0:T(8,128)(2,1)S(1)}, bf16[128,1024]{1,0:T(8,128)(2,1)S(1)}, u32[]{:S(2)}, u32[]{:S(2)}) %collective-permute-start.9) | collective-permute-done | bytes 262176 | tf_op jit(solution)/shard_map/ppermute | solution.py:25
  92.6 0.2 collective-permute-start.18
  92.8 1.8 %collective-permute-start.20 = (bf16[128,1024]{1,0:T(8,128)(2,1)S(1)}, bf16[128,1024]{1,0:T(8,128)(2,1)S(1)}, u32[]{:S(2)}, u32[]{:S(2)}) collective-permute-start(bf16[128,1024]{1,0:T(8,128)(2,1)S(1)} %collective-permute-done.19.refs_8_), channel_id=1, source_target_pairs={{0,1},{1,0},{2,3},{3,2},{4,5},{5,4},{6,7},{7,6},{8,9},{9,8},{10,11... | collective-permute-start | bytes 786440 | tf_op jit(solution)/shard_map/ppermute | solution.py:25
  94.6 2.8 %shard_map.102 = (bf16[256,1024]{1,0:T(8,128)(2,1)S(1)}, bf16[256,1024]{1,0:T(8,128)(2,1)S(1)}, bf16[256,1024]{1,0:T(8,128)(2,1)S(1)}, bf16[256,1024]{1,0:T(8,128)(2,1)S(1)}) custom-call(bf16[256,1024]{1,0:T(8,128)(2,1)S(1)} %collective-permute-done.5.refs_0_, bf16[256,1024]{1,0:T(8,128)(2,1)S(1)} %collective-permute-done.4.refs_1_, ...), custom_call_target="tpu_custom_call" | custom-call | flops 2147483648 | bytes 6291456 | tf_op jit(solution)/shard_map/pallas_call | solution.py:141
  97.5 0.7 collective-permute-done.14.refs_3_
  98.2 5.6 %collective-permute-done.16.refs_5_ = bf16[128,1024]{1,0:T(8,128)(2,1)S(1)} collective-permute-done((bf16[128,1024]{1,0:T(8,128)(2,1)S(1)}, bf16[128,1024]{1,0:T(8,128)(2,1)S(1)}, u32[]{:S(2)}, u32[]{:S(2)}) %collective-permute-start.16) | collective-permute-done | bytes 262176 | tf_op jit(solution)/shard_map/ppermute | solution.py:25
  103.8 5.6 %collective-permute-done.18.refs_7_ = bf16[128,1024]{1,0:T(8,128)(2,1)S(1)} collective-permute-done((bf16[128,1024]{1,0:T(8,128)(2,1)S(1)}, bf16[128,1024]{1,0:T(8,128)(2,1)S(1)}, u32[]{:S(2)}, u32[]{:S(2)}) %collective-permute-start.18) | collective-permute-done | bytes 262176 | tf_op jit(solution)/shard_map/ppermute | solution.py:25
  109.5 4.5 %collective-permute-done.20.refs_9_ = bf16[128,1024]{1,0:T(8,128)(2,1)S(1)} collective-permute-done((bf16[128,1024]{1,0:T(8,128)(2,1)S(1)}, bf16[128,1024]{1,0:T(8,128)(2,1)S(1)}, u32[]{:S(2)}, u32[]{:S(2)}) %collective-permute-start.20) | collective-permute-done | bytes 262176 | tf_op jit(solution)/shard_map/ppermute | solution.py:25
  113.9 2.3 %shard_map.104 = (bf16[256,1024]{1,0:T(8,128)(2,1)S(1)}, bf16[256,1024]{1,0:T(8,128)(2,1)S(1)}) custom-call(bf16[256,1024]{1,0:T(8,128)(2,1)S(1)} %get-tuple-element.21.refs_0_, bf16[256,1024]{1,0:T(8,128)(2,1)S(1)} %get-tuple-element.22.refs_1_, bf16[128,1024]{1,0:T(8,128)(2,1)S(1)} %copy-done.8, bf16[128,1024]{1,0:T(8,128)(2,1)S(1)} %collective-permute-done.14.refs_3_, ...), custom_call_target="tpu_custom_call" | custom-call | flops 1073741824 | bytes 6291456 | tf_op jit(solution)/shard_map/pallas_call | solution.py:169
  116.3 0.1 collective-permute-start.22
  116.4 2.3 %shard_map.103 = (bf16[256,1024]{1,0:T(8,128)(2,1)S(1)}, bf16[256,1024]{1,0:T(8,128)(2,1)S(1)}) custom-call(bf16[256,1024]{1,0:T(8,128)(2,1)S(1)} %get-tuple-element.17.refs_0_, bf16[256,1024]{1,0:T(8,128)(2,1)S(1)} %get-tuple-element.18.refs_1_, bf16[128,1024]{1,0:T(8,128)(2,1)S(1)} %copy-done.8, bf16[128,1024]{1,0:T(8,128)(2,1)S(1)} %collective-permute-done.14.refs_3_, ...), custom_call_target="tpu_custom_call" | custom-call | flops 1073741824 | bytes 6291456 | tf_op jit(solution)/shard_map/pallas_call | solution.py:169
  118.7 0.6 collective-permute-start.21
  119.3 0.1 shard_map.105
  119.4 0.5 collective-permute-start.23
  119.9 0.9 collective-permute-done.21.two_ref
  120.8 12.5 %collective-permute-done.23.three_ref = bf16[256,1024]{1,0:T(8,128)(2,1)S(1)} collective-permute-done((bf16[256,1024]{1,0:T(8,128)(2,1)S(1)}, bf16[256,1024]{1,0:T(8,128)(2,1)S(1)}, u32[]{:S(2)}, u32[]{:S(2)}) %collective-permute-start.23) | collective-permute-done | bytes 524320 | tf_op jit(solution)/shard_map/ppermute | solution.py:25
  133.3 1.7 %shard_map.106 = bf16[256,1024]{1,0:T(8,128)(2,1)} custom-call(s32[8]{0:T(128)S(1)} %stack.35.order_ref, bf16[256,1024]{1,0:T(8,128)(2,1)S(1)} %bitcast.16, bf16[256,1024]{1,0:T(8,128)(2,1)S(1)} %get-tuple-element.19.one_ref, bf16[256,1024]{1,0:T(8,128)(2,1)S(1)} %collective-permute-done.21.two_ref, bf16[256,1024]{1,0:T(8,128)(2,1)S(1)} %collective-permute-done.23.three_ref, ...), custom_call_target="tpu_custom_call" | custom-call | tf_op jit(solution)/shard_map/pallas_call | solution.py:207
  (32 shorter events, 0.1 us)
Async XLA Ops:
  0.8 5.6 %collective-permute-start = (bf16[3,8,1024]{2,1,0:T(8,128)(2,1)S(1)}, bf16[3,8,1024]{2,1,0:T(8,128)(2,1)S(1)}, u32[]{:S(2)}, u32[]{:S(2)}) collective-permute-start(bf16[3,8,1024]{2,1,0:T(8,128)(2,1)S(1)} %get-tuple-element.26), channel_id=1, source_target_pairs={{0,8},{8,16},{16,24},{1,9},{9,17},{17,25},{2,10},{10,18},{18,26},{... | collective-permute-start | bytes 147464 | tf_op jit(solution)/shard_map/ppermute | solution.py:256
  2.7 5.4 %collective-permute-start.1 = (bf16[3,8,1024]{2,1,0:T(8,128)(2,1)S(1)}, bf16[3,8,1024]{2,1,0:T(8,128)(2,1)S(1)}, u32[]{:S(2)}, u32[]{:S(2)}) collective-permute-start(bf16[3,8,1024]{2,1,0:T(8,128)(2,1)S(1)} %get-tuple-element.25), channel_id=1, source_target_pairs={{8,0},{16,8},{24,16},{9,1},{17,9},{25,17},{10,2},{18,10},{26,18},{... | collective-permute-start | bytes 147464 | tf_op jit(solution)/shard_map/ppermute | solution.py:257
  8.1 1.0 copy-start
  9.2 12.4 %copy-start.1 = (bf16[32,8,1024]{2,1,0:T(8,128)(2,1)S(1)}, bf16[32,8,1024]{2,1,0:T(8,128)(2,1)}, u32[]{:S(2)}) copy-start(bf16[32,8,1024]{2,1,0:T(8,128)(2,1)} %mid_ref.3) | copy-start | bytes 1572868
  9.6 3.0 %copy-start.10 = (bf16[7,7,1024]{2,1,0:T(8,128)(2,1)S(1)}, bf16[7,7,1024]{2,1,0:T(8,128)(2,1)}, u32[]{:S(2)}) copy-start(bf16[7,7,1024]{2,1,0:T(8,128)(2,1)} %param.11) | copy-start | bytes 301060
  9.6 10.2 %collective-permute-start.2 = (bf16[3,38,1024]{2,1,0:T(8,128)(2,1)S(1)}, bf16[3,38,1024]{2,1,0:T(8,128)(2,1)S(1)}, u32[]{:S(2)}, u32[]{:S(2)}) collective-permute-start(bf16[3,38,1024]{2,1,0:T(8,128)(2,1)S(1)} %get-tuple-element.15), channel_id=1, source_target_pairs={{0,1},{1,2},{2,3},{3,4},{4,5},{5,6},{6,7},{7,0},{8,9},{9,10},{10,1... | collective-permute-start | bytes 700424 | tf_op jit(solution)/shard_map/ppermute | solution.py:259
  11.2 10.4 %collective-permute-start.3 = (bf16[3,38,1024]{2,1,0:T(8,128)(2,1)S(1)}, bf16[3,38,1024]{2,1,0:T(8,128)(2,1)S(1)}, u32[]{:S(2)}, u32[]{:S(2)}) collective-permute-start(bf16[3,38,1024]{2,1,0:T(8,128)(2,1)S(1)} %get-tuple-element.16), channel_id=1, source_target_pairs={{1,0},{2,1},{3,2},{4,3},{5,4},{6,5},{7,6},{0,7},{9,8},{10,9},{11,1... | collective-permute-start | bytes 700424 | tf_op jit(solution)/shard_map/ppermute | solution.py:260
  12.6 9.0 %copy-start.4 = (f32[1024]{0:T(1024)S(1)}, f32[1024]{0:T(1024)}, u32[]{:S(2)}) copy-start(f32[1024]{0:T(1024)} %param.14) | copy-start | bytes 12292
  12.7 9.0 %copy-start.2 = (f32[1024]{0:T(1024)S(1)}, f32[1024]{0:T(1024)}, u32[]{:S(2)}) copy-start(f32[1024]{0:T(1024)} %param.12) | copy-start | bytes 12292
  12.7 8.9 %copy-start.3 = (f32[1024]{0:T(1024)S(1)}, f32[1024]{0:T(1024)}, u32[]{:S(2)}) copy-start(f32[1024]{0:T(1024)} %param.13) | copy-start | bytes 12292
  21.6 7.5 %copy-start.7 = (bf16[128,1024]{1,0:T(8,128)(2,1)S(1)}, bf16[128,1024]{1,0:T(8,128)(2,1)}, u32[]{:S(2)}) copy-start(bf16[128,1024]{1,0:T(8,128)(2,1)} %refs_4_.1) | copy-start | bytes 786436
  21.6 27.7 %copy-start.8 = (bf16[128,1024]{1,0:T(8,128)(2,1)S(1)}, bf16[128,1024]{1,0:T(8,128)(2,1)}, u32[]{:S(2)}) copy-start(bf16[128,1024]{1,0:T(8,128)(2,1)} %refs_2_.3) | copy-start | bytes 786436
  21.6 73.0 %copy-start.9 = (f32[1024]{0:T(1024)S(1)}, f32[1024]{0:T(1024)}, u32[]{:S(2)}) copy-start(f32[1024]{0:T(1024)} %param.16) | copy-start | bytes 12292
  26.7 33.7 %collective-permute-start.4 = (bf16[256,1024]{1,0:T(8,128)(2,1)S(1)}, bf16[256,1024]{1,0:T(8,128)(2,1)S(1)}, u32[]{:S(2)}, u32[]{:S(2)}) collective-permute-start(bf16[256,1024]{1,0:T(8,128)(2,1)S(1)} %shard_map.101.refs_3_), channel_id=1, source_target_pairs={{0,16},{8,24},{16,0},{24,8},{1,17},{9,25},{17,1},{25,9},{2,18},{10... | collective-permute-start | bytes 1572872 | tf_op jit(solution)/shard_map/ppermute | solution.py:25
  29.1 20.2 %collective-permute-start.10 = (bf16[128,1024]{1,0:T(8,128)(2,1)S(1)}, bf16[128,1024]{1,0:T(8,128)(2,1)S(1)}, u32[]{:S(2)}, u32[]{:S(2)}) collective-permute-start(bf16[128,1024]{1,0:T(8,128)(2,1)S(1)} %copy-done.7), channel_id=1, source_target_pairs={{0,4},{1,5},{2,6},{3,7},{4,0},{5,1},{6,2},{7,3},{8,12},{9,13},{10,... | collective-permute-start | bytes 786440 | tf_op jit(solution)/shard_map/ppermute | solution.py:20
  29.4 19.9 %collective-permute-start.12 = (bf16[128,1024]{1,0:T(8,128)(2,1)S(1)}, bf16[128,1024]{1,0:T(8,128)(2,1)S(1)}, u32[]{:S(2)}, u32[]{:S(2)}) collective-permute-start(bf16[128,1024]{1,0:T(8,128)(2,1)S(1)} %copy-done.7), channel_id=1, source_target_pairs={{0,6},{1,7},{2,0},{3,1},{4,2},{5,3},{6,4},{7,5},{8,14},{9,15},{10,... | collective-permute-start | bytes 786440 | tf_op jit(solution)/shard_map/ppermute | solution.py:20
  29.6 30.7 %collective-permute-start.8 = (bf16[128,1024]{1,0:T(8,128)(2,1)S(1)}, bf16[128,1024]{1,0:T(8,128)(2,1)S(1)}, u32[]{:S(2)}, u32[]{:S(2)}) collective-permute-start(bf16[128,1024]{1,0:T(8,128)(2,1)S(1)} %copy-done.7), channel_id=1, source_target_pairs={{0,2},{1,3},{2,4},{3,5},{4,6},{5,7},{6,0},{7,1},{8,10},{9,11},{10,... | collective-permute-start | bytes 786440 | tf_op jit(solution)/shard_map/ppermute | solution.py:20
  33.3 27.0 %collective-permute-start.7 = (bf16[128,1024]{1,0:T(8,128)(2,1)S(1)}, bf16[128,1024]{1,0:T(8,128)(2,1)S(1)}, u32[]{:S(2)}, u32[]{:S(2)}) collective-permute-start(bf16[128,1024]{1,0:T(8,128)(2,1)S(1)} %copy-done.7), channel_id=1, source_target_pairs={{0,1},{1,0},{2,3},{3,2},{4,5},{5,4},{6,7},{7,6},{8,9},{9,8},{10,11... | collective-permute-start | bytes 786440 | tf_op jit(solution)/shard_map/ppermute | solution.py:25
  49.3 11.6 %collective-permute-start.15 = (bf16[128,1024]{1,0:T(8,128)(2,1)S(1)}, bf16[128,1024]{1,0:T(8,128)(2,1)S(1)}, u32[]{:S(2)}, u32[]{:S(2)}) collective-permute-start(bf16[128,1024]{1,0:T(8,128)(2,1)S(1)} %copy-done.8), channel_id=1, source_target_pairs={{0,2},{1,3},{2,4},{3,5},{4,6},{5,7},{6,0},{7,1},{8,10},{9,11},{10,... | collective-permute-start | bytes 786440 | tf_op jit(solution)/shard_map/ppermute | solution.py:20
  49.3 28.5 %collective-permute-start.17 = (bf16[128,1024]{1,0:T(8,128)(2,1)S(1)}, bf16[128,1024]{1,0:T(8,128)(2,1)S(1)}, u32[]{:S(2)}, u32[]{:S(2)}) collective-permute-start(bf16[128,1024]{1,0:T(8,128)(2,1)S(1)} %copy-done.8), channel_id=1, source_target_pairs={{0,4},{1,5},{2,6},{3,7},{4,0},{5,1},{6,2},{7,3},{8,12},{9,13},{10,... | collective-permute-start | bytes 786440 | tf_op jit(solution)/shard_map/ppermute | solution.py:20
  60.3 17.7 %collective-permute-start.19 = (bf16[128,1024]{1,0:T(8,128)(2,1)S(1)}, bf16[128,1024]{1,0:T(8,128)(2,1)S(1)}, u32[]{:S(2)}, u32[]{:S(2)}) collective-permute-start(bf16[128,1024]{1,0:T(8,128)(2,1)S(1)} %copy-done.8), channel_id=1, source_target_pairs={{0,6},{1,7},{2,0},{3,1},{4,2},{5,3},{6,4},{7,5},{8,14},{9,15},{10,... | collective-permute-start | bytes 786440 | tf_op jit(solution)/shard_map/ppermute | solution.py:20
  60.3 32.5 %collective-permute-start.6 = (bf16[256,1024]{1,0:T(8,128)(2,1)S(1)}, bf16[256,1024]{1,0:T(8,128)(2,1)S(1)}, u32[]{:S(2)}, u32[]{:S(2)}) collective-permute-start(bf16[256,1024]{1,0:T(8,128)(2,1)S(1)} %shard_map.101.refs_3_), channel_id=1, source_target_pairs={{0,8},{8,0},{16,24},{24,16},{1,9},{9,1},{17,25},{25,17},{2,10},{10... | collective-permute-start | bytes 1572872 | tf_op jit(solution)/shard_map/ppermute | solution.py:25
  60.4 34.2 %collective-permute-start.5 = (bf16[256,1024]{1,0:T(8,128)(2,1)S(1)}, bf16[256,1024]{1,0:T(8,128)(2,1)S(1)}, u32[]{:S(2)}, u32[]{:S(2)}) collective-permute-start(bf16[256,1024]{1,0:T(8,128)(2,1)S(1)} %collective-permute-done.4.refs_1_), channel_id=1, source_target_pairs={{0,8},{8,0},{16,24},{24,16},{1,9},{9,1},{17,25},{25,17},{2,10},{10... | collective-permute-start | bytes 1572872 | tf_op jit(solution)/shard_map/ppermute | solution.py:25
  60.9 18.9 %collective-permute-start.11 = (bf16[128,1024]{1,0:T(8,128)(2,1)S(1)}, bf16[128,1024]{1,0:T(8,128)(2,1)S(1)}, u32[]{:S(2)}, u32[]{:S(2)}) collective-permute-start(bf16[128,1024]{1,0:T(8,128)(2,1)S(1)} %collective-permute-done.10.refs_8_), channel_id=1, source_target_pairs={{0,1},{1,0},{2,3},{3,2},{4,5},{5,4},{6,7},{7,6},{8,9},{9,8},{10,11... | collective-permute-start | bytes 786440 | tf_op jit(solution)/shard_map/ppermute | solution.py:25
  77.8 9.2 %collective-permute-start.13 = (bf16[128,1024]{1,0:T(8,128)(2,1)S(1)}, bf16[128,1024]{1,0:T(8,128)(2,1)S(1)}, u32[]{:S(2)}, u32[]{:S(2)}) collective-permute-start(bf16[128,1024]{1,0:T(8,128)(2,1)S(1)} %collective-permute-done.12.refs_10_), channel_id=1, source_target_pairs={{0,1},{1,0},{2,3},{3,2},{4,5},{5,4},{6,7},{7,6},{8,9},{9,8},{10,11... | collective-permute-start | bytes 786440 | tf_op jit(solution)/shard_map/ppermute | solution.py:25
  78.0 14.6 %collective-permute-start.9 = (bf16[128,1024]{1,0:T(8,128)(2,1)S(1)}, bf16[128,1024]{1,0:T(8,128)(2,1)S(1)}, u32[]{:S(2)}, u32[]{:S(2)}) collective-permute-start(bf16[128,1024]{1,0:T(8,128)(2,1)S(1)} %collective-permute-done.8.refs_6_), channel_id=1, source_target_pairs={{0,1},{1,0},{2,3},{3,2},{4,5},{5,4},{6,7},{7,6},{8,9},{9,8},{10,11... | collective-permute-start | bytes 786440 | tf_op jit(solution)/shard_map/ppermute | solution.py:25
  79.8 18.4 %collective-permute-start.14 = (bf16[128,1024]{1,0:T(8,128)(2,1)S(1)}, bf16[128,1024]{1,0:T(8,128)(2,1)S(1)}, u32[]{:S(2)}, u32[]{:S(2)}) collective-permute-start(bf16[128,1024]{1,0:T(8,128)(2,1)S(1)} %copy-done.8), channel_id=1, source_target_pairs={{0,1},{1,0},{2,3},{3,2},{4,5},{5,4},{6,7},{7,6},{8,9},{9,8},{10,11... | collective-permute-start | bytes 786440 | tf_op jit(solution)/shard_map/ppermute | solution.py:25
  87.0 16.9 %collective-permute-start.16 = (bf16[128,1024]{1,0:T(8,128)(2,1)S(1)}, bf16[128,1024]{1,0:T(8,128)(2,1)S(1)}, u32[]{:S(2)}, u32[]{:S(2)}) collective-permute-start(bf16[128,1024]{1,0:T(8,128)(2,1)S(1)} %collective-permute-done.15.refs_4_), channel_id=1, source_target_pairs={{0,1},{1,0},{2,3},{3,2},{4,5},{5,4},{6,7},{7,6},{8,9},{9,8},{10,11... | collective-permute-start | bytes 786440 | tf_op jit(solution)/shard_map/ppermute | solution.py:25
  92.6 16.9 %collective-permute-start.18 = (bf16[128,1024]{1,0:T(8,128)(2,1)S(1)}, bf16[128,1024]{1,0:T(8,128)(2,1)S(1)}, u32[]{:S(2)}, u32[]{:S(2)}) collective-permute-start(bf16[128,1024]{1,0:T(8,128)(2,1)S(1)} %collective-permute-done.17.refs_6_), channel_id=1, source_target_pairs={{0,1},{1,0},{2,3},{3,2},{4,5},{5,4},{6,7},{7,6},{8,9},{9,8},{10,11... | collective-permute-start | bytes 786440 | tf_op jit(solution)/shard_map/ppermute | solution.py:25
  92.8 21.2 %collective-permute-start.20 = (bf16[128,1024]{1,0:T(8,128)(2,1)S(1)}, bf16[128,1024]{1,0:T(8,128)(2,1)S(1)}, u32[]{:S(2)}, u32[]{:S(2)}) collective-permute-start(bf16[128,1024]{1,0:T(8,128)(2,1)S(1)} %collective-permute-done.19.refs_8_), channel_id=1, source_target_pairs={{0,1},{1,0},{2,3},{3,2},{4,5},{5,4},{6,7},{7,6},{8,9},{9,8},{10,11... | collective-permute-start | bytes 786440 | tf_op jit(solution)/shard_map/ppermute | solution.py:25
  116.3 3.0 %collective-permute-start.22 = (bf16[256,1024]{1,0:T(8,128)(2,1)S(1)}, bf16[256,1024]{1,0:T(8,128)(2,1)S(1)}, u32[]{:S(2)}, u32[]{:S(2)}) collective-permute-start(bf16[256,1024]{1,0:T(8,128)(2,1)S(1)} %get-tuple-element.24), channel_id=1, source_target_pairs={{0,8},{8,0},{16,24},{24,16},{1,9},{9,1},{17,25},{25,17},{2,10},{10... | collective-permute-start | bytes 1572872 | tf_op jit(solution)/shard_map/ppermute | solution.py:25
  118.7 2.1 %collective-permute-start.21 = (bf16[256,1024]{1,0:T(8,128)(2,1)S(1)}, bf16[256,1024]{1,0:T(8,128)(2,1)S(1)}, u32[]{:S(2)}, u32[]{:S(2)}) collective-permute-start(bf16[256,1024]{1,0:T(8,128)(2,1)S(1)} %get-tuple-element.20), channel_id=1, source_target_pairs={{0,8},{8,0},{16,24},{24,16},{1,9},{9,1},{17,25},{25,17},{2,10},{10... | collective-permute-start | bytes 1572872 | tf_op jit(solution)/shard_map/ppermute | solution.py:25
  119.3 14.1 %copy-start.6 = (f32[1024]{0:T(1024)S(1)}, f32[1024]{0:T(1024)}, u32[]{:S(2)}) copy-start(f32[1024]{0:T(1024)} %param.19) | copy-start | bytes 12292
  119.4 13.9 %copy-start.5 = (f32[1024]{0:T(1024)S(1)}, f32[1024]{0:T(1024)}, u32[]{:S(2)}) copy-start(f32[1024]{0:T(1024)} %param.18) | copy-start | bytes 12292
  119.4 13.9 %collective-permute-start.23 = (bf16[256,1024]{1,0:T(8,128)(2,1)S(1)}, bf16[256,1024]{1,0:T(8,128)(2,1)S(1)}, u32[]{:S(2)}, u32[]{:S(2)}) collective-permute-start(bf16[256,1024]{1,0:T(8,128)(2,1)S(1)} %shard_map.105), channel_id=1, source_target_pairs={{0,16},{8,24},{16,0},{24,8},{1,17},{9,25},{17,1},{25,9},{2,18},{10... | collective-permute-start | bytes 1572872 | tf_op jit(solution)/shard_map/ppermute | solution.py:25

commit v2 on v1

v2 whole, which is shorter than its diff:
```python
import functools

import jax
import jax.numpy as jnp
from jax import lax
from jax.experimental import pallas as pl
from jax.experimental.pallas import tpu as pltpu
from jax.sharding import PartitionSpec as P

F32 = jnp.float32
BF16 = jnp.bfloat16
LANES = 128
VMEM = pl.BlockSpec(memory_space=pltpu.VMEM)
SMEM = pl.BlockSpec(memory_space=pltpu.SMEM)
PARAMS = pltpu.CompilerParams(vmem_limit_bytes=40 * 1024 * 1024)


def shift(value, axis, step, inner):
    count = lax.axis_size(axis)
    return lax.ppermute(value, axis, [(i, (i + step * inner) % count) for i in range(count)])


def swap(value, axis, bit):
    count = lax.axis_size(axis)
    return lax.ppermute(value, axis, [(i, i ^ bit) for i in range(count)])


def edges_kernel(mid_ref, first_ref, last_ref, slab):
    rows, cols, chans = mid_ref.shape
    for at in range(0, chans, LANES):
        lanes = pl.ds(at, LANES)
        slab[...] = mid_ref[:, :, lanes].astype(F32).reshape(rows * cols, LANES)
        for col in range(3):
            first_ref[col, :, lanes] = slab[pl.ds(col, rows, stride=cols), :].astype(BF16)
            last_ref[col, :, lanes] = slab[pl.ds(cols - 3 + col, rows, stride=cols), :].astype(BF16)


def edges(mid):
    rows, cols, chans = mid.shape
    block = 256
    shape = jax.ShapeDtypeStruct((3, rows, chans), BF16)
    out = pl.BlockSpec((3, rows, block), lambda i: (0, 0, i))
    return pl.pallas_call(
        edges_kernel,
        grid=(chans // block,),
        out_shape=(shape, shape),
        in_specs=[pl.BlockSpec((rows, cols, block), lambda i: (0, 0, i))],
        out_specs=(out, out),
        scratch_shapes=[pltpu.VMEM((rows * cols, LANES), F32)],
        compiler_params=PARAMS,
    )(mid)


WIDE = 16


def rims_kernel(mid_ref, left_ref, right_ref, top_ref, bottom_ref, slab):
    rows, cols, chans = mid_ref.shape
    slab[...] = jnp.zeros_like(slab)

    @pl.loop(0, chans // LANES)
    def _(chunk):
        lanes = pl.ds(pl.multiple_of(chunk * LANES, LANES), LANES)
        for out_ref, near, begin in ((top_ref, 0, 0), (bottom_ref, rows - 16, 13)):
            for row in range(3):
                slab[pl.ds(row * WIDE + 3, cols), :] = mid_ref[near + begin + row, :, lanes].astype(F32)
            for col in range(3):
                for at, ref in ((col, left_ref), (cols + 3 + col, right_ref)):
                    edge = ref[col, pl.ds(near, 16), lanes].astype(F32)
                    slab[pl.ds(at, 3, stride=WIDE), :] = edge[begin:begin + 3]
            out_ref[:, lanes] = slab[...].astype(BF16)


def rims(mid, left, right):
    chans = mid.shape[2]
    shape = jax.ShapeDtypeStruct((3 * WIDE, chans), BF16)
    return pl.pallas_call(
        rims_kernel,
        out_shape=(shape, shape),
        in_specs=[VMEM] * 3,
        out_specs=(VMEM, VMEM),
        scratch_shapes=[pltpu.VMEM((3 * WIDE, LANES), F32)],
        compiler_params=PARAMS,
    )(mid, left, right)


def conv_kernel(
    order_ref, mid_ref, low_ref, high_ref, left_ref, right_ref, taps_ref, bias_ref, gain_ref, shift_ref,
    out_ref, slab, taps, total,
):
    rows, cols, chans = mid_ref.shape
    block = 16
    taps[pl.ds(0, 49), :] = taps_ref[...].astype(F32)

    def chunk_step(chunk, carry):
        lanes = pl.ds(pl.multiple_of(chunk * LANES, LANES), LANES)
        slab[pl.ds(0, 3 * WIDE), :] = low_ref[:, lanes].astype(F32)
        slab[pl.ds((rows + 3) * WIDE, 3 * WIDE), :] = high_ref[:, lanes].astype(F32)
        for row in range(rows):
            slab[pl.ds((row + 3) * WIDE + 3, cols), :] = mid_ref[row, :, lanes].astype(F32)
        for col in range(3):
            slab[pl.ds(3 * WIDE + col, rows, stride=WIDE), :] = left_ref[col, :, lanes].astype(F32)
            slab[pl.ds(3 * WIDE + cols + 3 + col, rows, stride=WIDE), :] = right_ref[col, :, lanes].astype(F32)
        for base in range(0, rows, block):
            start = jnp.broadcast_to(bias_ref[:, lanes], (cols, LANES))
            sums = [start] * block
            for b in range(7):
                weights = [jnp.broadcast_to(taps[pl.ds(7 * a + b, 1), lanes], (cols, LANES)) for a in range(7)]
                for row in range(block + 6):
                    window = slab[pl.ds((base + row) * WIDE + b, cols), :]
                    for a in range(7):
                        if 0 <= row - a < block:
                            sums[row - a] = sums[row - a] + window * weights[a]
            for row in range(block):
                total[pl.ds((base + row) * cols, cols), lanes] = sums[row]
        return carry

    lax.fori_loop(0, chans // LANES, chunk_step, 0)

    step = 64
    for base in range(0, rows * cols, step):
        part = pl.ds(base, step)
        values = total[part, :]
        centre = jnp.mean(values, axis=-1, keepdims=True)
        values = values - centre
        spread = jnp.mean(values * values, axis=-1, keepdims=True)
        total[part, :] = values * lax.rsqrt(spread + 1e-06)
    for place in range(chans // LANES):
        lanes = pl.ds(pl.multiple_of(order_ref[place] * LANES, LANES), LANES)
        out_ref[:, pl.ds(place * LANES, LANES)] = (
            total[:, lanes] * gain_ref[:, lanes] + shift_ref[:, lanes]
        ).astype(BF16)


def conv_norm(order, mid, low, high, left, right, taps, bias, gain, offset):
    rows, cols, chans = mid.shape
    return pl.pallas_call(
        conv_kernel,
        out_shape=jax.ShapeDtypeStruct((rows * cols, chans), BF16),
        in_specs=[SMEM] + [VMEM] * 9,
        out_specs=VMEM,
        scratch_shapes=[
            pltpu.VMEM(((rows + 6) * WIDE, LANES), F32),
            pltpu.VMEM((56, chans), F32),
            pltpu.VMEM((rows * cols, chans), F32),
        ],
        compiler_params=PARAMS,
        cost_estimate=pl.CostEstimate(flops=100 * rows * cols * chans, bytes_accessed=2 << 20, transcendentals=0),
    )(order, mid, low, high, left, right, taps, bias, gain, offset)


def up_kernel(parts, spans, *refs):
    pixels, shards, bias_ref = refs[:parts], refs[parts:-parts - 2], refs[-parts - 2]
    outs, weight = refs[-parts - 1:-1], refs[-1]
    at = 0
    for shard, (start, count) in zip(shards, spans):
        weight[pl.ds(at, count), :] = shard[pl.ds(start, count), :]
        at += count
    hidden = weight.shape[1]
    for pixel, out in zip(pixels, outs):
        for n in range(0, hidden, 256):
            cols = pl.ds(n, 256)
            pre = jnp.dot(pixel[...], weight[:, cols], preferred_element_type=F32) + bias_ref[:, cols]
            out[:, cols] = (0.5 * pre * (1.0 + lax.erf(pre * 0.7071067811865476))).astype(BF16)


def up(pixels, shards, bias):
    arrays, spans = [s[0] for s in shards], tuple(s[1:] for s in shards)
    depth = sum(count for _, count in spans)
    hidden = arrays[0].shape[1]
    outs = tuple(jax.ShapeDtypeStruct((p.shape[0], hidden), BF16) for p in pixels)
    return pl.pallas_call(
        functools.partial(up_kernel, len(pixels), spans),
        out_shape=outs,
        in_specs=[VMEM] * (len(pixels) + len(shards) + 1),
        out_specs=tuple(VMEM for _ in outs),
        scratch_shapes=[pltpu.VMEM((depth, hidden), BF16)],
        compiler_params=PARAMS,
        cost_estimate=pl.CostEstimate(
            flops=2 * depth * hidden * sum(p.shape[0] for p in pixels), bytes_accessed=6 << 20, transcendentals=0
        ),
    )(*pixels, *arrays, bias)


def down_kernel(parts, spans, *refs):
    hidden, shards, outs = refs[:parts], refs[parts:-parts], refs[-parts:]
    for act, out in zip(hidden, outs):
        at = 0
        for shard, (start, count) in zip(shards, spans):
            out[:, pl.ds(at, count)] = lax.dot_general(
                act[...], shard[pl.ds(start, count), :], (((1,), (1,)), ((), ())), preferred_element_type=F32
            ).astype(BF16)
            at += count


def down(hidden, shards):
    arrays, spans = [s[0] for s in shards], tuple(s[1:] for s in shards)
    chans = sum(count for _, count in spans)
    outs = tuple(jax.ShapeDtypeStruct((h.shape[0], chans), BF16) for h in hidden)
    return pl.pallas_call(
        functools.partial(down_kernel, len(hidden), spans),
        out_shape=outs,
        in_specs=[VMEM] * (len(hidden) + len(shards)),
        out_specs=tuple(VMEM for _ in outs),
        compiler_params=PARAMS,
        cost_estimate=pl.CostEstimate(
            flops=2 * chans * hidden[0].shape[1] * sum(h.shape[0] for h in hidden), bytes_accessed=6 << 20,
            transcendentals=0,
        ),
    )(*hidden, *arrays)


def add_kernel(one_ref, two_ref, out_ref):
    out_ref[...] = (one_ref[...].astype(F32) + two_ref[...].astype(F32)).astype(BF16)


def add(one, two):
    return pl.pallas_call(
        add_kernel,
        out_shape=jax.ShapeDtypeStruct(one.shape, BF16),
        in_specs=[VMEM, VMEM],
        out_specs=VMEM,
        compiler_params=PARAMS,
    )(one, two)


def settle(feature, one, two, three, bias, scale):
    branch = (one.astype(F32) + two.astype(F32)) + three.astype(F32)
    return (feature.astype(F32) + scale * (branch + bias)).astype(BF16)


def part_kernel(first, order_ref, feature_ref, one_ref, two_ref, three_ref, bias_ref, scale_ref, out_ref):
    for at in range(0, out_ref.shape[1], LANES):
        lanes = pl.ds(pl.multiple_of(order_ref[first + at // LANES] * LANES, LANES), LANES)
        held = pl.ds(at, LANES)
        out_ref[:, held] = settle(
            feature_ref[:, lanes], one_ref[:, held], two_ref[:, held], three_ref[:, held],
            bias_ref[:, lanes], scale_ref[:, lanes],
        )


def part(first, order, features, group, bias, scale):
    return pl.pallas_call(
        functools.partial(part_kernel, first),
        out_shape=jax.ShapeDtypeStruct(group[0].shape, BF16),
        in_specs=[SMEM] + [VMEM] * 6,
        out_specs=VMEM,
        compiler_params=PARAMS,
    )(order, features, *group, bias, scale)


def finish_kernel(done, order_ref, feature_ref, *refs):
    parts, (one_ref, two_ref, three_ref, bias_ref, scale_ref, out_ref) = refs[:done], refs[done:]
    place = 0
    for part_ref in parts:
        for at in range(0, part_ref.shape[1], LANES):
            lanes = pl.ds(pl.multiple_of(order_ref[place] * LANES, LANES), LANES)
            out_ref[:, lanes] = part_ref[:, pl.ds(at, LANES)]
            place += 1
    for at in range(0, one_ref.shape[1], LANES):
        lanes = pl.ds(pl.multiple_of(order_ref[place] * LANES, LANES), LANES)
        held = pl.ds(at, LANES)
        out_ref[:, lanes] = settle(
            feature_ref[:, lanes], one_ref[:, held], two_ref[:, held], three_ref[:, held],
            bias_ref[:, lanes], scale_ref[:, lanes],
        )
        place += 1


def finish(order, features, sums, bias, scale):
    parts, place = [], 0
    for group in sums[:-1]:
        parts.append(part(place, order, features, group, bias, scale))
        place += group[0].shape[1] // LANES
    return pl.pallas_call(
        functools.partial(finish_kernel, len(parts)),
        out_shape=jax.ShapeDtypeStruct(features.shape, BF16),
        in_specs=[SMEM] + [VMEM] * (len(parts) + 6),
        out_specs=VMEM,
        compiler_params=PARAMS,
    )(order, features, *parts, *sums[-1], bias, scale)


def after(value, *earlier):
    return lax.optimization_barrier((value,) + earlier)[0]


STEPS = (0, 1, 3, 2)


def chunk_order(weight):
    count = lax.axis_size("lon")
    if weight.shape[0] != LANES:
        return jnp.arange(count * weight.shape[0] // LANES, dtype=jnp.int32)
    me = lax.axis_index("lon").astype(jnp.int32)
    group, side = me // 2, me % 2
    return jnp.stack(
        [((group - step) % (count // 2)) * 2 + (side ^ flip) for step in STEPS for flip in range(2)]
    ).astype(jnp.int32)


def local(
    features,
    depth_kernel,
    depth_bias,
    norm_gain,
    norm_bias,
    up_weight,
    up_bias,
    down_weight,
    down_bias,
    layer_scale,
):
    rows, cols, chans = features.shape
    lats, lons = lax.axis_size("lat"), lax.axis_size("lon")
    line = lambda v: v.reshape(1, -1)

    forward = [(i, i + 1) for i in range(lats - 1)]
    order = chunk_order(up_weight)
    conv_args = (depth_kernel.reshape(49, chans), line(depth_bias), line(norm_gain), line(norm_bias))
    z_of = lambda w, k: shift(w, "lon", k, 2)
    x_of = lambda w: swap(w, "lon", 1)
    if up_weight.shape[0] == LANES:
        both = jnp.concatenate([up_weight, down_weight], axis=0)
        first, last = edges(features)
        left = lax.ppermute(last, "lon", [(i, (i + 1) % lons) for i in range(lons)])
        right = lax.ppermute(first, "lon", [((i + 1) % lons, i) for i in range(lons)])
        top, bottom = rims(features, left, right)
        low = lax.ppermute(bottom, "lat", forward)
        high = lax.ppermute(top, "lat", [(b, a) for a, b in forward])
        uz1 = z_of(after(up_weight, first), 1)
        x0 = x_of(after(both, left))
        z3 = z_of(after(both, left), 3)
        uz2 = z_of(after(uz1, low), 1)
        ux1 = x_of(after(uz1, high))
        x3 = x_of(after(z3, ux1))
        ux2 = x_of(after(uz2, x0))
        dz1 = z_of(jnp.concatenate([after(down_weight, uz2), x0[LANES:]], axis=0), 1)
        dz2 = z_of(dz1, 1)
        normed = conv_norm(order, features, low, high, left, right, *conv_args)
        across = swap(normed, "lat", 2)
        beside = swap(after(normed, x0, ux1, uz2), "lat", 1)
        opposite = swap(after(across, beside, x3), "lat", 1)
        up_shards = [(up_weight, 0, LANES), (x0, 0, LANES), (uz1, 0, LANES), (ux1, 0, LANES), (z3, 0, LANES), (x3, 0, LANES), (uz2, 0, LANES), (ux2, 0, LANES)]
        hid_opposite, hid_across, hid_beside, hid_own = up([opposite, across, beside, normed], up_shards, line(up_bias))
        down_a = [(down_weight, 0, LANES), (x0, LANES, LANES), (dz1, 0, 2 * LANES), (z3, LANES, LANES), (x3, LANES, LANES)]
        far_opp_a, = down([hid_opposite], down_a)
        far_acr_a, = down([hid_across], down_a)
        far_in_a = swap(far_opp_a, "lat", 1)
        far_a = add(far_acr_a, far_in_a)
        arrived_a = swap(far_a, "lat", 2)
        near_bes_a, near_own_a = down([hid_beside, hid_own], down_a)
        near_in_a = swap(near_bes_a, "lat", 1)
        down_b = [(dz2, 0, 2 * LANES)]
        far_opp_b, = down([hid_opposite], down_b)
        far_acr_b, = down([hid_across], down_b)
        far_in_b = swap(far_opp_b, "lat", 1)
        far_b = add(far_acr_b, far_in_b)
        arrived_b = swap(far_b, "lat", 2)
        near_bes_b, near_own_b = down([hid_beside, hid_own], down_b)
        near_in_b = swap(near_bes_b, "lat", 1)
        sums = [(near_own_a, near_in_a, arrived_a), (near_own_b, near_in_b, arrived_b)]
    else:
        up_shards = [(lax.all_gather(up_weight, "lon", axis=0, tiled=True), 0, chans)]
        down_a = [(lax.all_gather(down_weight, "lon", axis=0, tiled=True), 0, chans)]
        first, last = edges(features)
        left = lax.ppermute(last, "lon", [(i, (i + 1) % lons) for i in range(lons)])
        right = lax.ppermute(first, "lon", [((i + 1) % lons, i) for i in range(lons)])
        top, bottom = rims(features, left, right)
        low = lax.ppermute(bottom, "lat", forward)
        high = lax.ppermute(top, "lat", [(b, a) for a, b in forward])
        normed = conv_norm(order, features, low, high, left, right, *conv_args)
        across = swap(normed, "lat", 2)
        beside = swap(normed, "lat", 1)
        opposite = swap(across, "lat", 1)
        hid_opposite, hid_across, hid_beside, hid_own = up([opposite, across, beside, normed], up_shards, line(up_bias))
        far_opp_a, = down([hid_opposite], down_a)
        far_acr_a, = down([hid_across], down_a)
        far_in_a = swap(far_opp_a, "lat", 1)
        far_a = add(far_acr_a, far_in_a)
        arrived_a = swap(far_a, "lat", 2)
        near_bes_a, near_own_a = down([hid_beside, hid_own], down_a)
        near_in_a = swap(near_bes_a, "lat", 1)
        sums = [(near_own_a, near_in_a, arrived_a)]
    updated = finish(
        order, features.reshape(rows * cols, chans), sums, line(down_bias), line(layer_scale)
    )
    return updated.reshape(rows, cols, chans)


def solution(mesh):
    placed = (
        P("lat", "lon", None),
        P(),
        P(),
        P(),
        P(),
        P("lon", "lat"),
        P("lat"),
        P("lon", "lat"),
        P(),
        P(),
    )
    return jax.shard_map(
        local, mesh=mesh, in_specs=placed, out_specs=P("lat", "lon", None), check_vma=False
    )
```

time: 135 us -> 82.9 us (0.61)
  the two profiles are of different devices: /device:TPU:28 before, /device:TPU:0 now
where the time goes in v2:
time: 82.9 us; the launch traced here: 82.7 us
  waiting for transfers between devices  41.6 us (50%)
  starting transfers between devices  21.9 us (26%)
  Pallas kernels  16.2 us (20%)
  local copies, waits for them, and re-layouts  1.83 us (2%)
  other arithmetic  0.86 us (1%)
    ppermute x13, waiting for transfers between devices, swap(): return lax.ppermute(value, axis, [(i, i ^ bit) for i in range(count)])  29.5 us
    ppermute x13, starting transfers between devices, swap(): return lax.ppermute(value, axis, [(i, i ^ bit) for i in range(count)])  9.21 us
    pallas_call x1, Pallas kernels, conv_norm(): pl.pallas_call(conv_kernel, out_shape=jax.ShapeDtypeStruct((rows * cols,...  4.98 us
    ppermute x1, waiting for transfers between devices, local(): left = lax.ppermute(last, 'lon', [(i, (i + 1) % lons) for i in range(lons)])  4.87 us
    pallas_call x6, Pallas kernels, down(): pl.pallas_call(functools.partial(down_kernel, len(hidden), spans), out_sh...  4.37 us
    ppermute x5, starting transfers between devices, shift(): lax.ppermute(value, axis, [(i, (i + step * inner) % count) for i in range...  3.86 us
    pallas_call x1, Pallas kernels, up(): pl.pallas_call(functools.partial(up_kernel, len(pixels), spans), out_shap...  3.78 us
    ppermute x5, waiting for transfers between devices, shift(): lax.ppermute(value, axis, [(i, (i + step * inner) % count) for i in range...  3.61 us
  transfers between devices with their start and end apart: 22, of which 9 were waited for; matrix products, arithmetic and copies ran while one was open for 1% of the time, Pallas kernels for 17%

profile of v2, /device:TPU:0, one launch (start us, length us, event | category | flops | bytes accessed | tf_op | source)
XLA Modules:
  0.0 82.7 jit_solution(5454088156425674066)
XLA Ops:
  0.0 1.0 %copy-done = bf16[32,8,1024]{2,1,0:T(8,128)(2,1)S(1)} copy-done((bf16[32,8,1024]{2,1,0:T(8,128)(2,1)S(1)}, bf16[32,8,1024]{2,1,0:T(8,128)(2,1)}, u32[]{:S(2)}) %copy-start) | copy-done | bytes 524312
  1.0 0.4 shard_map.100
  1.5 3.0 %collective-permute-start = (bf16[3,32,1024]{2,1,0:T(8,128)(2,1)S(1)}, bf16[3,32,1024]{2,1,0:T(8,128)(2,1)S(1)}, u32[]{:S(2)}, u32[]{:S(2)}) collective-permute-start(bf16[3,32,1024]{2,1,0:T(8,128)(2,1)S(1)} %get-tuple-element.26), channel_id=1, source_target_pairs={{0,1},{1,2},{2,3},{3,4},{4,5},{5,6},{6,7},{7,0},{8,9},{9,10},{10,1... | collective-permute-start | bytes 589832 | tf_op jit(solution)/shard_map/ppermute | solution.py:326
  4.4 3.1 %collective-permute-start.1 = (bf16[3,32,1024]{2,1,0:T(8,128)(2,1)S(1)}, bf16[3,32,1024]{2,1,0:T(8,128)(2,1)S(1)}, u32[]{:S(2)}, u32[]{:S(2)}) collective-permute-start(bf16[3,32,1024]{2,1,0:T(8,128)(2,1)S(1)} %get-tuple-element.27), channel_id=1, source_target_pairs={{1,0},{2,1},{3,2},{4,3},{5,4},{6,5},{7,6},{0,7},{9,8},{10,9},{11,1... | collective-permute-start | bytes 589832 | tf_op jit(solution)/shard_map/ppermute | solution.py:327
  7.6 0.8 %pad_maximum_fusion = bf16[256,1024]{1,0:T(8,128)(2,1)} fusion(bf16[128,1024]{1,0:T(8,128)(2,1)S(1)} %copy-done.2, bf16[128,1024]{1,0:T(8,128)(2,1)S(1)} %copy-done.3), kind=kLoop, calls=%fused_computation | loop fusion | flops 1048576 | bytes 1048576 | tf_op jit(solution)/shard_map/concatenate | solution.py:324
  8.4 4.9 %collective-permute-done.left_ref = bf16[3,32,1024]{2,1,0:T(8,128)(2,1)S(1)} collective-permute-done((bf16[3,32,1024]{2,1,0:T(8,128)(2,1)S(1)}, bf16[3,32,1024]{2,1,0:T(8,128)(2,1)S(1)}, u32[]{:S(2)}, u32[]{:S(2)}) %collective-permute-start) | collective-permute-done | bytes 196640 | tf_op jit(solution)/shard_map/ppermute | solution.py:326
  13.3 2.0 %collective-permute-start.5 = (bf16[256,1024]{1,0:T(8,128)(2,1)}, bf16[256,1024]{1,0:T(8,128)(2,1)S(1)}, u32[]{:S(2)}, u32[]{:S(2)}) collective-permute-start(bf16[256,1024]{1,0:T(8,128)(2,1)} %pad_maximum_fusion), channel_id=1, source_target_pairs={{0,1},{1,0},{2,3},{3,2},{4,5},{5,4},{6,7},{7,6},{8,9},{9,8},{10,11... | collective-permute-start | bytes 1572872 | tf_op jit(solution)/shard_map/ppermute | solution.py:25
  15.3 3.6 %collective-permute-start.10 = (bf16[256,1024]{1,0:T(8,128)(2,1)}, bf16[256,1024]{1,0:T(8,128)(2,1)S(1)}, u32[]{:S(2)}, u32[]{:S(2)}) collective-permute-start(bf16[256,1024]{1,0:T(8,128)(2,1)} %pad_maximum_fusion), channel_id=1, source_target_pairs={{0,6},{1,7},{2,0},{3,1},{4,2},{5,3},{6,4},{7,5},{8,14},{9,15},{10,... | collective-permute-start | bytes 1572872 | tf_op jit(solution)/shard_map/ppermute | solution.py:20
  18.9 0.2 shard_map.101
  19.1 1.4 %collective-permute-start.2 = (bf16[48,1024]{1,0:T(8,128)(2,1)S(1)}, bf16[48,1024]{1,0:T(8,128)(2,1)S(1)}, u32[]{:S(2)}, u32[]{:S(2)}) collective-permute-start(bf16[48,1024]{1,0:T(8,128)(2,1)S(1)} %get-tuple-element.28), channel_id=1, source_target_pairs={{0,8},{8,16},{16,24},{1,9},{9,17},{17,25},{2,10},{10,18},{18,26},{... | collective-permute-start | bytes 294920 | tf_op jit(solution)/shard_map/ppermute | solution.py:329
  20.6 1.3 %collective-permute-start.3 = (bf16[48,1024]{1,0:T(8,128)(2,1)S(1)}, bf16[48,1024]{1,0:T(8,128)(2,1)S(1)}, u32[]{:S(2)}, u32[]{:S(2)}) collective-permute-start(bf16[48,1024]{1,0:T(8,128)(2,1)S(1)} %get-tuple-element.29), channel_id=1, source_target_pairs={{8,0},{16,8},{24,16},{9,1},{17,9},{25,17},{10,2},{18,10},{26,18},{... | collective-permute-start | bytes 294920 | tf_op jit(solution)/shard_map/ppermute | solution.py:330
  21.9 0.1 collective-permute-start.8
  21.9 3.6 %collective-permute-done.3.high_ref = bf16[48,1024]{1,0:T(8,128)(2,1)S(1)} collective-permute-done((bf16[48,1024]{1,0:T(8,128)(2,1)S(1)}, bf16[48,1024]{1,0:T(8,128)(2,1)S(1)}, u32[]{:S(2)}, u32[]{:S(2)}) %collective-permute-start.3) | collective-permute-done | bytes 98336 | tf_op jit(solution)/shard_map/ppermute | solution.py:330
  25.6 0.0 copy-start.8
  25.6 0.1 stack.35.order_ref
  25.7 0.6 copy-done.8
  26.2 0.0 copy-done.6
  26.3 0.0 copy-done.7
  26.3 5.0 %shard_map.102.refs_3_ = bf16[256,1024]{1,0:T(8,128)(2,1)S(1)} custom-call(s32[8]{0:T(128)S(1)} %stack.35.order_ref, bf16[32,8,1024]{2,1,0:T(8,128)(2,1)S(1)} %copy-done.1, bf16[48,1024]{1,0:T(8,128)(2,1)S(1)} %collective-permute-done.2.low_ref, bf16[48,1024]{1,0:T(8,128)(2,1)S(1)} %collective-permute-done.3.high_ref, ...), custom_call_target="tpu_custom_call" | custom-call | flops 26214400 | bytes 2097152 | tf_op jit(solution)/shard_map/pallas_call | solution.py:137
  31.3 3.1 %collective-permute-start.4 = (bf16[256,1024]{1,0:T(8,128)(2,1)S(1)}, bf16[256,1024]{1,0:T(8,128)(2,1)S(1)}, u32[]{:S(2)}, u32[]{:S(2)}) collective-permute-start(bf16[256,1024]{1,0:T(8,128)(2,1)S(1)} %shard_map.102.refs_3_), channel_id=1, source_target_pairs={{0,16},{8,24},{16,0},{24,8},{1,17},{9,25},{17,1},{25,9},{2,18},{10... | collective-permute-start | bytes 1572872 | tf_op jit(solution)/shard_map/ppermute | solution.py:25
  34.4 2.0 %collective-permute-done.8.refs_10_ = bf16[128,1024]{1,0:T(8,128)(2,1)S(1)} collective-permute-done((bf16[128,1024]{1,0:T(8,128)(2,1)S(1)}, bf16[128,1024]{1,0:T(8,128)(2,1)S(1)}, u32[]{:S(2)}, u32[]{:S(2)}) %collective-permute-start.8) | collective-permute-done | bytes 262176 | tf_op jit(solution)/shard_map/ppermute | solution.py:20
  36.4 0.4 collective-permute-start.11
  36.8 0.2 collective-permute-start.14
  37.0 9.5 %collective-permute-done.4.refs_1_ = bf16[256,1024]{1,0:T(8,128)(2,1)S(1)} collective-permute-done((bf16[256,1024]{1,0:T(8,128)(2,1)S(1)}, bf16[256,1024]{1,0:T(8,128)(2,1)S(1)}, u32[]{:S(2)}, u32[]{:S(2)}) %collective-permute-start.4) | collective-permute-done | bytes 524320 | tf_op jit(solution)/shard_map/ppermute | solution.py:25
  46.5 4.2 %collective-permute-done.11.refs_9_.refs_6_.refs_5_ = bf16[256,1024]{1,0:T(8,128)(2,1)S(1)} collective-permute-done((bf16[256,1024]{1,0:T(8,128)(2,1)S(1)}, bf16[256,1024]{1,0:T(8,128)(2,1)S(1)}, u32[]{:S(2)}, u32[]{:S(2)}) %collective-permute-start.11) | collective-permute-done | bytes 524320 | tf_op jit(solution)/shard_map/ppermute | solution.py:25
  50.7 0.3 collective-permute-start.13
  51.0 1.6 %collective-permute-done.14.refs_4_.refs_3_ = bf16[256,1024]{1,0:T(8,128)(2,1)S(1)} collective-permute-done((bf16[256,1024]{1,0:T(8,128)(2,1)S(1)}, bf16[256,1024]{1,0:T(8,128)(2,1)S(1)}, u32[]{:S(2)}, u32[]{:S(2)}) %collective-permute-start.14) | collective-permute-done | bytes 524320 | tf_op jit(solution)/shard_map/ppermute | solution.py:20
  52.6 6.8 %collective-permute-done.13.refs_11_ = bf16[128,1024]{1,0:T(8,128)(2,1)S(1)} collective-permute-done((bf16[128,1024]{1,0:T(8,128)(2,1)S(1)}, bf16[128,1024]{1,0:T(8,128)(2,1)S(1)}, u32[]{:S(2)}, u32[]{:S(2)}) %collective-permute-start.13) | collective-permute-done | bytes 262176 | tf_op jit(solution)/shard_map/ppermute | solution.py:25
  59.4 3.8 %shard_map.103 = (bf16[256,1024]{1,0:T(8,128)(2,1)S(1)}, bf16[256,1024]{1,0:T(8,128)(2,1)S(1)}, bf16[256,1024]{1,0:T(8,128)(2,1)S(1)}, bf16[256,1024]{1,0:T(8,128)(2,1)S(1)}) custom-call(bf16[256,1024]{1,0:T(8,128)(2,1)S(1)} %collective-permute-done.12.refs_0_, bf16[256,1024]{1,0:T(8,128)(2,1)S(1)} %collective-permute-done.4.refs_1_, ...), custom_call_target="tpu_custom_call" | custom-call | flops 2147483648 | bytes 6291456 | tf_op jit(solution)/shard_map/pallas_call | solution.py:172
  63.2 0.8 %shard_map.106 = bf16[256,768]{1,0:T(8,128)(2,1)S(1)} custom-call(bf16[256,1024]{1,0:T(8,128)(2,1)S(1)} %get-tuple-element.44.refs_0_, bf16[128,1024]{1,0:T(8,128)(2,1)S(1)} %copy-done.2, bf16[256,1024]{1,0:T(8,128)(2,1)S(1)} %collective-permute-done.5.refs_5_.refs_3_.refs_2_, bf16[256,1024]{1,0:T(8,128)(2,1)S(1)} %collective-permute-done.14.refs_4_.refs_3_, ...), custom_call_target="tpu_custom_call" | custom-call | flops 402653184 | bytes 6291456 | tf_op jit(solution)/shard_map/pallas_call | solution.py:200
  64.1 0.1 collective-permute-start.16
  64.1 1.5 %shard_map.104 = (bf16[256,768]{1,0:T(8,128)(2,1)S(1)}, bf16[256,768]{1,0:T(8,128)(2,1)S(1)}) custom-call(bf16[256,1024]{1,0:T(8,128)(2,1)S(1)} %get-tuple-element.38.refs_0_, bf16[256,1024]{1,0:T(8,128)(2,1)S(1)} %get-tuple-element.39.refs_1_, bf16[128,1024]{1,0:T(8,128)(2,1)S(1)} %copy-done.2, ...), custom_call_target="tpu_custom_call" | custom-call | flops 805306368 | bytes 6291456 | tf_op jit(solution)/shard_map/pallas_call | solution.py:200
  65.7 0.6 collective-permute-start.15
  66.2 0.8 %shard_map.105.one_ref = bf16[256,768]{1,0:T(8,128)(2,1)S(1)} custom-call(bf16[256,1024]{1,0:T(8,128)(2,1)S(1)} %get-tuple-element.43.refs_0_, bf16[128,1024]{1,0:T(8,128)(2,1)S(1)} %copy-done.2, bf16[256,1024]{1,0:T(8,128)(2,1)S(1)} %collective-permute-done.5.refs_5_.refs_3_.refs_2_, bf16[256,1024]{1,0:T(8,128)(2,1)S(1)} %collective-permute-done.14.refs_4_.refs_3_, ...), custom_call_target="tpu_custom_call" | custom-call | flops 402653184 | bytes 6291456 | tf_op jit(solution)/shard_map/pallas_call | solution.py:200
  67.1 0.1 shard_map.107
  67.2 1.6 %collective-permute-start.17 = (bf16[256,768]{1,0:T(8,128)(2,1)S(1)}, bf16[256,768]{1,0:T(8,128)(2,1)S(1)}, u32[]{:S(2)}, u32[]{:S(2)}) collective-permute-start(bf16[256,768]{1,0:T(8,128)(2,1)S(1)} %shard_map.107), channel_id=1, source_target_pairs={{0,16},{8,24},{16,0},{24,8},{1,17},{9,25},{17,1},{25,9},{2,18},{10... | collective-permute-start | bytes 1179656 | tf_op jit(solution)/shard_map/ppermute | solution.py:25
  68.8 0.3 shard_map.111
  69.1 0.1 collective-permute-start.20
  69.2 0.5 shard_map.109
  69.7 0.6 collective-permute-start.19
  70.3 0.3 shard_map.110.one_ref
  70.6 0.0 copy-start.5
  70.7 0.0 copy-start.4
  70.7 0.6 collective-permute-start.21
  71.3 8.0 %collective-permute-done.17.three_ref = bf16[256,768]{1,0:T(8,128)(2,1)S(1)} collective-permute-done((bf16[256,768]{1,0:T(8,128)(2,1)S(1)}, bf16[256,768]{1,0:T(8,128)(2,1)S(1)}, u32[]{:S(2)}, u32[]{:S(2)}) %collective-permute-start.17) | collective-permute-done | bytes 393248 | tf_op jit(solution)/shard_map/ppermute | solution.py:25
  79.3 0.8 %shard_map.108.refs_0_ = bf16[256,768]{1,0:T(8,128)(2,1)S(1)} custom-call(s32[8]{0:T(128)S(1)} %stack.35.order_ref, bf16[256,1024]{1,0:T(8,128)(2,1)S(1)} %bitcast.16, bf16[256,768]{1,0:T(8,128)(2,1)S(1)} %get-tuple-element.41.one_ref, bf16[256,768]{1,0:T(8,128)(2,1)S(1)} %collective-permute-done.15.two_ref, ...), custom_call_target="tpu_custom_call" | custom-call | tf_op jit(solution)/shard_map/pallas_call | solution.py:243
  80.1 1.0 %collective-permute-done.21.refs_3_ = bf16[256,256]{1,0:T(8,128)(2,1)S(1)} collective-permute-done((bf16[256,256]{1,0:T(8,128)(2,1)S(1)}, bf16[256,256]{1,0:T(8,128)(2,1)S(1)}, u32[]{:S(2)}, u32[]{:S(2)}) %collective-permute-start.21) | collective-permute-done | bytes 131104 | tf_op jit(solution)/shard_map/ppermute | solution.py:25
  81.1 1.5 %shard_map.113 = bf16[256,1024]{1,0:T(8,128)(2,1)} custom-call(s32[8]{0:T(128)S(1)} %stack.35.order_ref, bf16[256,1024]{1,0:T(8,128)(2,1)S(1)} %bitcast.17, bf16[256,768]{1,0:T(8,128)(2,1)S(1)} %shard_map.108.refs_0_, bf16[256,256]{1,0:T(8,128)(2,1)S(1)} %get-tuple-element.45.refs_1_, bf16[256,256]{1,0:T(8,128)(2,1)S(1)} %collective-permute-done.19.refs_2_, ...), custom_call_target="tpu_custom_call" | custom-call | tf_op jit(solution)/shard_map/pallas_call | solution.py:275
  (37 shorter events, 0.2 us)
Async XLA Ops:
  0.0 1.0 %copy-start = (bf16[32,8,1024]{2,1,0:T(8,128)(2,1)S(1)}, bf16[32,8,1024]{2,1,0:T(8,128)(2,1)}, u32[]{:S(2)}) copy-start(bf16[32,8,1024]{2,1,0:T(8,128)(2,1)} %mid_ref.5) | copy-start | bytes 1572868
  1.0 6.5 %copy-start.3 = (bf16[128,1024]{1,0:T(8,128)(2,1)S(1)}, bf16[128,1024]{1,0:T(8,128)(2,1)}, u32[]{:S(2)}) copy-start(bf16[128,1024]{1,0:T(8,128)(2,1)} %refs_4_.1) | copy-start | bytes 786436
  1.0 6.5 %copy-start.2 = (bf16[128,1024]{1,0:T(8,128)(2,1)S(1)}, bf16[128,1024]{1,0:T(8,128)(2,1)}, u32[]{:S(2)}) copy-start(bf16[128,1024]{1,0:T(8,128)(2,1)} %refs_1_.3) | copy-start | bytes 786436
  1.5 11.8 %collective-permute-start = (bf16[3,32,1024]{2,1,0:T(8,128)(2,1)S(1)}, bf16[3,32,1024]{2,1,0:T(8,128)(2,1)S(1)}, u32[]{:S(2)}, u32[]{:S(2)}) collective-permute-start(bf16[3,32,1024]{2,1,0:T(8,128)(2,1)S(1)} %get-tuple-element.26), channel_id=1, source_target_pairs={{0,1},{1,2},{2,3},{3,4},{4,5},{5,6},{6,7},{7,0},{8,9},{9,10},{10,1... | collective-permute-start | bytes 589832 | tf_op jit(solution)/shard_map/ppermute | solution.py:326
  4.4 14.5 %collective-permute-start.1 = (bf16[3,32,1024]{2,1,0:T(8,128)(2,1)S(1)}, bf16[3,32,1024]{2,1,0:T(8,128)(2,1)S(1)}, u32[]{:S(2)}, u32[]{:S(2)}) collective-permute-start(bf16[3,32,1024]{2,1,0:T(8,128)(2,1)S(1)} %get-tuple-element.27), channel_id=1, source_target_pairs={{1,0},{2,1},{3,2},{4,3},{5,4},{6,5},{7,6},{0,7},{9,8},{10,9},{11,1... | collective-permute-start | bytes 589832 | tf_op jit(solution)/shard_map/ppermute | solution.py:327
  7.6 14.3 %collective-permute-start.6 = (bf16[128,1024]{1,0:T(8,128)(2,1)S(1)}, bf16[128,1024]{1,0:T(8,128)(2,1)S(1)}, u32[]{:S(2)}, u32[]{:S(2)}) collective-permute-start(bf16[128,1024]{1,0:T(8,128)(2,1)S(1)} %copy-done.3), channel_id=1, source_target_pairs={{0,2},{1,3},{2,4},{3,5},{4,6},{5,7},{6,0},{7,1},{8,10},{9,11},{10,... | collective-permute-start | bytes 786440 | tf_op jit(solution)/shard_map/ppermute | solution.py:20
  8.4 17.3 %copy-start.1 = (bf16[32,8,1024]{2,1,0:T(8,128)(2,1)S(1)}, bf16[32,8,1024]{2,1,0:T(8,128)(2,1)}, u32[]{:S(2)}) copy-start(bf16[32,8,1024]{2,1,0:T(8,128)(2,1)} %mid_ref.5) | copy-start | bytes 1572868
  13.3 23.1 %collective-permute-start.5 = (bf16[256,1024]{1,0:T(8,128)(2,1)}, bf16[256,1024]{1,0:T(8,128)(2,1)S(1)}, u32[]{:S(2)}, u32[]{:S(2)}) collective-permute-start(bf16[256,1024]{1,0:T(8,128)(2,1)} %pad_maximum_fusion), channel_id=1, source_target_pairs={{0,1},{1,0},{2,3},{3,2},{4,5},{5,4},{6,7},{7,6},{8,9},{9,8},{10,11... | collective-permute-start | bytes 1572872 | tf_op jit(solution)/shard_map/ppermute | solution.py:25
  15.3 21.0 %collective-permute-start.10 = (bf16[256,1024]{1,0:T(8,128)(2,1)}, bf16[256,1024]{1,0:T(8,128)(2,1)S(1)}, u32[]{:S(2)}, u32[]{:S(2)}) collective-permute-start(bf16[256,1024]{1,0:T(8,128)(2,1)} %pad_maximum_fusion), channel_id=1, source_target_pairs={{0,6},{1,7},{2,0},{3,1},{4,2},{5,3},{6,4},{7,5},{8,14},{9,15},{10,... | collective-permute-start | bytes 1572872 | tf_op jit(solution)/shard_map/ppermute | solution.py:20
  19.1 6.4 %copy-start.10 = (bf16[7,7,1024]{2,1,0:T(8,128)(2,1)S(1)}, bf16[7,7,1024]{2,1,0:T(8,128)(2,1)}, u32[]{:S(2)}) copy-start(bf16[7,7,1024]{2,1,0:T(8,128)(2,1)} %param.11) | copy-start | bytes 301060
  19.1 2.7 %collective-permute-start.2 = (bf16[48,1024]{1,0:T(8,128)(2,1)S(1)}, bf16[48,1024]{1,0:T(8,128)(2,1)S(1)}, u32[]{:S(2)}, u32[]{:S(2)}) collective-permute-start(bf16[48,1024]{1,0:T(8,128)(2,1)S(1)} %get-tuple-element.28), channel_id=1, source_target_pairs={{0,8},{8,16},{16,24},{1,9},{9,17},{17,25},{2,10},{10,18},{18,26},{... | collective-permute-start | bytes 294920 | tf_op jit(solution)/shard_map/ppermute | solution.py:329
  20.6 4.9 %collective-permute-start.3 = (bf16[48,1024]{1,0:T(8,128)(2,1)S(1)}, bf16[48,1024]{1,0:T(8,128)(2,1)S(1)}, u32[]{:S(2)}, u32[]{:S(2)}) collective-permute-start(bf16[48,1024]{1,0:T(8,128)(2,1)S(1)} %get-tuple-element.29), channel_id=1, source_target_pairs={{8,0},{16,8},{24,16},{9,1},{17,9},{25,17},{10,2},{18,10},{26,18},{... | collective-permute-start | bytes 294920 | tf_op jit(solution)/shard_map/ppermute | solution.py:330
  21.9 14.5 %collective-permute-start.8 = (bf16[128,1024]{1,0:T(8,128)(2,1)S(1)}, bf16[128,1024]{1,0:T(8,128)(2,1)S(1)}, u32[]{:S(2)}, u32[]{:S(2)}) collective-permute-start(bf16[128,1024]{1,0:T(8,128)(2,1)S(1)} %collective-permute-done.6.refs_6_), channel_id=1, source_target_pairs={{0,2},{1,3},{2,4},{3,5},{4,6},{5,7},{6,0},{7,1},{8,10},{9,11},{10,... | collective-permute-start | bytes 786440 | tf_op jit(solution)/shard_map/ppermute | solution.py:20
  25.5 10.8 %collective-permute-start.7 = (bf16[128,1024]{1,0:T(8,128)(2,1)S(1)}, bf16[128,1024]{1,0:T(8,128)(2,1)}, u32[]{:S(2)}, u32[]{:S(2)}) collective-permute-start(bf16[128,1024]{1,0:T(8,128)(2,1)S(1)} %collective-permute-done.6.refs_6_), channel_id=1, source_target_pairs={{0,1},{1,0},{2,3},{3,2},{4,5},{5,4},{6,7},{7,6},{8,9},{9,8},{10,11... | collective-permute-start | bytes 786440 | tf_op jit(solution)/shard_map/ppermute | solution.py:25
  25.6 0.7 copy-start.8
  25.6 0.7 copy-start.6
  25.6 0.7 copy-start.7
  31.3 15.2 %collective-permute-start.4 = (bf16[256,1024]{1,0:T(8,128)(2,1)S(1)}, bf16[256,1024]{1,0:T(8,128)(2,1)S(1)}, u32[]{:S(2)}, u32[]{:S(2)}) collective-permute-start(bf16[256,1024]{1,0:T(8,128)(2,1)S(1)} %shard_map.102.refs_3_), channel_id=1, source_target_pairs={{0,16},{8,24},{16,0},{24,8},{1,17},{9,25},{17,1},{25,9},{2,18},{10... | collective-permute-start | bytes 1572872 | tf_op jit(solution)/shard_map/ppermute | solution.py:25
  36.3 10.2 %collective-permute-start.9 = (bf16[256,1024]{1,0:T(8,128)(2,1)S(1)}, bf16[256,1024]{1,0:T(8,128)(2,1)S(1)}, u32[]{:S(2)}, u32[]{:S(2)}) collective-permute-start(bf16[256,1024]{1,0:T(8,128)(2,1)S(1)} %shard_map.102.refs_3_), channel_id=1, source_target_pairs={{0,8},{8,0},{16,24},{24,16},{1,9},{9,1},{17,25},{25,17},{2,10},{10... | collective-permute-start | bytes 1572872 | tf_op jit(solution)/shard_map/ppermute | solution.py:25
  36.4 14.3 %collective-permute-start.11 = (bf16[256,1024]{1,0:T(8,128)(2,1)S(1)}, bf16[256,1024]{1,0:T(8,128)(2,1)S(1)}, u32[]{:S(2)}, u32[]{:S(2)}) collective-permute-start(bf16[256,1024]{1,0:T(8,128)(2,1)S(1)} %collective-permute-done.10.refs_8_.refs_5_.refs_4_), channel_id=1, source_target_pairs={{0,1},{1,0},{2,3},{3,2},{4,5},{5,4},{6,7},{7,6},{8,9},{9,8},{10,11... | collective-permute-start | bytes 1572872 | tf_op jit(solution)/shard_map/ppermute | solution.py:25
  36.7 22.7 %copy-start.9 = (f32[1024]{0:T(1024)S(1)}, f32[1024]{0:T(1024)}, u32[]{:S(2)}) copy-start(f32[1024]{0:T(1024)} %param.16) | copy-start | bytes 12292
  36.8 15.8 %collective-permute-start.14 = (bf16[256,1024]{1,0:T(8,128)(2,1)S(1)}, bf16[256,1024]{1,0:T(8,128)(2,1)S(1)}, u32[]{:S(2)}, u32[]{:S(2)}) collective-permute-start(bf16[256,1024]{1,0:T(8,128)(2,1)S(1)} %pad_maximum_fusion.1), channel_id=1, source_target_pairs={{0,2},{1,3},{2,4},{3,5},{4,6},{5,7},{6,0},{7,1},{8,10},{9,11},{10,... | collective-permute-start | bytes 1572872 | tf_op jit(solution)/shard_map/ppermute | solution.py:20
  50.7 8.7 %collective-permute-start.12 = (bf16[256,1024]{1,0:T(8,128)(2,1)S(1)}, bf16[256,1024]{1,0:T(8,128)(2,1)S(1)}, u32[]{:S(2)}, u32[]{:S(2)}) collective-permute-start(bf16[256,1024]{1,0:T(8,128)(2,1)S(1)} %collective-permute-done.4.refs_1_), channel_id=1, source_target_pairs={{0,8},{8,0},{16,24},{24,16},{1,9},{9,1},{17,25},{25,17},{2,10},{10... | collective-permute-start | bytes 1572872 | tf_op jit(solution)/shard_map/ppermute | solution.py:25
  50.7 8.7 %collective-permute-start.13 = (bf16[128,1024]{1,0:T(8,128)(2,1)S(1)}, bf16[128,1024]{1,0:T(8,128)(2,1)S(1)}, u32[]{:S(2)}, u32[]{:S(2)}) collective-permute-start(bf16[128,1024]{1,0:T(8,128)(2,1)S(1)} %collective-permute-done.8.refs_10_), channel_id=1, source_target_pairs={{0,1},{1,0},{2,3},{3,2},{4,5},{5,4},{6,7},{7,6},{8,9},{9,8},{10,11... | collective-permute-start | bytes 786440 | tf_op jit(solution)/shard_map/ppermute | solution.py:25
  52.6 16.2 %collective-permute-start.18 = (bf16[256,1024]{1,0:T(8,128)(2,1)S(1)}, bf16[256,1024]{1,0:T(8,128)(2,1)S(1)}, u32[]{:S(2)}, u32[]{:S(2)}) collective-permute-start(bf16[256,1024]{1,0:T(8,128)(2,1)S(1)} %collective-permute-done.14.refs_4_.refs_3_), channel_id=1, source_target_pairs={{0,2},{1,3},{2,4},{3,5},{4,6},{5,7},{6,0},{7,1},{8,10},{9,11},{10,... | collective-permute-start | bytes 1572872 | tf_op jit(solution)/shard_map/ppermute | solution.py:20
  64.1 3.0 %collective-permute-start.16 = (bf16[256,768]{1,0:T(8,128)(2,1)S(1)}, bf16[256,768]{1,0:T(8,128)(2,1)S(1)}, u32[]{:S(2)}, u32[]{:S(2)}) collective-permute-start(bf16[256,768]{1,0:T(8,128)(2,1)S(1)} %shard_map.106), channel_id=1, source_target_pairs={{0,8},{8,0},{16,24},{24,16},{1,9},{9,1},{17,25},{25,17},{2,10},{10... | collective-permute-start | bytes 1179656 | tf_op jit(solution)/shard_map/ppermute | solution.py:25
  65.7 5.6 %collective-permute-start.15 = (bf16[256,768]{1,0:T(8,128)(2,1)S(1)}, bf16[256,768]{1,0:T(8,128)(2,1)S(1)}, u32[]{:S(2)}, u32[]{:S(2)}) collective-permute-start(bf16[256,768]{1,0:T(8,128)(2,1)S(1)} %get-tuple-element.42), channel_id=1, source_target_pairs={{0,8},{8,0},{16,24},{24,16},{1,9},{9,1},{17,25},{25,17},{2,10},{10... | collective-permute-start | bytes 1179656 | tf_op jit(solution)/shard_map/ppermute | solution.py:25
  67.2 12.0 %collective-permute-start.17 = (bf16[256,768]{1,0:T(8,128)(2,1)S(1)}, bf16[256,768]{1,0:T(8,128)(2,1)S(1)}, u32[]{:S(2)}, u32[]{:S(2)}) collective-permute-start(bf16[256,768]{1,0:T(8,128)(2,1)S(1)} %shard_map.107), channel_id=1, source_target_pairs={{0,16},{8,24},{16,0},{24,8},{1,17},{9,25},{17,1},{25,9},{2,18},{10... | collective-permute-start | bytes 1179656 | tf_op jit(solution)/shard_map/ppermute | solution.py:25
  69.1 1.5 %collective-permute-start.20 = (bf16[256,256]{1,0:T(8,128)(2,1)S(1)}, bf16[256,256]{1,0:T(8,128)(2,1)S(1)}, u32[]{:S(2)}, u32[]{:S(2)}) collective-permute-start(bf16[256,256]{1,0:T(8,128)(2,1)S(1)} %shard_map.111), channel_id=1, source_target_pairs={{0,8},{8,0},{16,24},{24,16},{1,9},{9,1},{17,25},{25,17},{2,10},{10... | collective-permute-start | bytes 393224 | tf_op jit(solution)/shard_map/ppermute | solution.py:25
  69.7 10.4 %collective-permute-start.19 = (bf16[256,256]{1,0:T(8,128)(2,1)S(1)}, bf16[256,256]{1,0:T(8,128)(2,1)S(1)}, u32[]{:S(2)}, u32[]{:S(2)}) collective-permute-start(bf16[256,256]{1,0:T(8,128)(2,1)S(1)} %get-tuple-element.46), channel_id=1, source_target_pairs={{0,8},{8,0},{16,24},{24,16},{1,9},{9,1},{17,25},{25,17},{2,10},{10... | collective-permute-start | bytes 393224 | tf_op jit(solution)/shard_map/ppermute | solution.py:25
  70.6 8.6 %copy-start.5 = (f32[1024]{0:T(1024)S(1)}, f32[1024]{0:T(1024)}, u32[]{:S(2)}) copy-start(f32[1024]{0:T(1024)} %param.19) | copy-start | bytes 12292
  70.7 8.6 %copy-start.4 = (f32[1024]{0:T(1024)S(1)}, f32[1024]{0:T(1024)}, u32[]{:S(2)}) copy-start(f32[1024]{0:T(1024)} %param.18) | copy-start | bytes 12292
  70.7 10.4 %collective-permute-start.21 = (bf16[256,256]{1,0:T(8,128)(2,1)S(1)}, bf16[256,256]{1,0:T(8,128)(2,1)S(1)}, u32[]{:S(2)}, u32[]{:S(2)}) collective-permute-start(bf16[256,256]{1,0:T(8,128)(2,1)S(1)} %shard_map.112), channel_id=1, source_target_pairs={{0,16},{8,24},{16,0},{24,8},{1,17},{9,25},{17,1},{25,9},{2,18},{10... | collective-permute-start | bytes 393224 | tf_op jit(solution)/shard_map/ppermute | solution.py:25

commit v3 on v2

--- a/solution.py
+++ b/solution.py
@@ -149,22 +149,58 @@
     )(order, mid, low, high, left, right, taps, bias, gain, offset)
 
 
-def up_kernel(parts, spans, *refs):
-    pixels, shards, bias_ref = refs[:parts], refs[parts:-parts - 2], refs[-parts - 2]
-    outs, weight = refs[-parts - 1:-1], refs[-1]
+def fill(weight, shards, spans):
     at = 0
     for shard, (start, count) in zip(shards, spans):
         weight[pl.ds(at, count), :] = shard[pl.ds(start, count), :]
         at += count
-    hidden = weight.shape[1]
+
+
+def begin_kernel(parts, spans, *refs):
+    pixels, shards, bias_ref = refs[:parts], refs[parts:-parts - 2], refs[-parts - 2]
+    outs, weight = refs[-parts - 1:-1], refs[-1]
+    fill(weight, shards, spans)
+    depth, hidden = weight.shape
     for pixel, out in zip(pixels, outs):
         for n in range(0, hidden, 256):
             cols = pl.ds(n, 256)
-            pre = jnp.dot(pixel[...], weight[:, cols], preferred_element_type=F32) + bias_ref[:, cols]
+            out[:, cols] = (
+                jnp.dot(pixel[:, pl.ds(0, depth)], weight[:, cols], preferred_element_type=F32) + bias_ref[:, cols]
+            )
+
+
+def begin(pixels, shards, bias):
+    arrays, spans = [s[0] for s in shards], tuple(s[1:] for s in shards)
+    depth = sum(count for _, count in spans)
+    hidden = arrays[0].shape[1]
+    outs = tuple(jax.ShapeDtypeStruct((p.shape[0], hidden), F32) for p in pixels)
+    return pl.pallas_call(
+        functools.partial(begin_kernel, len(pixels), spans),
+        out_shape=outs,
+        in_specs=[VMEM] * (len(pixels) + len(shards) + 1),
+        out_specs=tuple(VMEM for _ in outs),
+        scratch_shapes=[pltpu.VMEM((depth, hidden), BF16)],
+        compiler_params=PARAMS,
+        cost_estimate=pl.CostEstimate(
+            flops=2 * depth * hidden * sum(p.shape[0] for p in pixels), bytes_accessed=1 << 20, transcendentals=0
+        ),
+    )(*pixels, *arrays, bias)
+
+
+def up_kernel(parts, spans, *refs):
+    pixels, sums, shards = refs[:parts], refs[parts:2 * parts], refs[2 * parts:-parts - 1]
+    outs, weight = refs[-parts - 1:-1], refs[-1]
+    fill(weight, shards, spans)
+    depth, hidden = weight.shape
+    for pixel, held, out in zip(pixels, sums, outs):
+        rest = pl.ds(pixel.shape[1] - depth, depth)
+        for n in range(0, hidden, 256):
+            cols = pl.ds(n, 256)
+            pre = held[:, cols] + jnp.dot(pixel[:, rest], weight[:, cols], preferred_element_type=F32)
             out[:, cols] = (0.5 * pre * (1.0 + lax.erf(pre * 0.7071067811865476))).astype(BF16)
 
 
-def up(pixels, shards, bias):
+def up(pixels, sums, shards):
     arrays, spans = [s[0] for s in shards], tuple(s[1:] for s in shards)
     depth = sum(count for _, count in spans)
     hidden = arrays[0].shape[1]
@@ -172,14 +208,14 @@
     return pl.pallas_call(
         functools.partial(up_kernel, len(pixels), spans),
         out_shape=outs,
-        in_specs=[VMEM] * (len(pixels) + len(shards) + 1),
+        in_specs=[VMEM] * (2 * len(pixels) + len(shards)),
         out_specs=tuple(VMEM for _ in outs),
         scratch_shapes=[pltpu.VMEM((depth, hidden), BF16)],
         compiler_params=PARAMS,
         cost_estimate=pl.CostEstimate(
-            flops=2 * depth * hidden * sum(p.shape[0] for p in pixels), bytes_accessed=6 << 20, transcendentals=0
+            flops=2 * depth * hidden * sum(p.shape[0] for p in pixels), bytes_accessed=1 << 20, transcendentals=0
         ),
-    )(*pixels, *arrays, bias)
+    )(*pixels, *sums, *arrays)
 
 
 def down_kernel(parts, spans, *refs):
@@ -224,61 +260,42 @@
     )(one, two)
 
 
-def settle(feature, one, two, three, bias, scale):
-    branch = (one.astype(F32) + two.astype(F32)) + three.astype(F32)
-    return (feature.astype(F32) + scale * (branch + bias)).astype(BF16)
-
-
-def part_kernel(first, order_ref, feature_ref, one_ref, two_ref, three_ref, bias_ref, scale_ref, out_ref):
-    for at in range(0, out_ref.shape[1], LANES):
-        lanes = pl.ds(pl.multiple_of(order_ref[first + at // LANES] * LANES, LANES), LANES)
-        held = pl.ds(at, LANES)
-        out_ref[:, held] = settle(
-            feature_ref[:, lanes], one_ref[:, held], two_ref[:, held], three_ref[:, held],
-            bias_ref[:, lanes], scale_ref[:, lanes],
-        )
-
-
-def part(first, order, features, group, bias, scale):
-    return pl.pallas_call(
-        functools.partial(part_kernel, first),
-        out_shape=jax.ShapeDtypeStruct(group[0].shape, BF16),
-        in_specs=[SMEM] + [VMEM] * 6,
-        out_specs=VMEM,
-        compiler_params=PARAMS,
-    )(order, features, *group, bias, scale)
-
-
-def finish_kernel(done, order_ref, feature_ref, *refs):
-    parts, (one_ref, two_ref, three_ref, bias_ref, scale_ref, out_ref) = refs[:done], refs[done:]
-    place = 0
-    for part_ref in parts:
-        for at in range(0, part_ref.shape[1], LANES):
-            lanes = pl.ds(pl.multiple_of(order_ref[place] * LANES, LANES), LANES)
-            out_ref[:, lanes] = part_ref[:, pl.ds(at, LANES)]
-            place += 1
-    for at in range(0, one_ref.shape[1], LANES):
-        lanes = pl.ds(pl.multiple_of(order_ref[place] * LANES, LANES), LANES)
-        held = pl.ds(at, LANES)
-        out_ref[:, lanes] = settle(
-            feature_ref[:, lanes], one_ref[:, held], two_ref[:, held], three_ref[:, held],
-            bias_ref[:, lanes], scale_ref[:, lanes],
-        )
-        place += 1
-
-
-def finish(order, features, sums, bias, scale):
-    parts, place = [], 0
-    for group in sums[:-1]:
-        parts.append(part(place, order, features, group, bias, scale))
-        place += group[0].shape[1] // LANES
-    return pl.pallas_call(
-        functools.partial(finish_kernel, len(parts)),
-        out_shape=jax.ShapeDtypeStruct(features.shape, BF16),
-        in_specs=[SMEM] + [VMEM] * (len(parts) + 6),
-        out_specs=VMEM,
-        compiler_params=PARAMS,
-    )(order, features, *parts, *sums[-1], bias, scale)
+def settle_kernel(first, order_ref, feature_ref, one_ref, two_ref, far_ref, bias_ref, scale_ref, *refs):
+    out_ref, held, sems = refs[-3:]
+    rows, chans = far_ref.shape
+    copies = []
+    for index in range(chans // LANES):
+        lanes = pl.ds(pl.multiple_of(order_ref[first + index] * LANES, LANES), LANES)
+        place = pl.ds(index * LANES, LANES)
+        branch = (one_ref[:, place].astype(F32) + two_ref[:, place].astype(F32)) + far_ref[:, place].astype(F32)
+        held[:, place] = (
+            feature_ref[:, lanes].astype(F32) + scale_ref[:, lanes] * (branch + bias_ref[:, lanes])
+        ).astype(BF16)
+        copies.append(pltpu.make_async_copy(held.at[:, place], out_ref.at[:, lanes], sems.at[index]))
+        copies[-1].start()
+    for copy in copies:
+        copy.wait()
+
+
+def finish(order, features, groups, bias, scale):
+    out, first = None, 0
+    for one, two, far in groups:
+        chans = far.shape[1]
+        operands = (order, features, one, two, far, bias, scale)
+        specs = [SMEM] + [VMEM] * 6
+        if out is not None:
+            operands, specs = operands + (out,), specs + [pl.BlockSpec(memory_space=pltpu.HBM)]
+        out = pl.pallas_call(
+            functools.partial(settle_kernel, first),
+            out_shape=jax.ShapeDtypeStruct(features.shape, BF16),
+            in_specs=specs,
+            out_specs=pl.BlockSpec(memory_space=pltpu.HBM),
+            scratch_shapes=[pltpu.VMEM(far.shape, BF16), pltpu.SemaphoreType.DMA((chans // LANES,))],
+            input_output_aliases={7: 0} if out is not None else {},
+            compiler_params=PARAMS,
+        )(*operands)
+        first += chans // LANES
+    return out
 
 
 def after(value, *earlier):
@@ -330,7 +347,7 @@
         high = lax.ppermute(top, "lat", [(b, a) for a, b in forward])
         uz1 = z_of(after(up_weight, first), 1)
         x0 = x_of(after(both, left))
-        z3 = z_of(after(both, left), 3)
+        z3 = z_of(after(both, first), 3)
         uz2 = z_of(after(uz1, low), 1)
         ux1 = x_of(after(uz1, high))
         x3 = x_of(after(z3, ux1))
@@ -342,7 +359,8 @@
         beside = swap(after(normed, x0, ux1, uz2), "lat", 1)
         opposite = swap(after(across, beside, x3), "lat", 1)
         up_shards = [(up_weight, 0, LANES), (x0, 0, LANES), (uz1, 0, LANES), (ux1, 0, LANES), (z3, 0, LANES), (x3, 0, LANES), (uz2, 0, LANES), (ux2, 0, LANES)]
-        hid_opposite, hid_across, hid_beside, hid_own = up([opposite, across, beside, normed], up_shards, line(up_bias))
+        sums = begin([after(opposite, dz1), across, beside, normed], up_shards[:-1], line(up_bias))
+        hid_opposite, hid_across, hid_beside, hid_own = up([opposite, across, beside, normed], sums, up_shards[-1:])
         down_a = [(down_weight, 0, LANES), (x0, LANES, LANES), (dz1, 0, 2 * LANES), (z3, LANES, LANES), (x3, LANES, LANES)]
         far_opp_a, = down([hid_opposite], down_a)
         far_acr_a, = down([hid_across], down_a)
@@ -359,9 +377,10 @@
         arrived_b = swap(far_b, "lat", 2)
         near_bes_b, near_own_b = down([hid_beside, hid_own], down_b)
         near_in_b = swap(near_bes_b, "lat", 1)
-        sums = [(near_own_a, near_in_a, arrived_a), (near_own_b, near_in_b, arrived_b)]
+        groups = [(near_own_a, near_in_a, arrived_a), (near_own_b, near_in_b, arrived_b)]
     else:
-        up_shards = [(lax.all_gather(up_weight, "lon", axis=0, tiled=True), 0, chans)]
+        up_whole = lax.all_gather(up_weight, "lon", axis=0, tiled=True)
+        up_shards = [(up_whole, 0, chans - LANES), (up_whole, chans - LANES, LANES)]
         down_a = [(lax.all_gather(down_weight, "lon", axis=0, tiled=True), 0, chans)]
         first, last = edges(features)
         left = lax.ppermute(last, "lon", [(i, (i + 1) % lons) for i in range(lons)])
@@ -373,7 +392,8 @@
         across = swap(normed, "lat", 2)
         beside = swap(normed, "lat", 1)
         opposite = swap(across, "lat", 1)
-        hid_opposite, hid_across, hid_beside, hid_own = up([opposite, across, beside, normed], up_shards, line(up_bias))
+        sums = begin([opposite, across, beside, normed], up_shards[:-1], line(up_bias))
+        hid_opposite, hid_across, hid_beside, hid_own = up([opposite, across, beside, normed], sums, up_shards[-1:])
         far_opp_a, = down([hid_opposite], down_a)
         far_acr_a, = down([hid_across], down_a)
         far_in_a = swap(far_opp_a, "lat", 1)
@@ -381,10 +401,8 @@
         arrived_a = swap(far_a, "lat", 2)
         near_bes_a, near_own_a = down([hid_beside, hid_own], down_a)
         near_in_a = swap(near_bes_a, "lat", 1)
-        sums = [(near_own_a, near_in_a, arrived_a)]
-    updated = finish(
-        order, features.reshape(rows * cols, chans), sums, line(down_bias), line(layer_scale)
-    )
+        groups = [(near_own_a, near_in_a, arrived_a)]
+    updated = finish(order, features.reshape(rows * cols, chans), groups, line(down_bias), line(layer_scale))
     return updated.reshape(rows, cols, chans)
 
 

time: 82.9 us -> 77.8 us (0.938)
  waiting for transfers between devices: 41.6 us -> 30.4 us
  starting transfers between devices: 21.9 us -> 26.1 us
  local copies, waits for them, and re-layouts: 1.83 us -> 3.43 us
  Pallas kernels: 16.2 us -> 17.2 us
    ppermute x13, waiting for transfers between devices: 29.5 us -> 13.6 us  [swap(): return lax.ppermute(value, axis, [(i, i ^ bit) for i in range(count)])]
    ppermute x5, waiting for transfers between devices: 3.61 us -> 11.4 us  [shift(): lax.ppermute(value, axis, [(i, (i + step * inner) % count) for i in range...]
    pallas_call x2 -> x3, Pallas kernels: 2.37 us -> 6.09 us  [the longest x1 3.31 us: begin(): pl.pallas_call(functools.partial(begin_kernel, len(pixels), spans), out_s...]
    ppermute x1, waiting for transfers between devices: 3.56 us -> 0.01 us  [local(): high = lax.ppermute(top, 'lat', [(b, a) for a, b in forward])]
    ppermute x1, starting transfers between devices: 2.99 us -> 0.01 us  [local(): left = lax.ppermute(last, 'lon', [(i, (i + 1) % lons) for i in range(lons)])]
    ppermute x1, starting transfers between devices: 3.1 us -> 6.03 us  [local(): lax.ppermute(first, 'lon', [((i + 1) % lons, i) for i in range(lons)])]
    pallas_call x1, Pallas kernels: 3.78 us -> 1.11 us  [up(): pl.pallas_call(functools.partial(up_kernel, len(pixels), spans), out_shap...]
    ppermute x1, starting transfers between devices: 1.43 us -> 3.04 us  [local(): low = lax.ppermute(bottom, 'lat', forward)]
  transfers between devices with their start and end apart: 22 -> 22, of which waited for: 9 -> 9; matrix products, arithmetic and copies ran while one was open for 1% -> 2% of each run, Pallas kernels for 17% -> 20%
where the time goes in v3:
time: 77.8 us; the launch traced here: 77.5 us
  waiting for transfers between devices  30.4 us (39%)
  starting transfers between devices  26.1 us (34%)
  Pallas kernels  17.2 us (22%)
  local copies, waits for them, and re-layouts  3.43 us (4%)
    ppermute x13, waiting for transfers between devices, swap(): return lax.ppermute(value, axis, [(i, i ^ bit) for i in range(count)])  13.6 us
    ppermute x5, waiting for transfers between devices, shift(): lax.ppermute(value, axis, [(i, (i + step * inner) % count) for i in range...  11.4 us
    ppermute x13, starting transfers between devices, swap(): return lax.ppermute(value, axis, [(i, i ^ bit) for i in range(count)])  10.6 us
    ppermute x1, starting transfers between devices, local(): lax.ppermute(first, 'lon', [((i + 1) % lons, i) for i in range(lons)])  6.03 us
    ppermute x1, waiting for transfers between devices, local(): left = lax.ppermute(last, 'lon', [(i, (i + 1) % lons) for i in range(lons)])  5.4 us
    pallas_call x1, Pallas kernels, conv_norm(): pl.pallas_call(conv_kernel, out_shape=jax.ShapeDtypeStruct((rows * cols,...  4.98 us
    ppermute x5, starting transfers between devices, shift(): lax.ppermute(value, axis, [(i, (i + step * inner) % count) for i in range...  4.95 us
    pallas_call x6, Pallas kernels, down(): pl.pallas_call(functools.partial(down_kernel, len(hidden), spans), out_sh...  4.33 us
  transfers between devices with their start and end apart: 22, of which 9 were waited for; matrix products, arithmetic and copies ran while one was open for 2% of the time, Pallas kernels for 20%

profile of v3, /device:TPU:0, one launch (start us, length us, event | category | flops | bytes accessed | tf_op | source)
XLA Modules:
  0.0 77.5 jit_solution(10233260061216788135)
XLA Ops:
  0.0 1.0 %copy-done = bf16[32,8,1024]{2,1,0:T(8,128)(2,1)S(1)} copy-done((bf16[32,8,1024]{2,1,0:T(8,128)(2,1)S(1)}, bf16[32,8,1024]{2,1,0:T(8,128)(2,1)}, u32[]{:S(2)}) %copy-start) | copy-done | bytes 524312
  1.0 0.4 shard_map.100
  1.5 6.0 %collective-permute-start.1 = (bf16[3,32,1024]{2,1,0:T(8,128)(2,1)S(1)}, bf16[3,32,1024]{2,1,0:T(8,128)(2,1)S(1)}, u32[]{:S(2)}, u32[]{:S(2)}) collective-permute-start(bf16[3,32,1024]{2,1,0:T(8,128)(2,1)S(1)} %get-tuple-element.33), channel_id=1, source_target_pairs={{1,0},{2,1},{3,2},{4,3},{5,4},{6,5},{7,6},{0,7},{9,8},{10,9},{11,1... | collective-permute-start | bytes 589832 | tf_op jit(solution)/shard_map/ppermute | solution.py:344
  7.5 0.1 collective-permute-start.6
  7.6 0.7 constant_dynamic-update-slice_fusion.1
  8.3 0.2 copy-done.2
  8.4 0.7 constant_dynamic-update-slice_fusion
  9.2 3.7 %collective-permute-start.10 = (bf16[256,1024]{1,0:T(8,128)(2,1)}, bf16[256,1024]{1,0:T(8,128)(2,1)S(1)}, u32[]{:S(2)}, u32[]{:S(2)}) collective-permute-start(bf16[256,1024]{1,0:T(8,128)(2,1)} %constant_dynamic-update-slice_fusion), channel_id=1, source_target_pairs={{0,6},{1,7},{2,0},{3,1},{4,2},{5,3},{6,4},{7,5},{8,14},{9,15},{10,... | collective-permute-start | bytes 1572872 | tf_op jit(solution)/shard_map/ppermute | solution.py:20
  12.8 5.4 %collective-permute-done.left_ref = bf16[3,32,1024]{2,1,0:T(8,128)(2,1)S(1)} collective-permute-done((bf16[3,32,1024]{2,1,0:T(8,128)(2,1)S(1)}, bf16[3,32,1024]{2,1,0:T(8,128)(2,1)S(1)}, u32[]{:S(2)}, u32[]{:S(2)}) %collective-permute-start) | collective-permute-done | bytes 196640 | tf_op jit(solution)/shard_map/ppermute | solution.py:343
  18.2 0.2 shard_map.101
  18.4 0.0 copy-start.10
  18.4 1.4 %collective-permute-start.3 = (bf16[48,1024]{1,0:T(8,128)(2,1)S(1)}, bf16[48,1024]{1,0:T(8,128)(2,1)S(1)}, u32[]{:S(2)}, u32[]{:S(2)}) collective-permute-start(bf16[48,1024]{1,0:T(8,128)(2,1)S(1)} %get-tuple-element.35), channel_id=1, source_target_pairs={{8,0},{16,8},{24,16},{9,1},{17,9},{25,17},{10,2},{18,10},{26,18},{... | collective-permute-start | bytes 294920 | tf_op jit(solution)/shard_map/ppermute | solution.py:347
  19.9 3.0 %collective-permute-start.2 = (bf16[48,1024]{1,0:T(8,128)(2,1)S(1)}, bf16[48,1024]{1,0:T(8,128)(2,1)S(1)}, u32[]{:S(2)}, u32[]{:S(2)}) collective-permute-start(bf16[48,1024]{1,0:T(8,128)(2,1)S(1)} %get-tuple-element.34), channel_id=1, source_target_pairs={{0,8},{8,16},{16,24},{1,9},{9,17},{17,25},{2,10},{10,18},{18,26},{... | collective-permute-start | bytes 294920 | tf_op jit(solution)/shard_map/ppermute | solution.py:346
  22.9 2.1 %collective-permute-start.7 = (bf16[128,1024]{1,0:T(8,128)(2,1)S(1)}, bf16[128,1024]{1,0:T(8,128)(2,1)S(1)}, u32[]{:S(2)}, u32[]{:S(2)}) collective-permute-start(bf16[128,1024]{1,0:T(8,128)(2,1)S(1)} %collective-permute-done.6.refs_6_), channel_id=1, source_target_pairs={{0,1},{1,0},{2,3},{3,2},{4,5},{5,4},{6,7},{7,6},{8,9},{9,8},{10,11... | collective-permute-start | bytes 786440 | tf_op jit(solution)/shard_map/ppermute | solution.py:25
  25.1 0.1 stack.35.order_ref
  25.2 0.6 copy-done.8
  25.8 0.0 copy-done.6
  25.8 0.0 copy-done.7
  25.8 5.0 %shard_map.102.refs_3_ = bf16[256,1024]{1,0:T(8,128)(2,1)S(1)} custom-call(s32[8]{0:T(128)S(1)} %stack.35.order_ref, bf16[32,8,1024]{2,1,0:T(8,128)(2,1)S(1)} %copy-done.1, bf16[48,1024]{1,0:T(8,128)(2,1)S(1)} %collective-permute-done.2.low_ref, bf16[48,1024]{1,0:T(8,128)(2,1)S(1)} %collective-permute-done.3.high_ref, ...), custom_call_target="tpu_custom_call" | custom-call | flops 26214400 | bytes 2097152 | tf_op jit(solution)/shard_map/pallas_call | solution.py:137
  30.8 3.0 %collective-permute-start.4 = (bf16[256,1024]{1,0:T(8,128)(2,1)S(1)}, bf16[256,1024]{1,0:T(8,128)(2,1)S(1)}, u32[]{:S(2)}, u32[]{:S(2)}) collective-permute-start(bf16[256,1024]{1,0:T(8,128)(2,1)S(1)} %shard_map.102.refs_3_), channel_id=1, source_target_pairs={{0,16},{8,24},{16,0},{24,8},{1,17},{9,25},{17,1},{25,9},{2,18},{10... | collective-permute-start | bytes 1572872 | tf_op jit(solution)/shard_map/ppermute | solution.py:25
  33.8 1.2 %collective-permute-done.7.refs_7_ = bf16[128,1024]{1,0:T(8,128)(2,1)S(1)} collective-permute-done((bf16[128,1024]{1,0:T(8,128)(2,1)S(1)}, bf16[128,1024]{1,0:T(8,128)(2,1)S(1)}, u32[]{:S(2)}, u32[]{:S(2)}) %collective-permute-start.7) | collective-permute-done | bytes 262176 | tf_op jit(solution)/shard_map/ppermute | solution.py:25
  35.0 0.9 %collective-permute-start.11 = (bf16[256,1024]{1,0:T(8,128)(2,1)S(1)}, bf16[256,1024]{1,0:T(8,128)(2,1)S(1)}, u32[]{:S(2)}, u32[]{:S(2)}) collective-permute-start(bf16[256,1024]{1,0:T(8,128)(2,1)S(1)} %collective-permute-done.10.refs_8_.refs_5_.refs_4_), channel_id=1, source_target_pairs={{0,1},{1,0},{2,3},{3,2},{4,5},{5,4},{6,7},{7,6},{8,9},{9,8},{10,11... | collective-permute-start | bytes 1572872 | tf_op jit(solution)/shard_map/ppermute | solution.py:25
  35.9 1.3 %collective-permute-done.8.refs_10_ = bf16[128,1024]{1,0:T(8,128)(2,1)} collective-permute-done((bf16[128,1024]{1,0:T(8,128)(2,1)S(1)}, bf16[128,1024]{1,0:T(8,128)(2,1)}, u32[]{:S(2)}, u32[]{:S(2)}) %collective-permute-start.8) | collective-permute-done | bytes 262176 | tf_op jit(solution)/shard_map/ppermute | solution.py:20
  37.2 1.2 %collective-permute-start.13 = (bf16[256,1024]{1,0:T(8,128)(2,1)S(1)}, bf16[256,1024]{1,0:T(8,128)(2,1)S(1)}, u32[]{:S(2)}, u32[]{:S(2)}) collective-permute-start(bf16[256,1024]{1,0:T(8,128)(2,1)S(1)} %pad_maximum_fusion), channel_id=1, source_target_pairs={{0,2},{1,3},{2,4},{3,5},{4,6},{5,7},{6,0},{7,1},{8,10},{9,11},{10,... | collective-permute-start | bytes 1572872 | tf_op jit(solution)/shard_map/ppermute | solution.py:20
  38.4 7.7 %collective-permute-done.4.refs_1_ = bf16[256,1024]{1,0:T(8,128)(2,1)S(1)} collective-permute-done((bf16[256,1024]{1,0:T(8,128)(2,1)S(1)}, bf16[256,1024]{1,0:T(8,128)(2,1)S(1)}, u32[]{:S(2)}, u32[]{:S(2)}) %collective-permute-start.4) | collective-permute-done | bytes 524320 | tf_op jit(solution)/shard_map/ppermute | solution.py:25
  46.1 1.1 %collective-permute-done.11.refs_9_.refs_6_.refs_5_ = bf16[256,1024]{1,0:T(8,128)(2,1)S(1)} collective-permute-done((bf16[256,1024]{1,0:T(8,128)(2,1)S(1)}, bf16[256,1024]{1,0:T(8,128)(2,1)S(1)}, u32[]{:S(2)}, u32[]{:S(2)}) %collective-permute-start.11) | collective-permute-done | bytes 524320 | tf_op jit(solution)/shard_map/ppermute | solution.py:25
  47.2 1.7 %collective-permute-start.14 = (bf16[128,1024]{1,0:T(8,128)(2,1)}, bf16[128,1024]{1,0:T(8,128)(2,1)S(1)}, u32[]{:S(2)}, u32[]{:S(2)}) collective-permute-start(bf16[128,1024]{1,0:T(8,128)(2,1)} %collective-permute-done.8.refs_10_), channel_id=1, source_target_pairs={{0,1},{1,0},{2,3},{3,2},{4,5},{5,4},{6,7},{7,6},{8,9},{9,8},{10,11... | collective-permute-start | bytes 786440 | tf_op jit(solution)/shard_map/ppermute | solution.py:25
  48.9 4.5 %collective-permute-done.13.refs_4_.refs_3_ = bf16[256,1024]{1,0:T(8,128)(2,1)S(1)} collective-permute-done((bf16[256,1024]{1,0:T(8,128)(2,1)S(1)}, bf16[256,1024]{1,0:T(8,128)(2,1)S(1)}, u32[]{:S(2)}, u32[]{:S(2)}) %collective-permute-start.13) | collective-permute-done | bytes 524320 | tf_op jit(solution)/shard_map/ppermute | solution.py:20
  53.4 3.3 %shard_map.103 = (f32[256,1024]{1,0:T(8,128)S(1)}, f32[256,1024]{1,0:T(8,128)S(1)}, f32[256,1024]{1,0:T(8,128)S(1)}, f32[256,1024]{1,0:T(8,128)S(1)}) custom-call(bf16[256,1024]{1,0:T(8,128)(2,1)S(1)} %collective-permute-done.12.refs_0_, bf16[256,1024]{1,0:T(8,128)(2,1)S(1)} %collective-permute-done.4.refs_1_, ...), custom_call_target="tpu_custom_call" | custom-call | flops 1879048192 | bytes 1048576 | tf_op jit(solution)/shard_map/pallas_call | solution.py:177
  56.7 1.1 %shard_map.104 = (bf16[256,1024]{1,0:T(8,128)(2,1)S(1)}, bf16[256,1024]{1,0:T(8,128)(2,1)S(1)}, bf16[256,1024]{1,0:T(8,128)(2,1)S(1)}, bf16[256,1024]{1,0:T(8,128)(2,1)S(1)}) custom-call(bf16[256,1024]{1,0:T(8,128)(2,1)S(1)} %collective-permute-done.12.refs_0_, bf16[256,1024]{1,0:T(8,128)(2,1)S(1)} %collective-permute-done.4.refs_1_, ...), custom_call_target="tpu_custom_call" | custom-call | flops 268435456 | bytes 1048576 | tf_op jit(solution)/shard_map/pallas_call | solution.py:208
  57.9 0.8 %shard_map.111 = bf16[256,768]{1,0:T(8,128)(2,1)S(1)} custom-call(bf16[256,1024]{1,0:T(8,128)(2,1)S(1)} %get-tuple-element.56.refs_0_, bf16[128,1024]{1,0:T(8,128)(2,1)S(1)} %copy-done.2, bf16[256,1024]{1,0:T(8,128)(2,1)S(1)} %collective-permute-done.5.refs_5_.refs_3_.refs_2_, bf16[256,1024]{1,0:T(8,128)(2,1)S(1)} %collective-permute-done.13.refs_4_.refs_3_, ...), custom_call_target="tpu_custom_call" | custom-call | flops 402653184 | bytes 6291456 | tf_op jit(solution)/shard_map/pallas_call | solution.py:236
  58.7 0.1 collective-permute-start.20
  58.8 1.5 %shard_map.109 = (bf16[256,768]{1,0:T(8,128)(2,1)S(1)}, bf16[256,768]{1,0:T(8,128)(2,1)S(1)}) custom-call(bf16[256,1024]{1,0:T(8,128)(2,1)S(1)} %get-tuple-element.51.refs_0_, bf16[256,1024]{1,0:T(8,128)(2,1)S(1)} %get-tuple-element.52.refs_1_, bf16[128,1024]{1,0:T(8,128)(2,1)S(1)} %copy-done.2, ...), custom_call_target="tpu_custom_call" | custom-call | flops 805306368 | bytes 6291456 | tf_op jit(solution)/shard_map/pallas_call | solution.py:236
  60.3 0.6 collective-permute-start.19
  60.9 0.8 %shard_map.110.one_ref = bf16[256,768]{1,0:T(8,128)(2,1)S(1)} custom-call(bf16[256,1024]{1,0:T(8,128)(2,1)S(1)} %get-tuple-element.55.refs_0_, bf16[128,1024]{1,0:T(8,128)(2,1)S(1)} %copy-done.2, bf16[256,1024]{1,0:T(8,128)(2,1)S(1)} %collective-permute-done.5.refs_5_.refs_3_.refs_2_, bf16[256,1024]{1,0:T(8,128)(2,1)S(1)} %collective-permute-done.13.refs_4_.refs_3_, ...), custom_call_target="tpu_custom_call" | custom-call | flops 402653184 | bytes 6291456 | tf_op jit(solution)/shard_map/pallas_call | solution.py:236
  61.7 0.1 shard_map.112
  61.8 1.3 %collective-permute-start.21 = (bf16[256,768]{1,0:T(8,128)(2,1)S(1)}, bf16[256,768]{1,0:T(8,128)(2,1)S(1)}, u32[]{:S(2)}, u32[]{:S(2)}) collective-permute-start(bf16[256,768]{1,0:T(8,128)(2,1)S(1)} %shard_map.112), channel_id=1, source_target_pairs={{0,16},{8,24},{16,0},{24,8},{1,17},{9,25},{17,1},{25,9},{2,18},{10... | collective-permute-start | bytes 1179656 | tf_op jit(solution)/shard_map/ppermute | solution.py:25
  63.1 5.6 %collective-permute-done.15.refs_2_.refs_1_ = bf16[256,1024]{1,0:T(8,128)(2,1)S(1)} collective-permute-done((bf16[256,1024]{1,0:T(8,128)(2,1)S(1)}, bf16[256,1024]{1,0:T(8,128)(2,1)S(1)}, u32[]{:S(2)}, u32[]{:S(2)}) %collective-permute-start.15) | collective-permute-done | bytes 524320 | tf_op jit(solution)/shard_map/ppermute | solution.py:20
  68.8 0.3 shard_map.107
  69.1 0.1 collective-permute-start.17
  69.2 0.5 shard_map.105
  69.7 0.6 collective-permute-start.16
  70.2 0.3 shard_map.106.one_ref
  70.6 0.3 collective-permute-start.18
  71.0 2.0 %collective-permute-done.21.far_ref = bf16[256,768]{1,0:T(8,128)(2,1)S(1)} collective-permute-done((bf16[256,768]{1,0:T(8,128)(2,1)S(1)}, bf16[256,768]{1,0:T(8,128)(2,1)S(1)}, u32[]{:S(2)}, u32[]{:S(2)}) %collective-permute-start.21) | collective-permute-done | bytes 393248 | tf_op jit(solution)/shard_map/ppermute | solution.py:25
  72.9 1.5 %shard_map.113.refs_0_ = bf16[256,1024]{1,0:T(8,128)(2,1)} custom-call(s32[8]{0:T(128)S(1)} %stack.35.order_ref, bf16[256,1024]{1,0:T(8,128)(2,1)S(1)} %bitcast.16, bf16[256,768]{1,0:T(8,128)(2,1)S(1)} %get-tuple-element.57.one_ref, bf16[256,768]{1,0:T(8,128)(2,1)S(1)} %collective-permute-done.19.two_ref, ...), custom_call_target="tpu_custom_call" | custom-call | tf_op jit(solution)/shard_map/pallas_call | solution.py:288
  74.4 1.7 %collective-permute-done.18.far_ref = bf16[256,256]{1,0:T(8,128)(2,1)S(1)} collective-permute-done((bf16[256,256]{1,0:T(8,128)(2,1)S(1)}, bf16[256,256]{1,0:T(8,128)(2,1)S(1)}, u32[]{:S(2)}, u32[]{:S(2)}) %collective-permute-start.18) | collective-permute-done | bytes 131104 | tf_op jit(solution)/shard_map/ppermute | solution.py:25
  76.2 1.3 %shard_map.114 = bf16[256,1024]{1,0:T(8,128)(2,1)} custom-call(s32[8]{0:T(128)S(1)} %stack.35.order_ref, bf16[256,1024]{1,0:T(8,128)(2,1)S(1)} %bitcast.17, bf16[256,256]{1,0:T(8,128)(2,1)S(1)} %get-tuple-element.53.one_ref, bf16[256,256]{1,0:T(8,128)(2,1)S(1)} %collective-permute-done.16.two_ref, ...), custom_call_target="tpu_custom_call", output_to_operand_aliasing={{}: (7, {})} | custom-call | tf_op jit(solution)/shard_map/pallas_call | solution.py:288
  (39 shorter events, 0.2 us)
Async XLA Ops:
  0.0 1.0 %copy-start = (bf16[32,8,1024]{2,1,0:T(8,128)(2,1)S(1)}, bf16[32,8,1024]{2,1,0:T(8,128)(2,1)}, u32[]{:S(2)}) copy-start(bf16[32,8,1024]{2,1,0:T(8,128)(2,1)} %mid_ref.5) | copy-start | bytes 1572868
  1.0 6.4 %copy-start.3 = (bf16[128,1024]{1,0:T(8,128)(2,1)S(1)}, bf16[128,1024]{1,0:T(8,128)(2,1)}, u32[]{:S(2)}) copy-start(bf16[128,1024]{1,0:T(8,128)(2,1)} %refs_4_.1) | copy-start | bytes 786436
  1.5 16.8 %collective-permute-start.1 = (bf16[3,32,1024]{2,1,0:T(8,128)(2,1)S(1)}, bf16[3,32,1024]{2,1,0:T(8,128)(2,1)S(1)}, u32[]{:S(2)}, u32[]{:S(2)}) collective-permute-start(bf16[3,32,1024]{2,1,0:T(8,128)(2,1)S(1)} %get-tuple-element.33), channel_id=1, source_target_pairs={{1,0},{2,1},{3,2},{4,3},{5,4},{6,5},{7,6},{0,7},{9,8},{10,9},{11,1... | collective-permute-start | bytes 589832 | tf_op jit(solution)/shard_map/ppermute | solution.py:344
  7.5 0.9 %copy-start.2 = (bf16[128,1024]{1,0:T(8,128)(2,1)S(1)}, bf16[128,1024]{1,0:T(8,128)(2,1)}, u32[]{:S(2)}) copy-start(bf16[128,1024]{1,0:T(8,128)(2,1)} %refs_1_.3) | copy-start | bytes 786436
  7.5 10.7 %collective-permute-start = (bf16[3,32,1024]{2,1,0:T(8,128)(2,1)S(1)}, bf16[3,32,1024]{2,1,0:T(8,128)(2,1)S(1)}, u32[]{:S(2)}, u32[]{:S(2)}) collective-permute-start(bf16[3,32,1024]{2,1,0:T(8,128)(2,1)S(1)} %get-tuple-element.32), channel_id=1, source_target_pairs={{0,1},{1,2},{2,3},{3,4},{4,5},{5,6},{6,7},{7,0},{8,9},{9,10},{10,1... | collective-permute-start | bytes 589832 | tf_op jit(solution)/shard_map/ppermute | solution.py:343
  7.5 15.4 %collective-permute-start.6 = (bf16[128,1024]{1,0:T(8,128)(2,1)S(1)}, bf16[128,1024]{1,0:T(8,128)(2,1)S(1)}, u32[]{:S(2)}, u32[]{:S(2)}) collective-permute-start(bf16[128,1024]{1,0:T(8,128)(2,1)S(1)} %copy-done.3), channel_id=1, source_target_pairs={{0,2},{1,3},{2,4},{3,5},{4,6},{5,7},{6,0},{7,1},{8,10},{9,11},{10,... | collective-permute-start | bytes 786440 | tf_op jit(solution)/shard_map/ppermute | solution.py:20
  9.2 16.1 %copy-start.1 = (bf16[32,8,1024]{2,1,0:T(8,128)(2,1)S(1)}, bf16[32,8,1024]{2,1,0:T(8,128)(2,1)}, u32[]{:S(2)}) copy-start(bf16[32,8,1024]{2,1,0:T(8,128)(2,1)} %mid_ref.5) | copy-start | bytes 1572868
  9.2 24.6 %collective-permute-start.10 = (bf16[256,1024]{1,0:T(8,128)(2,1)}, bf16[256,1024]{1,0:T(8,128)(2,1)S(1)}, u32[]{:S(2)}, u32[]{:S(2)}) collective-permute-start(bf16[256,1024]{1,0:T(8,128)(2,1)} %constant_dynamic-update-slice_fusion), channel_id=1, source_target_pairs={{0,6},{1,7},{2,0},{3,1},{4,2},{5,3},{6,4},{7,5},{8,14},{9,15},{10,... | collective-permute-start | bytes 1572872 | tf_op jit(solution)/shard_map/ppermute | solution.py:20
  18.2 18.9 %collective-permute-start.5 = (bf16[256,1024]{1,0:T(8,128)(2,1)}, bf16[256,1024]{1,0:T(8,128)(2,1)S(1)}, u32[]{:S(2)}, u32[]{:S(2)}) collective-permute-start(bf16[256,1024]{1,0:T(8,128)(2,1)} %constant_dynamic-update-slice_fusion), channel_id=1, source_target_pairs={{0,1},{1,0},{2,3},{3,2},{4,5},{5,4},{6,7},{7,6},{8,9},{9,8},{10,11... | collective-permute-start | bytes 1572872 | tf_op jit(solution)/shard_map/ppermute | solution.py:25
  18.4 6.6 %copy-start.10 = (bf16[7,7,1024]{2,1,0:T(8,128)(2,1)S(1)}, bf16[7,7,1024]{2,1,0:T(8,128)(2,1)}, u32[]{:S(2)}) copy-start(bf16[7,7,1024]{2,1,0:T(8,128)(2,1)} %param.11) | copy-start | bytes 301060
  18.4 4.5 %collective-permute-start.3 = (bf16[48,1024]{1,0:T(8,128)(2,1)S(1)}, bf16[48,1024]{1,0:T(8,128)(2,1)S(1)}, u32[]{:S(2)}, u32[]{:S(2)}) collective-permute-start(bf16[48,1024]{1,0:T(8,128)(2,1)S(1)} %get-tuple-element.35), channel_id=1, source_target_pairs={{8,0},{16,8},{24,16},{9,1},{17,9},{25,17},{10,2},{18,10},{26,18},{... | collective-permute-start | bytes 294920 | tf_op jit(solution)/shard_map/ppermute | solution.py:347
  19.9 5.2 %collective-permute-start.2 = (bf16[48,1024]{1,0:T(8,128)(2,1)S(1)}, bf16[48,1024]{1,0:T(8,128)(2,1)S(1)}, u32[]{:S(2)}, u32[]{:S(2)}) collective-permute-start(bf16[48,1024]{1,0:T(8,128)(2,1)S(1)} %get-tuple-element.34), channel_id=1, source_target_pairs={{0,8},{8,16},{16,24},{1,9},{9,17},{17,25},{2,10},{10,18},{18,26},{... | collective-permute-start | bytes 294920 | tf_op jit(solution)/shard_map/ppermute | solution.py:346
  22.9 12.0 %collective-permute-start.7 = (bf16[128,1024]{1,0:T(8,128)(2,1)S(1)}, bf16[128,1024]{1,0:T(8,128)(2,1)S(1)}, u32[]{:S(2)}, u32[]{:S(2)}) collective-permute-start(bf16[128,1024]{1,0:T(8,128)(2,1)S(1)} %collective-permute-done.6.refs_6_), channel_id=1, source_target_pairs={{0,1},{1,0},{2,3},{3,2},{4,5},{5,4},{6,7},{7,6},{8,9},{9,8},{10,11... | collective-permute-start | bytes 786440 | tf_op jit(solution)/shard_map/ppermute | solution.py:25
  25.0 12.1 %collective-permute-start.8 = (bf16[128,1024]{1,0:T(8,128)(2,1)S(1)}, bf16[128,1024]{1,0:T(8,128)(2,1)}, u32[]{:S(2)}, u32[]{:S(2)}) collective-permute-start(bf16[128,1024]{1,0:T(8,128)(2,1)S(1)} %collective-permute-done.6.refs_6_), channel_id=1, source_target_pairs={{0,2},{1,3},{2,4},{3,5},{4,6},{5,7},{6,0},{7,1},{8,10},{9,11},{10,... | collective-permute-start | bytes 786440 | tf_op jit(solution)/shard_map/ppermute | solution.py:20
  25.1 0.7 copy-start.8
  25.1 0.7 copy-start.6
  25.1 0.7 copy-start.7
  30.8 15.3 %collective-permute-start.4 = (bf16[256,1024]{1,0:T(8,128)(2,1)S(1)}, bf16[256,1024]{1,0:T(8,128)(2,1)S(1)}, u32[]{:S(2)}, u32[]{:S(2)}) collective-permute-start(bf16[256,1024]{1,0:T(8,128)(2,1)S(1)} %shard_map.102.refs_3_), channel_id=1, source_target_pairs={{0,16},{8,24},{16,0},{24,8},{1,17},{9,25},{17,1},{25,9},{2,18},{10... | collective-permute-start | bytes 1572872 | tf_op jit(solution)/shard_map/ppermute | solution.py:25
  35.0 12.2 %collective-permute-start.11 = (bf16[256,1024]{1,0:T(8,128)(2,1)S(1)}, bf16[256,1024]{1,0:T(8,128)(2,1)S(1)}, u32[]{:S(2)}, u32[]{:S(2)}) collective-permute-start(bf16[256,1024]{1,0:T(8,128)(2,1)S(1)} %collective-permute-done.10.refs_8_.refs_5_.refs_4_), channel_id=1, source_target_pairs={{0,1},{1,0},{2,3},{3,2},{4,5},{5,4},{6,7},{7,6},{8,9},{9,8},{10,11... | collective-permute-start | bytes 1572872 | tf_op jit(solution)/shard_map/ppermute | solution.py:25
  37.1 10.1 %collective-permute-start.9 = (bf16[256,1024]{1,0:T(8,128)(2,1)S(1)}, bf16[256,1024]{1,0:T(8,128)(2,1)S(1)}, u32[]{:S(2)}, u32[]{:S(2)}) collective-permute-start(bf16[256,1024]{1,0:T(8,128)(2,1)S(1)} %shard_map.102.refs_3_), channel_id=1, source_target_pairs={{0,8},{8,0},{16,24},{24,16},{1,9},{9,1},{17,25},{25,17},{2,10},{10... | collective-permute-start | bytes 1572872 | tf_op jit(solution)/shard_map/ppermute | solution.py:25
  37.2 16.3 %copy-start.9 = (f32[1024]{0:T(1024)S(1)}, f32[1024]{0:T(1024)}, u32[]{:S(2)}) copy-start(f32[1024]{0:T(1024)} %param.16) | copy-start | bytes 12292
  37.2 16.2 %collective-permute-start.13 = (bf16[256,1024]{1,0:T(8,128)(2,1)S(1)}, bf16[256,1024]{1,0:T(8,128)(2,1)S(1)}, u32[]{:S(2)}, u32[]{:S(2)}) collective-permute-start(bf16[256,1024]{1,0:T(8,128)(2,1)S(1)} %pad_maximum_fusion), channel_id=1, source_target_pairs={{0,2},{1,3},{2,4},{3,5},{4,6},{5,7},{6,0},{7,1},{8,10},{9,11},{10,... | collective-permute-start | bytes 1572872 | tf_op jit(solution)/shard_map/ppermute | solution.py:20
  47.2 6.2 %collective-permute-start.12 = (bf16[256,1024]{1,0:T(8,128)(2,1)S(1)}, bf16[256,1024]{1,0:T(8,128)(2,1)S(1)}, u32[]{:S(2)}, u32[]{:S(2)}) collective-permute-start(bf16[256,1024]{1,0:T(8,128)(2,1)S(1)} %collective-permute-done.4.refs_1_), channel_id=1, source_target_pairs={{0,8},{8,0},{16,24},{24,16},{1,9},{9,1},{17,25},{25,17},{2,10},{10... | collective-permute-start | bytes 1572872 | tf_op jit(solution)/shard_map/ppermute | solution.py:25
  47.2 9.5 %collective-permute-start.14 = (bf16[128,1024]{1,0:T(8,128)(2,1)}, bf16[128,1024]{1,0:T(8,128)(2,1)S(1)}, u32[]{:S(2)}, u32[]{:S(2)}) collective-permute-start(bf16[128,1024]{1,0:T(8,128)(2,1)} %collective-permute-done.8.refs_10_), channel_id=1, source_target_pairs={{0,1},{1,0},{2,3},{3,2},{4,5},{5,4},{6,7},{7,6},{8,9},{9,8},{10,11... | collective-permute-start | bytes 786440 | tf_op jit(solution)/shard_map/ppermute | solution.py:25
  53.4 15.4 %collective-permute-start.15 = (bf16[256,1024]{1,0:T(8,128)(2,1)S(1)}, bf16[256,1024]{1,0:T(8,128)(2,1)S(1)}, u32[]{:S(2)}, u32[]{:S(2)}) collective-permute-start(bf16[256,1024]{1,0:T(8,128)(2,1)S(1)} %collective-permute-done.13.refs_4_.refs_3_), channel_id=1, source_target_pairs={{0,2},{1,3},{2,4},{3,5},{4,6},{5,7},{6,0},{7,1},{8,10},{9,11},{10,... | collective-permute-start | bytes 1572872 | tf_op jit(solution)/shard_map/ppermute | solution.py:20
  58.7 3.0 %collective-permute-start.20 = (bf16[256,768]{1,0:T(8,128)(2,1)S(1)}, bf16[256,768]{1,0:T(8,128)(2,1)S(1)}, u32[]{:S(2)}, u32[]{:S(2)}) collective-permute-start(bf16[256,768]{1,0:T(8,128)(2,1)S(1)} %shard_map.111), channel_id=1, source_target_pairs={{0,8},{8,0},{16,24},{24,16},{1,9},{9,1},{17,25},{25,17},{2,10},{10... | collective-permute-start | bytes 1179656 | tf_op jit(solution)/shard_map/ppermute | solution.py:25
  60.3 10.7 %collective-permute-start.19 = (bf16[256,768]{1,0:T(8,128)(2,1)S(1)}, bf16[256,768]{1,0:T(8,128)(2,1)S(1)}, u32[]{:S(2)}, u32[]{:S(2)}) collective-permute-start(bf16[256,768]{1,0:T(8,128)(2,1)S(1)} %get-tuple-element.58), channel_id=1, source_target_pairs={{0,8},{8,0},{16,24},{24,16},{1,9},{9,1},{17,25},{25,17},{2,10},{10... | collective-permute-start | bytes 1179656 | tf_op jit(solution)/shard_map/ppermute | solution.py:25
  61.8 11.1 %collective-permute-start.21 = (bf16[256,768]{1,0:T(8,128)(2,1)S(1)}, bf16[256,768]{1,0:T(8,128)(2,1)S(1)}, u32[]{:S(2)}, u32[]{:S(2)}) collective-permute-start(bf16[256,768]{1,0:T(8,128)(2,1)S(1)} %shard_map.112), channel_id=1, source_target_pairs={{0,16},{8,24},{16,0},{24,8},{1,17},{9,25},{17,1},{25,9},{2,18},{10... | collective-permute-start | bytes 1179656 | tf_op jit(solution)/shard_map/ppermute | solution.py:25
  69.1 1.5 %collective-permute-start.17 = (bf16[256,256]{1,0:T(8,128)(2,1)S(1)}, bf16[256,256]{1,0:T(8,128)(2,1)S(1)}, u32[]{:S(2)}, u32[]{:S(2)}) collective-permute-start(bf16[256,256]{1,0:T(8,128)(2,1)S(1)} %shard_map.107), channel_id=1, source_target_pairs={{0,8},{8,0},{16,24},{24,16},{1,9},{9,1},{17,25},{25,17},{2,10},{10... | collective-permute-start | bytes 393224 | tf_op jit(solution)/shard_map/ppermute | solution.py:25
  69.7 4.8 %collective-permute-start.16 = (bf16[256,256]{1,0:T(8,128)(2,1)S(1)}, bf16[256,256]{1,0:T(8,128)(2,1)S(1)}, u32[]{:S(2)}, u32[]{:S(2)}) collective-permute-start(bf16[256,256]{1,0:T(8,128)(2,1)S(1)} %get-tuple-element.54), channel_id=1, source_target_pairs={{0,8},{8,0},{16,24},{24,16},{1,9},{9,1},{17,25},{25,17},{2,10},{10... | collective-permute-start | bytes 393224 | tf_op jit(solution)/shard_map/ppermute | solution.py:25
  70.6 2.4 %copy-start.5 = (f32[1024]{0:T(1024)S(1)}, f32[1024]{0:T(1024)}, u32[]{:S(2)}) copy-start(f32[1024]{0:T(1024)} %param.19) | copy-start | bytes 12292
  70.6 2.3 %copy-start.4 = (f32[1024]{0:T(1024)S(1)}, f32[1024]{0:T(1024)}, u32[]{:S(2)}) copy-start(f32[1024]{0:T(1024)} %param.18) | copy-start | bytes 12292
  70.6 5.5 %collective-permute-start.18 = (bf16[256,256]{1,0:T(8,128)(2,1)S(1)}, bf16[256,256]{1,0:T(8,128)(2,1)S(1)}, u32[]{:S(2)}, u32[]{:S(2)}) collective-permute-start(bf16[256,256]{1,0:T(8,128)(2,1)S(1)} %shard_map.108), channel_id=1, source_target_pairs={{0,16},{8,24},{16,0},{24,8},{1,17},{9,25},{17,1},{25,9},{2,18},{10... | collective-permute-start | bytes 393224 | tf_op jit(solution)/shard_map/ppermute | solution.py:25

commit v4 on v3

--- a/solution.py
+++ b/solution.py
@@ -345,18 +345,18 @@
         top, bottom = rims(features, left, right)
         low = lax.ppermute(bottom, "lat", forward)
         high = lax.ppermute(top, "lat", [(b, a) for a, b in forward])
-        uz1 = z_of(after(up_weight, first), 1)
+        uz1 = z_of(up_weight, 1)
         x0 = x_of(after(both, left))
         z3 = z_of(after(both, first), 3)
         uz2 = z_of(after(uz1, low), 1)
         ux1 = x_of(after(uz1, high))
-        x3 = x_of(after(z3, ux1))
         ux2 = x_of(after(uz2, x0))
         dz1 = z_of(jnp.concatenate([after(down_weight, uz2), x0[LANES:]], axis=0), 1)
         dz2 = z_of(dz1, 1)
-        normed = conv_norm(order, features, low, high, left, right, *conv_args)
+        normed = conv_norm(order, features, after(low, top), high, left, right, *conv_args)
+        x3 = x_of(after(z3, normed))
         across = swap(normed, "lat", 2)
-        beside = swap(after(normed, x0, ux1, uz2), "lat", 1)
+        beside = swap(after(normed, ux1, uz2, x0), "lat", 1)
         opposite = swap(after(across, beside, x3), "lat", 1)
         up_shards = [(up_weight, 0, LANES), (x0, 0, LANES), (uz1, 0, LANES), (ux1, 0, LANES), (z3, 0, LANES), (x3, 0, LANES), (uz2, 0, LANES), (ux2, 0, LANES)]
         sums = begin([after(opposite, dz1), across, beside, normed], up_shards[:-1], line(up_bias))
@@ -367,16 +367,18 @@
         far_in_a = swap(far_opp_a, "lat", 1)
         far_a = add(far_acr_a, far_in_a)
         arrived_a = swap(far_a, "lat", 2)
-        near_bes_a, near_own_a = down([hid_beside, hid_own], down_a)
+        near_bes_a, = down([hid_beside], down_a)
         near_in_a = swap(near_bes_a, "lat", 1)
+        near_own_a, = down([hid_own], down_a)
         down_b = [(dz2, 0, 2 * LANES)]
         far_opp_b, = down([hid_opposite], down_b)
         far_acr_b, = down([hid_across], down_b)
         far_in_b = swap(far_opp_b, "lat", 1)
-        far_b = add(far_acr_b, far_in_b)
-        arrived_b = swap(far_b, "lat", 2)
-        near_bes_b, near_own_b = down([hid_beside, hid_own], down_b)
+        far_b = add(after(far_acr_b, far_a), far_in_b)
+        arrived_b = swap(after(far_b, far_opp_a), "lat", 2)
+        near_bes_b, = down([hid_beside], down_b)
         near_in_b = swap(near_bes_b, "lat", 1)
+        near_own_b, = down([hid_own], down_b)
         groups = [(near_own_a, near_in_a, arrived_a), (near_own_b, near_in_b, arrived_b)]
     else:
         up_whole = lax.all_gather(up_weight, "lon", axis=0, tiled=True)
@@ -399,8 +401,9 @@
         far_in_a = swap(far_opp_a, "lat", 1)
         far_a = add(far_acr_a, far_in_a)
         arrived_a = swap(far_a, "lat", 2)
-        near_bes_a, near_own_a = down([hid_beside, hid_own], down_a)
+        near_bes_a, = down([hid_beside], down_a)
         near_in_a = swap(near_bes_a, "lat", 1)
+        near_own_a, = down([hid_own], down_a)
         groups = [(near_own_a, near_in_a, arrived_a)]
     updated = finish(order, features.reshape(rows * cols, chans), groups, line(down_bias), line(layer_scale))
     return updated.reshape(rows, cols, chans)

time: 77.8 us -> 77 us (0.990)
  waiting for transfers between devices: 30.4 us -> 27.9 us
  starting transfers between devices: 26.1 us -> 27 us
    ppermute x5, waiting for transfers between devices: 11.4 us -> 18 us  [shift(): lax.ppermute(value, axis, [(i, (i + step * inner) % count) for i in range...]
    ppermute x13, waiting for transfers between devices: 13.6 us -> 8.34 us  [swap(): return lax.ppermute(value, axis, [(i, i ^ bit) for i in range(count)])]
    ppermute x1, waiting for transfers between devices: 5.4 us -> 0.54 us  [local(): left = lax.ppermute(last, 'lon', [(i, (i + 1) % lons) for i in range(lons)])]
    ppermute x1, starting transfers between devices: 0.01 us -> 2.99 us  [local(): left = lax.ppermute(last, 'lon', [(i, (i + 1) % lons) for i in range(lons)])]
    ppermute x1, starting transfers between devices: 6.03 us -> 3.11 us  [local(): lax.ppermute(first, 'lon', [((i + 1) % lons, i) for i in range(lons)])]
    ppermute x13, starting transfers between devices: 10.6 us -> 13.2 us  [swap(): return lax.ppermute(value, axis, [(i, i ^ bit) for i in range(count)])]
    ppermute x1, starting transfers between devices: 3.04 us -> 1.43 us  [local(): low = lax.ppermute(bottom, 'lat', forward)]
    ppermute x1, waiting for transfers between devices: 0.01 us -> 0.93 us  [local(): high = lax.ppermute(top, 'lat', [(b, a) for a, b in forward])]
  transfers between devices with their start and end apart: 22 -> 22, of which waited for: 9 -> 10; matrix products, arithmetic and copies ran while one was open for 2% -> 2% of each run, Pallas kernels for 20% -> 21%
where the time goes in v4:
time: 77 us; the launch traced here: 76.7 us
  waiting for transfers between devices  27.9 us (36%)
  starting transfers between devices  27 us (35%)
  Pallas kernels  17.6 us (23%)
  local copies, waits for them, and re-layouts  3.92 us (5%)
    ppermute x5, waiting for transfers between devices, shift(): lax.ppermute(value, axis, [(i, (i + step * inner) % count) for i in range...  18 us
    ppermute x13, starting transfers between devices, swap(): return lax.ppermute(value, axis, [(i, i ^ bit) for i in range(count)])  13.2 us
    ppermute x13, waiting for transfers between devices, swap(): return lax.ppermute(value, axis, [(i, i ^ bit) for i in range(count)])  8.34 us
    pallas_call x1, Pallas kernels, conv_norm(): pl.pallas_call(conv_kernel, out_shape=jax.ShapeDtypeStruct((rows * cols,...  4.98 us
    ppermute x5, starting transfers between devices, shift(): lax.ppermute(value, axis, [(i, (i + step * inner) % count) for i in range...  4.97 us
    pallas_call x8, Pallas kernels, down(): pl.pallas_call(functools.partial(down_kernel, len(hidden), spans), out_sh...  4.67 us
    pallas_call x1, Pallas kernels, begin(): pl.pallas_call(functools.partial(begin_kernel, len(pixels), spans), out_s...  3.3 us
    ppermute x1, starting transfers between devices, local(): lax.ppermute(first, 'lon', [((i + 1) % lons, i) for i in range(lons)])  3.11 us
  transfers between devices with their start and end apart: 22, of which 10 were waited for; matrix products, arithmetic and copies ran while one was open for 2% of the time, Pallas kernels for 21%

profile of v4, /device:TPU:0, one launch (start us, length us, event | category | flops | bytes accessed | tf_op | source)
XLA Modules:
  0.0 76.7 jit_solution(12940774046471501666)
XLA Ops:
  0.0 1.0 %copy-done = bf16[32,8,1024]{2,1,0:T(8,128)(2,1)S(1)} copy-done((bf16[32,8,1024]{2,1,0:T(8,128)(2,1)S(1)}, bf16[32,8,1024]{2,1,0:T(8,128)(2,1)}, u32[]{:S(2)}) %copy-start) | copy-done | bytes 524312
  1.0 0.4 shard_map.100
  1.5 3.0 %collective-permute-start = (bf16[3,32,1024]{2,1,0:T(8,128)(2,1)S(1)}, bf16[3,32,1024]{2,1,0:T(8,128)(2,1)S(1)}, u32[]{:S(2)}, u32[]{:S(2)}) collective-permute-start(bf16[3,32,1024]{2,1,0:T(8,128)(2,1)S(1)} %get-tuple-element.30), channel_id=1, source_target_pairs={{0,1},{1,2},{2,3},{3,4},{4,5},{5,6},{6,7},{7,0},{8,9},{9,10},{10,1... | collective-permute-start | bytes 589832 | tf_op jit(solution)/shard_map/ppermute | solution.py:343
  4.4 3.1 %collective-permute-start.1 = (bf16[3,32,1024]{2,1,0:T(8,128)(2,1)S(1)}, bf16[3,32,1024]{2,1,0:T(8,128)(2,1)S(1)}, u32[]{:S(2)}, u32[]{:S(2)}) collective-permute-start(bf16[3,32,1024]{2,1,0:T(8,128)(2,1)S(1)} %get-tuple-element.31), channel_id=1, source_target_pairs={{1,0},{2,1},{3,2},{4,3},{5,4},{6,5},{7,6},{0,7},{9,8},{10,9},{11,1... | collective-permute-start | bytes 589832 | tf_op jit(solution)/shard_map/ppermute | solution.py:344
  7.6 0.7 constant_dynamic-update-slice_fusion.1
  8.3 0.7 constant_dynamic-update-slice_fusion
  9.0 3.8 %collective-permute-start.10 = (bf16[256,1024]{1,0:T(8,128)(2,1)}, bf16[256,1024]{1,0:T(8,128)(2,1)S(1)}, u32[]{:S(2)}, u32[]{:S(2)}) collective-permute-start(bf16[256,1024]{1,0:T(8,128)(2,1)} %constant_dynamic-update-slice_fusion), channel_id=1, source_target_pairs={{0,6},{1,7},{2,0},{3,1},{4,2},{5,3},{6,4},{7,5},{8,14},{9,15},{10,... | collective-permute-start | bytes 1572872 | tf_op jit(solution)/shard_map/ppermute | solution.py:20
  12.8 0.5 collective-permute-done.left_ref
  13.4 1.9 %collective-permute-start.8 = (bf16[256,1024]{1,0:T(8,128)(2,1)}, bf16[256,1024]{1,0:T(8,128)(2,1)S(1)}, u32[]{:S(2)}, u32[]{:S(2)}) collective-permute-start(bf16[256,1024]{1,0:T(8,128)(2,1)} %constant_dynamic-update-slice_fusion), channel_id=1, source_target_pairs={{0,1},{1,0},{2,3},{3,2},{4,5},{5,4},{6,7},{7,6},{8,9},{9,8},{10,11... | collective-permute-start | bytes 1572872 | tf_op jit(solution)/shard_map/ppermute | solution.py:25
  15.3 0.2 shard_map.101
  15.5 1.4 %collective-permute-start.2 = (bf16[48,1024]{1,0:T(8,128)(2,1)S(1)}, bf16[48,1024]{1,0:T(8,128)(2,1)S(1)}, u32[]{:S(2)}, u32[]{:S(2)}) collective-permute-start(bf16[48,1024]{1,0:T(8,128)(2,1)S(1)} %get-tuple-element.32), channel_id=1, source_target_pairs={{0,8},{8,16},{16,24},{1,9},{9,17},{17,25},{2,10},{10,18},{18,26},{... | collective-permute-start | bytes 294920 | tf_op jit(solution)/shard_map/ppermute | solution.py:346
  17.0 1.3 %collective-permute-start.3 = (bf16[48,1024]{1,0:T(8,128)(2,1)S(1)}, bf16[48,1024]{1,0:T(8,128)(2,1)S(1)}, u32[]{:S(2)}, u32[]{:S(2)}) collective-permute-start(bf16[48,1024]{1,0:T(8,128)(2,1)S(1)} %get-tuple-element.33), channel_id=1, source_target_pairs={{8,0},{16,8},{24,16},{9,1},{17,9},{25,17},{10,2},{18,10},{26,18},{... | collective-permute-start | bytes 294920 | tf_op jit(solution)/shard_map/ppermute | solution.py:347
  18.3 2.7 %collective-permute-done.5.refs_6_ = bf16[128,1024]{1,0:T(8,128)(2,1)S(1)} collective-permute-done((bf16[128,1024]{1,0:T(8,128)(2,1)S(1)}, bf16[128,1024]{1,0:T(8,128)(2,1)S(1)}, u32[]{:S(2)}, u32[]{:S(2)}) %collective-permute-start.5) | collective-permute-done | bytes 262176 | tf_op jit(solution)/shard_map/ppermute | solution.py:20
  21.0 0.9 %collective-permute-done.3.high_ref = bf16[48,1024]{1,0:T(8,128)(2,1)S(1)} collective-permute-done((bf16[48,1024]{1,0:T(8,128)(2,1)S(1)}, bf16[48,1024]{1,0:T(8,128)(2,1)S(1)}, u32[]{:S(2)}, u32[]{:S(2)}) %collective-permute-start.3) | collective-permute-done | bytes 98336 | tf_op jit(solution)/shard_map/ppermute | solution.py:347
  21.9 0.3 collective-permute-start.6
  22.3 0.1 stack.35.order_ref
  22.4 0.6 copy-done.8
  23.0 5.0 %shard_map.102.refs_3_ = bf16[256,1024]{1,0:T(8,128)(2,1)S(1)} custom-call(s32[8]{0:T(128)S(1)} %stack.35.order_ref, bf16[32,8,1024]{2,1,0:T(8,128)(2,1)S(1)} %copy-done.1, bf16[48,1024]{1,0:T(8,128)(2,1)S(1)} %collective-permute-done.2.low_ref, bf16[48,1024]{1,0:T(8,128)(2,1)S(1)} %collective-permute-done.3.high_ref, ...), custom_call_target="tpu_custom_call" | custom-call | flops 26214400 | bytes 2097152 | tf_op jit(solution)/shard_map/pallas_call | solution.py:137
  28.0 3.1 %collective-permute-start.4 = (bf16[256,1024]{1,0:T(8,128)(2,1)S(1)}, bf16[256,1024]{1,0:T(8,128)(2,1)S(1)}, u32[]{:S(2)}, u32[]{:S(2)}) collective-permute-start(bf16[256,1024]{1,0:T(8,128)(2,1)S(1)} %shard_map.102.refs_3_), channel_id=1, source_target_pairs={{0,16},{8,24},{16,0},{24,8},{1,17},{9,25},{17,1},{25,9},{2,18},{10... | collective-permute-start | bytes 1572872 | tf_op jit(solution)/shard_map/ppermute | solution.py:25
  31.1 1.7 %collective-permute-start.11 = (bf16[256,1024]{1,0:T(8,128)(2,1)S(1)}, bf16[256,1024]{1,0:T(8,128)(2,1)S(1)}, u32[]{:S(2)}, u32[]{:S(2)}) collective-permute-start(bf16[256,1024]{1,0:T(8,128)(2,1)S(1)} %collective-permute-done.10.refs_8_.refs_4_), channel_id=1, source_target_pairs={{0,1},{1,0},{2,3},{3,2},{4,5},{5,4},{6,7},{7,6},{8,9},{9,8},{10,11... | collective-permute-start | bytes 1572872 | tf_op jit(solution)/shard_map/ppermute | solution.py:25
  32.8 3.6 %collective-permute-done.7.refs_10_ = bf16[128,1024]{1,0:T(8,128)(2,1)S(1)} collective-permute-done((bf16[128,1024]{1,0:T(8,128)(2,1)S(1)}, bf16[128,1024]{1,0:T(8,128)(2,1)S(1)}, u32[]{:S(2)}, u32[]{:S(2)}) %collective-permute-start.7) | collective-permute-done | bytes 262176 | tf_op jit(solution)/shard_map/ppermute | solution.py:20
  36.5 1.1 %collective-permute-start.13 = (bf16[256,1024]{1,0:T(8,128)(2,1)S(1)}, bf16[256,1024]{1,0:T(8,128)(2,1)S(1)}, u32[]{:S(2)}, u32[]{:S(2)}) collective-permute-start(bf16[256,1024]{1,0:T(8,128)(2,1)S(1)} %pad_maximum_fusion), channel_id=1, source_target_pairs={{0,2},{1,3},{2,4},{3,5},{4,6},{5,7},{6,0},{7,1},{8,10},{9,11},{10,... | collective-permute-start | bytes 1572872 | tf_op jit(solution)/shard_map/ppermute | solution.py:20
  37.6 5.3 %collective-permute-done.4.refs_1_ = bf16[256,1024]{1,0:T(8,128)(2,1)S(1)} collective-permute-done((bf16[256,1024]{1,0:T(8,128)(2,1)S(1)}, bf16[256,1024]{1,0:T(8,128)(2,1)S(1)}, u32[]{:S(2)}, u32[]{:S(2)}) %collective-permute-start.4) | collective-permute-done | bytes 524320 | tf_op jit(solution)/shard_map/ppermute | solution.py:25
  42.9 2.3 %collective-permute-done.11.refs_9_.refs_5_ = bf16[256,1024]{1,0:T(8,128)(2,1)S(1)} collective-permute-done((bf16[256,1024]{1,0:T(8,128)(2,1)S(1)}, bf16[256,1024]{1,0:T(8,128)(2,1)S(1)}, u32[]{:S(2)}, u32[]{:S(2)}) %collective-permute-start.11) | collective-permute-done | bytes 524320 | tf_op jit(solution)/shard_map/ppermute | solution.py:25
  45.2 1.7 %collective-permute-start.14 = (bf16[128,1024]{1,0:T(8,128)(2,1)S(1)}, bf16[128,1024]{1,0:T(8,128)(2,1)S(1)}, u32[]{:S(2)}, u32[]{:S(2)}) collective-permute-start(bf16[128,1024]{1,0:T(8,128)(2,1)S(1)} %collective-permute-done.7.refs_10_), channel_id=1, source_target_pairs={{0,1},{1,0},{2,3},{3,2},{4,5},{5,4},{6,7},{7,6},{8,9},{9,8},{10,11... | collective-permute-start | bytes 786440 | tf_op jit(solution)/shard_map/ppermute | solution.py:25
  46.9 5.7 %collective-permute-done.13.refs_3_ = bf16[256,1024]{1,0:T(8,128)(2,1)S(1)} collective-permute-done((bf16[256,1024]{1,0:T(8,128)(2,1)S(1)}, bf16[256,1024]{1,0:T(8,128)(2,1)S(1)}, u32[]{:S(2)}, u32[]{:S(2)}) %collective-permute-start.13) | collective-permute-done | bytes 524320 | tf_op jit(solution)/shard_map/ppermute | solution.py:20
  52.7 3.3 %shard_map.103 = (f32[256,1024]{1,0:T(8,128)S(1)}, f32[256,1024]{1,0:T(8,128)S(1)}, f32[256,1024]{1,0:T(8,128)S(1)}, f32[256,1024]{1,0:T(8,128)S(1)}) custom-call(bf16[256,1024]{1,0:T(8,128)(2,1)S(1)} %collective-permute-done.12.refs_0_, bf16[256,1024]{1,0:T(8,128)(2,1)S(1)} %collective-permute-done.4.refs_1_, ...), custom_call_target="tpu_custom_call" | custom-call | flops 1879048192 | bytes 1048576 | tf_op jit(solution)/shard_map/pallas_call | solution.py:177
  56.0 1.1 %shard_map.104 = (bf16[256,1024]{1,0:T(8,128)(2,1)S(1)}, bf16[256,1024]{1,0:T(8,128)(2,1)S(1)}, bf16[256,1024]{1,0:T(8,128)(2,1)S(1)}, bf16[256,1024]{1,0:T(8,128)(2,1)S(1)}) custom-call(bf16[256,1024]{1,0:T(8,128)(2,1)S(1)} %collective-permute-done.12.refs_0_, bf16[256,1024]{1,0:T(8,128)(2,1)S(1)} %collective-permute-done.4.refs_1_, ...), custom_call_target="tpu_custom_call" | custom-call | flops 268435456 | bytes 1048576 | tf_op jit(solution)/shard_map/pallas_call | solution.py:208
  57.1 0.8 %shard_map.109 = bf16[256,768]{1,0:T(8,128)(2,1)S(1)} custom-call(bf16[256,1024]{1,0:T(8,128)(2,1)S(1)} %get-tuple-element.52.refs_0_, bf16[128,1024]{1,0:T(8,128)(2,1)S(1)} %copy-done.2, bf16[256,1024]{1,0:T(8,128)(2,1)S(1)} %collective-permute-done.8.refs_5_.refs_2_, bf16[256,1024]{1,0:T(8,128)(2,1)S(1)} %collective-permute-done.13.refs_3_, ...), custom_call_target="tpu_custom_call" | custom-call | flops 402653184 | bytes 6291456 | tf_op jit(solution)/shard_map/pallas_call | solution.py:236
  57.9 0.1 collective-permute-start.17
  58.0 0.8 %shard_map.114 = bf16[256,768]{1,0:T(8,128)(2,1)S(1)} custom-call(bf16[256,1024]{1,0:T(8,128)(2,1)S(1)} %get-tuple-element.50.refs_0_, bf16[128,1024]{1,0:T(8,128)(2,1)S(1)} %copy-done.2, bf16[256,1024]{1,0:T(8,128)(2,1)S(1)} %collective-permute-done.8.refs_5_.refs_2_, bf16[256,1024]{1,0:T(8,128)(2,1)S(1)} %collective-permute-done.13.refs_3_, ...), custom_call_target="tpu_custom_call" | custom-call | flops 402653184 | bytes 6291456 | tf_op jit(solution)/shard_map/pallas_call | solution.py:236
  58.9 0.6 collective-permute-start.20
  59.4 0.8 %shard_map.108.one_ref = bf16[256,768]{1,0:T(8,128)(2,1)S(1)} custom-call(bf16[256,1024]{1,0:T(8,128)(2,1)S(1)} %get-tuple-element.51.refs_0_, bf16[128,1024]{1,0:T(8,128)(2,1)S(1)} %copy-done.2, bf16[256,1024]{1,0:T(8,128)(2,1)S(1)} %collective-permute-done.8.refs_5_.refs_2_, bf16[256,1024]{1,0:T(8,128)(2,1)S(1)} %collective-permute-done.13.refs_3_, ...), custom_call_target="tpu_custom_call" | custom-call | flops 402653184 | bytes 6291456 | tf_op jit(solution)/shard_map/pallas_call | solution.py:236
  60.3 0.1 shard_map.110
  60.4 1.6 %collective-permute-start.21 = (bf16[256,768]{1,0:T(8,128)(2,1)S(1)}, bf16[256,768]{1,0:T(8,128)(2,1)S(1)}, u32[]{:S(2)}, u32[]{:S(2)}) collective-permute-start(bf16[256,768]{1,0:T(8,128)(2,1)S(1)} %shard_map.110), channel_id=1, source_target_pairs={{0,16},{8,24},{16,0},{24,8},{1,17},{9,25},{17,1},{25,9},{2,18},{10... | collective-permute-start | bytes 1179656 | tf_op jit(solution)/shard_map/ppermute | solution.py:25
  62.0 6.0 %collective-permute-done.15.refs_1_ = bf16[256,1024]{1,0:T(8,128)(2,1)S(1)} collective-permute-done((bf16[256,1024]{1,0:T(8,128)(2,1)S(1)}, bf16[256,1024]{1,0:T(8,128)(2,1)S(1)}, u32[]{:S(2)}, u32[]{:S(2)}) %collective-permute-start.15) | collective-permute-done | bytes 524320 | tf_op jit(solution)/shard_map/ppermute | solution.py:20
  68.0 0.3 shard_map.111
  68.4 0.3 shard_map.106
  68.8 0.6 collective-permute-start.16
  69.3 0.3 shard_map.107.one_ref
  69.7 0.1 collective-permute-done.18.two_ref
  69.8 1.6 %collective-permute-start.19 = (bf16[256,256]{1,0:T(8,128)(2,1)S(1)}, bf16[256,256]{1,0:T(8,128)(2,1)S(1)}, u32[]{:S(2)}, u32[]{:S(2)}) collective-permute-start(bf16[256,256]{1,0:T(8,128)(2,1)S(1)} %shard_map.112), channel_id=1, source_target_pairs={{0,16},{8,24},{16,0},{24,8},{1,17},{9,25},{17,1},{25,9},{2,18},{10... | collective-permute-start | bytes 393224 | tf_op jit(solution)/shard_map/ppermute | solution.py:25
  71.4 0.3 shard_map.105.one_ref
  71.7 0.8 %shard_map.113.one_ref = bf16[256,768]{1,0:T(8,128)(2,1)S(1)} custom-call(bf16[256,1024]{1,0:T(8,128)(2,1)S(1)} %get-tuple-element.49.refs_0_, bf16[128,1024]{1,0:T(8,128)(2,1)S(1)} %copy-done.2, bf16[256,1024]{1,0:T(8,128)(2,1)S(1)} %collective-permute-done.8.refs_5_.refs_2_, bf16[256,1024]{1,0:T(8,128)(2,1)S(1)} %collective-permute-done.13.refs_3_, ...), custom_call_target="tpu_custom_call" | custom-call | flops 402653184 | bytes 6291456 | tf_op jit(solution)/shard_map/pallas_call | solution.py:236
  72.6 0.6 copy-done.4
  73.3 1.5 %shard_map.115.refs_0_ = bf16[256,1024]{1,0:T(8,128)(2,1)} custom-call(s32[8]{0:T(128)S(1)} %stack.35.order_ref, bf16[256,1024]{1,0:T(8,128)(2,1)S(1)} %bitcast.16, bf16[256,768]{1,0:T(8,128)(2,1)S(1)} %shard_map.113.one_ref, bf16[256,768]{1,0:T(8,128)(2,1)S(1)} %collective-permute-done.20.two_ref, bf16[256,768]{1,0:T(8,128)(2,1)S(1)} %collective-permute-done.21.far_ref, ...), custom_call_target="tpu_custom_call" | custom-call | tf_op jit(solution)/shard_map/pallas_call | solution.py:288
  74.8 0.6 collective-permute-done.19.far_ref
  75.4 1.3 %shard_map.116 = bf16[256,1024]{1,0:T(8,128)(2,1)} custom-call(s32[8]{0:T(128)S(1)} %stack.35.order_ref, bf16[256,1024]{1,0:T(8,128)(2,1)S(1)} %bitcast.17, bf16[256,256]{1,0:T(8,128)(2,1)S(1)} %shard_map.105.one_ref, bf16[256,256]{1,0:T(8,128)(2,1)S(1)} %collective-permute-done.16.two_ref, ...), custom_call_target="tpu_custom_call", output_to_operand_aliasing={{}: (7, {})} | custom-call | tf_op jit(solution)/shard_map/pallas_call | solution.py:288
  (41 shorter events, 0.3 us)
Async XLA Ops:
  0.0 1.0 %copy-start = (bf16[32,8,1024]{2,1,0:T(8,128)(2,1)S(1)}, bf16[32,8,1024]{2,1,0:T(8,128)(2,1)}, u32[]{:S(2)}) copy-start(bf16[32,8,1024]{2,1,0:T(8,128)(2,1)} %mid_ref.5) | copy-start | bytes 1572868
  1.0 6.5 %copy-start.3 = (bf16[128,1024]{1,0:T(8,128)(2,1)S(1)}, bf16[128,1024]{1,0:T(8,128)(2,1)}, u32[]{:S(2)}) copy-start(bf16[128,1024]{1,0:T(8,128)(2,1)} %refs_4_.1) | copy-start | bytes 786436
  1.5 11.9 %collective-permute-start = (bf16[3,32,1024]{2,1,0:T(8,128)(2,1)S(1)}, bf16[3,32,1024]{2,1,0:T(8,128)(2,1)S(1)}, u32[]{:S(2)}, u32[]{:S(2)}) collective-permute-start(bf16[3,32,1024]{2,1,0:T(8,128)(2,1)S(1)} %get-tuple-element.30), channel_id=1, source_target_pairs={{0,1},{1,2},{2,3},{3,4},{4,5},{5,6},{6,7},{7,0},{8,9},{9,10},{10,1... | collective-permute-start | bytes 589832 | tf_op jit(solution)/shard_map/ppermute | solution.py:343
  4.4 3.8 %copy-start.2 = (bf16[128,1024]{1,0:T(8,128)(2,1)S(1)}, bf16[128,1024]{1,0:T(8,128)(2,1)}, u32[]{:S(2)}) copy-start(bf16[128,1024]{1,0:T(8,128)(2,1)} %refs_1_.7) | copy-start | bytes 786436
  4.4 10.9 %collective-permute-start.1 = (bf16[3,32,1024]{2,1,0:T(8,128)(2,1)S(1)}, bf16[3,32,1024]{2,1,0:T(8,128)(2,1)S(1)}, u32[]{:S(2)}, u32[]{:S(2)}) collective-permute-start(bf16[3,32,1024]{2,1,0:T(8,128)(2,1)S(1)} %get-tuple-element.31), channel_id=1, source_target_pairs={{1,0},{2,1},{3,2},{4,3},{5,4},{6,5},{7,6},{0,7},{9,8},{10,9},{11,1... | collective-permute-start | bytes 589832 | tf_op jit(solution)/shard_map/ppermute | solution.py:344
  7.6 13.4 %collective-permute-start.5 = (bf16[128,1024]{1,0:T(8,128)(2,1)S(1)}, bf16[128,1024]{1,0:T(8,128)(2,1)S(1)}, u32[]{:S(2)}, u32[]{:S(2)}) collective-permute-start(bf16[128,1024]{1,0:T(8,128)(2,1)S(1)} %copy-done.3), channel_id=1, source_target_pairs={{0,2},{1,3},{2,4},{3,5},{4,6},{5,7},{6,0},{7,1},{8,10},{9,11},{10,... | collective-permute-start | bytes 786440 | tf_op jit(solution)/shard_map/ppermute | solution.py:20
  9.0 13.4 %copy-start.1 = (bf16[32,8,1024]{2,1,0:T(8,128)(2,1)S(1)}, bf16[32,8,1024]{2,1,0:T(8,128)(2,1)}, u32[]{:S(2)}) copy-start(bf16[32,8,1024]{2,1,0:T(8,128)(2,1)} %mid_ref.5) | copy-start | bytes 1572868
  9.0 22.1 %collective-permute-start.10 = (bf16[256,1024]{1,0:T(8,128)(2,1)}, bf16[256,1024]{1,0:T(8,128)(2,1)S(1)}, u32[]{:S(2)}, u32[]{:S(2)}) collective-permute-start(bf16[256,1024]{1,0:T(8,128)(2,1)} %constant_dynamic-update-slice_fusion), channel_id=1, source_target_pairs={{0,6},{1,7},{2,0},{3,1},{4,2},{5,3},{6,4},{7,5},{8,14},{9,15},{10,... | collective-permute-start | bytes 1572872 | tf_op jit(solution)/shard_map/ppermute | solution.py:20
  13.4 23.0 %collective-permute-start.8 = (bf16[256,1024]{1,0:T(8,128)(2,1)}, bf16[256,1024]{1,0:T(8,128)(2,1)S(1)}, u32[]{:S(2)}, u32[]{:S(2)}) collective-permute-start(bf16[256,1024]{1,0:T(8,128)(2,1)} %constant_dynamic-update-slice_fusion), channel_id=1, source_target_pairs={{0,1},{1,0},{2,3},{3,2},{4,5},{5,4},{6,7},{7,6},{8,9},{9,8},{10,11... | collective-permute-start | bytes 1572872 | tf_op jit(solution)/shard_map/ppermute | solution.py:25
  15.5 6.7 %copy-start.10 = (bf16[7,7,1024]{2,1,0:T(8,128)(2,1)S(1)}, bf16[7,7,1024]{2,1,0:T(8,128)(2,1)}, u32[]{:S(2)}) copy-start(bf16[7,7,1024]{2,1,0:T(8,128)(2,1)} %param.11) | copy-start | bytes 301060
  15.5 5.4 %collective-permute-start.2 = (bf16[48,1024]{1,0:T(8,128)(2,1)S(1)}, bf16[48,1024]{1,0:T(8,128)(2,1)S(1)}, u32[]{:S(2)}, u32[]{:S(2)}) collective-permute-start(bf16[48,1024]{1,0:T(8,128)(2,1)S(1)} %get-tuple-element.32), channel_id=1, source_target_pairs={{0,8},{8,16},{16,24},{1,9},{9,17},{17,25},{2,10},{10,18},{18,26},{... | collective-permute-start | bytes 294920 | tf_op jit(solution)/shard_map/ppermute | solution.py:346
  17.0 4.9 %collective-permute-start.3 = (bf16[48,1024]{1,0:T(8,128)(2,1)S(1)}, bf16[48,1024]{1,0:T(8,128)(2,1)S(1)}, u32[]{:S(2)}, u32[]{:S(2)}) collective-permute-start(bf16[48,1024]{1,0:T(8,128)(2,1)S(1)} %get-tuple-element.33), channel_id=1, source_target_pairs={{8,0},{16,8},{24,16},{9,1},{17,9},{25,17},{10,2},{18,10},{26,18},{... | collective-permute-start | bytes 294920 | tf_op jit(solution)/shard_map/ppermute | solution.py:347
  21.0 15.4 %collective-permute-start.7 = (bf16[128,1024]{1,0:T(8,128)(2,1)S(1)}, bf16[128,1024]{1,0:T(8,128)(2,1)S(1)}, u32[]{:S(2)}, u32[]{:S(2)}) collective-permute-start(bf16[128,1024]{1,0:T(8,128)(2,1)S(1)} %collective-permute-done.5.refs_6_), channel_id=1, source_target_pairs={{0,2},{1,3},{2,4},{3,5},{4,6},{5,7},{6,0},{7,1},{8,10},{9,11},{10,... | collective-permute-start | bytes 786440 | tf_op jit(solution)/shard_map/ppermute | solution.py:20
  21.9 14.5 %collective-permute-start.6 = (bf16[128,1024]{1,0:T(8,128)(2,1)S(1)}, bf16[128,1024]{1,0:T(8,128)(2,1)}, u32[]{:S(2)}, u32[]{:S(2)}) collective-permute-start(bf16[128,1024]{1,0:T(8,128)(2,1)S(1)} %collective-permute-done.5.refs_6_), channel_id=1, source_target_pairs={{0,1},{1,0},{2,3},{3,2},{4,5},{5,4},{6,7},{7,6},{8,9},{9,8},{10,11... | collective-permute-start | bytes 786440 | tf_op jit(solution)/shard_map/ppermute | solution.py:25
  22.3 0.7 copy-start.8
  22.3 0.7 copy-start.6
  22.3 0.7 copy-start.7
  28.0 15.0 %collective-permute-start.4 = (bf16[256,1024]{1,0:T(8,128)(2,1)S(1)}, bf16[256,1024]{1,0:T(8,128)(2,1)S(1)}, u32[]{:S(2)}, u32[]{:S(2)}) collective-permute-start(bf16[256,1024]{1,0:T(8,128)(2,1)S(1)} %shard_map.102.refs_3_), channel_id=1, source_target_pairs={{0,16},{8,24},{16,0},{24,8},{1,17},{9,25},{17,1},{25,9},{2,18},{10... | collective-permute-start | bytes 1572872 | tf_op jit(solution)/shard_map/ppermute | solution.py:25
  31.1 14.1 %collective-permute-start.11 = (bf16[256,1024]{1,0:T(8,128)(2,1)S(1)}, bf16[256,1024]{1,0:T(8,128)(2,1)S(1)}, u32[]{:S(2)}, u32[]{:S(2)}) collective-permute-start(bf16[256,1024]{1,0:T(8,128)(2,1)S(1)} %collective-permute-done.10.refs_8_.refs_4_), channel_id=1, source_target_pairs={{0,1},{1,0},{2,3},{3,2},{4,5},{5,4},{6,7},{7,6},{8,9},{9,8},{10,11... | collective-permute-start | bytes 1572872 | tf_op jit(solution)/shard_map/ppermute | solution.py:25
  36.4 8.8 %collective-permute-start.9 = (bf16[256,1024]{1,0:T(8,128)(2,1)S(1)}, bf16[256,1024]{1,0:T(8,128)(2,1)S(1)}, u32[]{:S(2)}, u32[]{:S(2)}) collective-permute-start(bf16[256,1024]{1,0:T(8,128)(2,1)S(1)} %shard_map.102.refs_3_), channel_id=1, source_target_pairs={{0,8},{8,0},{16,24},{24,16},{1,9},{9,1},{17,25},{25,17},{2,10},{10... | collective-permute-start | bytes 1572872 | tf_op jit(solution)/shard_map/ppermute | solution.py:25
  36.4 16.2 %copy-start.9 = (f32[1024]{0:T(1024)S(1)}, f32[1024]{0:T(1024)}, u32[]{:S(2)}) copy-start(f32[1024]{0:T(1024)} %param.16) | copy-start | bytes 12292
  36.5 16.2 %collective-permute-start.13 = (bf16[256,1024]{1,0:T(8,128)(2,1)S(1)}, bf16[256,1024]{1,0:T(8,128)(2,1)S(1)}, u32[]{:S(2)}, u32[]{:S(2)}) collective-permute-start(bf16[256,1024]{1,0:T(8,128)(2,1)S(1)} %pad_maximum_fusion), channel_id=1, source_target_pairs={{0,2},{1,3},{2,4},{3,5},{4,6},{5,7},{6,0},{7,1},{8,10},{9,11},{10,... | collective-permute-start | bytes 1572872 | tf_op jit(solution)/shard_map/ppermute | solution.py:20
  45.2 7.4 %collective-permute-start.12 = (bf16[256,1024]{1,0:T(8,128)(2,1)S(1)}, bf16[256,1024]{1,0:T(8,128)(2,1)S(1)}, u32[]{:S(2)}, u32[]{:S(2)}) collective-permute-start(bf16[256,1024]{1,0:T(8,128)(2,1)S(1)} %collective-permute-done.4.refs_1_), channel_id=1, source_target_pairs={{0,8},{8,0},{16,24},{24,16},{1,9},{9,1},{17,25},{25,17},{2,10},{10... | collective-permute-start | bytes 1572872 | tf_op jit(solution)/shard_map/ppermute | solution.py:25
  45.2 10.8 %collective-permute-start.14 = (bf16[128,1024]{1,0:T(8,128)(2,1)S(1)}, bf16[128,1024]{1,0:T(8,128)(2,1)S(1)}, u32[]{:S(2)}, u32[]{:S(2)}) collective-permute-start(bf16[128,1024]{1,0:T(8,128)(2,1)S(1)} %collective-permute-done.7.refs_10_), channel_id=1, source_target_pairs={{0,1},{1,0},{2,3},{3,2},{4,5},{5,4},{6,7},{7,6},{8,9},{9,8},{10,11... | collective-permute-start | bytes 786440 | tf_op jit(solution)/shard_map/ppermute | solution.py:25
  52.7 15.3 %collective-permute-start.15 = (bf16[256,1024]{1,0:T(8,128)(2,1)S(1)}, bf16[256,1024]{1,0:T(8,128)(2,1)S(1)}, u32[]{:S(2)}, u32[]{:S(2)}) collective-permute-start(bf16[256,1024]{1,0:T(8,128)(2,1)S(1)} %collective-permute-done.13.refs_3_), channel_id=1, source_target_pairs={{0,2},{1,3},{2,4},{3,5},{4,6},{5,7},{6,0},{7,1},{8,10},{9,11},{10,... | collective-permute-start | bytes 1572872 | tf_op jit(solution)/shard_map/ppermute | solution.py:20
  57.9 2.3 %collective-permute-start.17 = (bf16[256,768]{1,0:T(8,128)(2,1)S(1)}, bf16[256,768]{1,0:T(8,128)(2,1)S(1)}, u32[]{:S(2)}, u32[]{:S(2)}) collective-permute-start(bf16[256,768]{1,0:T(8,128)(2,1)S(1)} %shard_map.109), channel_id=1, source_target_pairs={{0,8},{8,0},{16,24},{24,16},{1,9},{9,1},{17,25},{25,17},{2,10},{10... | collective-permute-start | bytes 1179656 | tf_op jit(solution)/shard_map/ppermute | solution.py:25
  58.9 13.7 %collective-permute-start.20 = (bf16[256,768]{1,0:T(8,128)(2,1)S(1)}, bf16[256,768]{1,0:T(8,128)(2,1)S(1)}, u32[]{:S(2)}, u32[]{:S(2)}) collective-permute-start(bf16[256,768]{1,0:T(8,128)(2,1)S(1)} %shard_map.114), channel_id=1, source_target_pairs={{0,8},{8,0},{16,24},{24,16},{1,9},{9,1},{17,25},{25,17},{2,10},{10... | collective-permute-start | bytes 1179656 | tf_op jit(solution)/shard_map/ppermute | solution.py:25
  60.4 12.2 %collective-permute-start.21 = (bf16[256,768]{1,0:T(8,128)(2,1)S(1)}, bf16[256,768]{1,0:T(8,128)(2,1)S(1)}, u32[]{:S(2)}, u32[]{:S(2)}) collective-permute-start(bf16[256,768]{1,0:T(8,128)(2,1)S(1)} %shard_map.110), channel_id=1, source_target_pairs={{0,16},{8,24},{16,0},{24,8},{1,17},{9,25},{17,1},{25,9},{2,18},{10... | collective-permute-start | bytes 1179656 | tf_op jit(solution)/shard_map/ppermute | solution.py:25
  68.3 1.4 %collective-permute-start.18 = (bf16[256,256]{1,0:T(8,128)(2,1)S(1)}, bf16[256,256]{1,0:T(8,128)(2,1)S(1)}, u32[]{:S(2)}, u32[]{:S(2)}) collective-permute-start(bf16[256,256]{1,0:T(8,128)(2,1)S(1)} %shard_map.111), channel_id=1, source_target_pairs={{0,8},{8,0},{16,24},{24,16},{1,9},{9,1},{17,25},{25,17},{2,10},{10... | collective-permute-start | bytes 393224 | tf_op jit(solution)/shard_map/ppermute | solution.py:25
  68.8 6.0 %collective-permute-start.16 = (bf16[256,256]{1,0:T(8,128)(2,1)S(1)}, bf16[256,256]{1,0:T(8,128)(2,1)S(1)}, u32[]{:S(2)}, u32[]{:S(2)}) collective-permute-start(bf16[256,256]{1,0:T(8,128)(2,1)S(1)} %shard_map.106), channel_id=1, source_target_pairs={{0,8},{8,0},{16,24},{24,16},{1,9},{9,1},{17,25},{25,17},{2,10},{10... | collective-permute-start | bytes 393224 | tf_op jit(solution)/shard_map/ppermute | solution.py:25
  69.8 5.6 %collective-permute-start.19 = (bf16[256,256]{1,0:T(8,128)(2,1)S(1)}, bf16[256,256]{1,0:T(8,128)(2,1)S(1)}, u32[]{:S(2)}, u32[]{:S(2)}) collective-permute-start(bf16[256,256]{1,0:T(8,128)(2,1)S(1)} %shard_map.112), channel_id=1, source_target_pairs={{0,16},{8,24},{16,0},{24,8},{1,17},{9,25},{17,1},{25,9},{2,18},{10... | collective-permute-start | bytes 393224 | tf_op jit(solution)/shard_map/ppermute | solution.py:25
  71.7 0.9 %copy-start.5 = (f32[1024]{0:T(1024)S(1)}, f32[1024]{0:T(1024)}, u32[]{:S(2)}) copy-start(f32[1024]{0:T(1024)} %param.19) | copy-start | bytes 12292
  72.6 0.7 copy-start.4

commit v5 on v4

--- a/solution.py
+++ b/solution.py
@@ -29,7 +29,7 @@
     rows, cols, chans = mid_ref.shape
     for at in range(0, chans, LANES):
         lanes = pl.ds(at, LANES)
-        slab[...] = mid_ref[:, :, lanes].astype(F32).reshape(rows * cols, LANES)
+        slab[pl.ds(0, rows * cols), :] = mid_ref[:, :, lanes].astype(F32).reshape(rows * cols, LANES)
         for col in range(3):
             first_ref[col, :, lanes] = slab[pl.ds(col, rows, stride=cols), :].astype(BF16)
             last_ref[col, :, lanes] = slab[pl.ds(cols - 3 + col, rows, stride=cols), :].astype(BF16)
@@ -46,7 +46,7 @@
         out_shape=(shape, shape),
         in_specs=[pl.BlockSpec((rows, cols, block), lambda i: (0, 0, i))],
         out_specs=(out, out),
-        scratch_shapes=[pltpu.VMEM((rows * cols, LANES), F32)],
+        scratch_shapes=[pltpu.VMEM(((rows + 1) * cols, LANES), F32)],
         compiler_params=PARAMS,
     )(mid)
 
@@ -68,7 +68,7 @@
                 for at, ref in ((col, left_ref), (cols + 3 + col, right_ref)):
                     edge = ref[col, pl.ds(near, 16), lanes].astype(F32)
                     slab[pl.ds(at, 3, stride=WIDE), :] = edge[begin:begin + 3]
-            out_ref[:, lanes] = slab[...].astype(BF16)
+            out_ref[:, lanes] = slab[pl.ds(0, 3 * WIDE), :].astype(BF16)
 
 
 def rims(mid, left, right):
@@ -79,7 +79,7 @@
         out_shape=(shape, shape),
         in_specs=[VMEM] * 3,
         out_specs=(VMEM, VMEM),
-        scratch_shapes=[pltpu.VMEM((3 * WIDE, LANES), F32)],
+        scratch_shapes=[pltpu.VMEM((11 * WIDE, LANES), F32)],
         compiler_params=PARAMS,
     )(mid, left, right)
 

time: 77 us -> 77 us (level)
  no operation moved by 1% of the time
where the time goes in v5:
time: 77 us; the launch traced here: 76.7 us
  waiting for transfers between devices  27.9 us (36%)
  starting transfers between devices  27 us (35%)
  Pallas kernels  17.6 us (23%)
  local copies, waits for them, and re-layouts  3.92 us (5%)
    ppermute x5, waiting for transfers between devices, shift(): lax.ppermute(value, axis, [(i, (i + step * inner) % count) for i in range...  18 us
    ppermute x13, starting transfers between devices, swap(): return lax.ppermute(value, axis, [(i, i ^ bit) for i in range(count)])  13.2 us
    ppermute x13, waiting for transfers between devices, swap(): return lax.ppermute(value, axis, [(i, i ^ bit) for i in range(count)])  8.34 us
    pallas_call x1, Pallas kernels, conv_norm(): pl.pallas_call(conv_kernel, out_shape=jax.ShapeDtypeStruct((rows * cols,...  4.98 us
    ppermute x5, starting transfers between devices, shift(): lax.ppermute(value, axis, [(i, (i + step * inner) % count) for i in range...  4.97 us
    pallas_call x8, Pallas kernels, down(): pl.pallas_call(functools.partial(down_kernel, len(hidden), spans), out_sh...  4.67 us
    pallas_call x1, Pallas kernels, begin(): pl.pallas_call(functools.partial(begin_kernel, len(pixels), spans), out_s...  3.3 us
    ppermute x1, starting transfers between devices, local(): lax.ppermute(first, 'lon', [((i + 1) % lons, i) for i in range(lons)])  3.11 us
  transfers between devices with their start and end apart: 22, of which 10 were waited for; matrix products, arithmetic and copies ran while one was open for 2% of the time, Pallas kernels for 21%

profile of v5, /device:TPU:0, one launch (start us, length us, event | category | flops | bytes accessed | tf_op | source)
XLA Modules:
  0.0 76.7 jit_solution(11439044006031825445)
XLA Ops:
  0.0 1.0 %copy-done = bf16[32,8,1024]{2,1,0:T(8,128)(2,1)S(1)} copy-done((bf16[32,8,1024]{2,1,0:T(8,128)(2,1)S(1)}, bf16[32,8,1024]{2,1,0:T(8,128)(2,1)}, u32[]{:S(2)}) %copy-start) | copy-done | bytes 524312
  1.0 0.4 shard_map.100
  1.5 3.0 %collective-permute-start = (bf16[3,32,1024]{2,1,0:T(8,128)(2,1)S(1)}, bf16[3,32,1024]{2,1,0:T(8,128)(2,1)S(1)}, u32[]{:S(2)}, u32[]{:S(2)}) collective-permute-start(bf16[3,32,1024]{2,1,0:T(8,128)(2,1)S(1)} %get-tuple-element.30), channel_id=1, source_target_pairs={{0,1},{1,2},{2,3},{3,4},{4,5},{5,6},{6,7},{7,0},{8,9},{9,10},{10,1... | collective-permute-start | bytes 589832 | tf_op jit(solution)/shard_map/ppermute | solution.py:343
  4.4 3.1 %collective-permute-start.1 = (bf16[3,32,1024]{2,1,0:T(8,128)(2,1)S(1)}, bf16[3,32,1024]{2,1,0:T(8,128)(2,1)S(1)}, u32[]{:S(2)}, u32[]{:S(2)}) collective-permute-start(bf16[3,32,1024]{2,1,0:T(8,128)(2,1)S(1)} %get-tuple-element.31), channel_id=1, source_target_pairs={{1,0},{2,1},{3,2},{4,3},{5,4},{6,5},{7,6},{0,7},{9,8},{10,9},{11,1... | collective-permute-start | bytes 589832 | tf_op jit(solution)/shard_map/ppermute | solution.py:344
  7.6 0.7 constant_dynamic-update-slice_fusion.1
  8.3 0.7 constant_dynamic-update-slice_fusion
  9.0 3.8 %collective-permute-start.10 = (bf16[256,1024]{1,0:T(8,128)(2,1)}, bf16[256,1024]{1,0:T(8,128)(2,1)S(1)}, u32[]{:S(2)}, u32[]{:S(2)}) collective-permute-start(bf16[256,1024]{1,0:T(8,128)(2,1)} %constant_dynamic-update-slice_fusion), channel_id=1, source_target_pairs={{0,6},{1,7},{2,0},{3,1},{4,2},{5,3},{6,4},{7,5},{8,14},{9,15},{10,... | collective-permute-start | bytes 1572872 | tf_op jit(solution)/shard_map/ppermute | solution.py:20
  12.8 0.5 collective-permute-done.left_ref
  13.4 1.9 %collective-permute-start.8 = (bf16[256,1024]{1,0:T(8,128)(2,1)}, bf16[256,1024]{1,0:T(8,128)(2,1)S(1)}, u32[]{:S(2)}, u32[]{:S(2)}) collective-permute-start(bf16[256,1024]{1,0:T(8,128)(2,1)} %constant_dynamic-update-slice_fusion), channel_id=1, source_target_pairs={{0,1},{1,0},{2,3},{3,2},{4,5},{5,4},{6,7},{7,6},{8,9},{9,8},{10,11... | collective-permute-start | bytes 1572872 | tf_op jit(solution)/shard_map/ppermute | solution.py:25
  15.3 0.2 shard_map.101
  15.5 1.4 %collective-permute-start.2 = (bf16[48,1024]{1,0:T(8,128)(2,1)S(1)}, bf16[48,1024]{1,0:T(8,128)(2,1)S(1)}, u32[]{:S(2)}, u32[]{:S(2)}) collective-permute-start(bf16[48,1024]{1,0:T(8,128)(2,1)S(1)} %get-tuple-element.32), channel_id=1, source_target_pairs={{0,8},{8,16},{16,24},{1,9},{9,17},{17,25},{2,10},{10,18},{18,26},{... | collective-permute-start | bytes 294920 | tf_op jit(solution)/shard_map/ppermute | solution.py:346
  17.0 1.3 %collective-permute-start.3 = (bf16[48,1024]{1,0:T(8,128)(2,1)S(1)}, bf16[48,1024]{1,0:T(8,128)(2,1)S(1)}, u32[]{:S(2)}, u32[]{:S(2)}) collective-permute-start(bf16[48,1024]{1,0:T(8,128)(2,1)S(1)} %get-tuple-element.33), channel_id=1, source_target_pairs={{8,0},{16,8},{24,16},{9,1},{17,9},{25,17},{10,2},{18,10},{26,18},{... | collective-permute-start | bytes 294920 | tf_op jit(solution)/shard_map/ppermute | solution.py:347
  18.3 2.7 %collective-permute-done.5.refs_6_ = bf16[128,1024]{1,0:T(8,128)(2,1)S(1)} collective-permute-done((bf16[128,1024]{1,0:T(8,128)(2,1)S(1)}, bf16[128,1024]{1,0:T(8,128)(2,1)S(1)}, u32[]{:S(2)}, u32[]{:S(2)}) %collective-permute-start.5) | collective-permute-done | bytes 262176 | tf_op jit(solution)/shard_map/ppermute | solution.py:20
  21.0 0.9 %collective-permute-done.3.high_ref = bf16[48,1024]{1,0:T(8,128)(2,1)S(1)} collective-permute-done((bf16[48,1024]{1,0:T(8,128)(2,1)S(1)}, bf16[48,1024]{1,0:T(8,128)(2,1)S(1)}, u32[]{:S(2)}, u32[]{:S(2)}) %collective-permute-start.3) | collective-permute-done | bytes 98336 | tf_op jit(solution)/shard_map/ppermute | solution.py:347
  21.9 0.3 collective-permute-start.6
  22.3 0.1 stack.35.order_ref
  22.4 0.6 copy-done.8
  23.0 5.0 %shard_map.102.refs_3_ = bf16[256,1024]{1,0:T(8,128)(2,1)S(1)} custom-call(s32[8]{0:T(128)S(1)} %stack.35.order_ref, bf16[32,8,1024]{2,1,0:T(8,128)(2,1)S(1)} %copy-done.1, bf16[48,1024]{1,0:T(8,128)(2,1)S(1)} %collective-permute-done.2.low_ref, bf16[48,1024]{1,0:T(8,128)(2,1)S(1)} %collective-permute-done.3.high_ref, ...), custom_call_target="tpu_custom_call" | custom-call | flops 26214400 | bytes 2097152 | tf_op jit(solution)/shard_map/pallas_call | solution.py:137
  28.0 3.1 %collective-permute-start.4 = (bf16[256,1024]{1,0:T(8,128)(2,1)S(1)}, bf16[256,1024]{1,0:T(8,128)(2,1)S(1)}, u32[]{:S(2)}, u32[]{:S(2)}) collective-permute-start(bf16[256,1024]{1,0:T(8,128)(2,1)S(1)} %shard_map.102.refs_3_), channel_id=1, source_target_pairs={{0,16},{8,24},{16,0},{24,8},{1,17},{9,25},{17,1},{25,9},{2,18},{10... | collective-permute-start | bytes 1572872 | tf_op jit(solution)/shard_map/ppermute | solution.py:25
  31.1 1.7 %collective-permute-start.11 = (bf16[256,1024]{1,0:T(8,128)(2,1)S(1)}, bf16[256,1024]{1,0:T(8,128)(2,1)S(1)}, u32[]{:S(2)}, u32[]{:S(2)}) collective-permute-start(bf16[256,1024]{1,0:T(8,128)(2,1)S(1)} %collective-permute-done.10.refs_8_.refs_4_), channel_id=1, source_target_pairs={{0,1},{1,0},{2,3},{3,2},{4,5},{5,4},{6,7},{7,6},{8,9},{9,8},{10,11... | collective-permute-start | bytes 1572872 | tf_op jit(solution)/shard_map/ppermute | solution.py:25
  32.8 3.6 %collective-permute-done.7.refs_10_ = bf16[128,1024]{1,0:T(8,128)(2,1)S(1)} collective-permute-done((bf16[128,1024]{1,0:T(8,128)(2,1)S(1)}, bf16[128,1024]{1,0:T(8,128)(2,1)S(1)}, u32[]{:S(2)}, u32[]{:S(2)}) %collective-permute-start.7) | collective-permute-done | bytes 262176 | tf_op jit(solution)/shard_map/ppermute | solution.py:20
  36.5 1.1 %collective-permute-start.13 = (bf16[256,1024]{1,0:T(8,128)(2,1)S(1)}, bf16[256,1024]{1,0:T(8,128)(2,1)S(1)}, u32[]{:S(2)}, u32[]{:S(2)}) collective-permute-start(bf16[256,1024]{1,0:T(8,128)(2,1)S(1)} %pad_maximum_fusion), channel_id=1, source_target_pairs={{0,2},{1,3},{2,4},{3,5},{4,6},{5,7},{6,0},{7,1},{8,10},{9,11},{10,... | collective-permute-start | bytes 1572872 | tf_op jit(solution)/shard_map/ppermute | solution.py:20
  37.6 5.3 %collective-permute-done.4.refs_1_ = bf16[256,1024]{1,0:T(8,128)(2,1)S(1)} collective-permute-done((bf16[256,1024]{1,0:T(8,128)(2,1)S(1)}, bf16[256,1024]{1,0:T(8,128)(2,1)S(1)}, u32[]{:S(2)}, u32[]{:S(2)}) %collective-permute-start.4) | collective-permute-done | bytes 524320 | tf_op jit(solution)/shard_map/ppermute | solution.py:25
  42.9 2.3 %collective-permute-done.11.refs_9_.refs_5_ = bf16[256,1024]{1,0:T(8,128)(2,1)S(1)} collective-permute-done((bf16[256,1024]{1,0:T(8,128)(2,1)S(1)}, bf16[256,1024]{1,0:T(8,128)(2,1)S(1)}, u32[]{:S(2)}, u32[]{:S(2)}) %collective-permute-start.11) | collective-permute-done | bytes 524320 | tf_op jit(solution)/shard_map/ppermute | solution.py:25
  45.2 1.7 %collective-permute-start.14 = (bf16[128,1024]{1,0:T(8,128)(2,1)S(1)}, bf16[128,1024]{1,0:T(8,128)(2,1)S(1)}, u32[]{:S(2)}, u32[]{:S(2)}) collective-permute-start(bf16[128,1024]{1,0:T(8,128)(2,1)S(1)} %collective-permute-done.7.refs_10_), channel_id=1, source_target_pairs={{0,1},{1,0},{2,3},{3,2},{4,5},{5,4},{6,7},{7,6},{8,9},{9,8},{10,11... | collective-permute-start | bytes 786440 | tf_op jit(solution)/shard_map/ppermute | solution.py:25
  46.9 5.7 %collective-permute-done.13.refs_3_ = bf16[256,1024]{1,0:T(8,128)(2,1)S(1)} collective-permute-done((bf16[256,1024]{1,0:T(8,128)(2,1)S(1)}, bf16[256,1024]{1,0:T(8,128)(2,1)S(1)}, u32[]{:S(2)}, u32[]{:S(2)}) %collective-permute-start.13) | collective-permute-done | bytes 524320 | tf_op jit(solution)/shard_map/ppermute | solution.py:20
  52.7 3.3 %shard_map.103 = (f32[256,1024]{1,0:T(8,128)S(1)}, f32[256,1024]{1,0:T(8,128)S(1)}, f32[256,1024]{1,0:T(8,128)S(1)}, f32[256,1024]{1,0:T(8,128)S(1)}) custom-call(bf16[256,1024]{1,0:T(8,128)(2,1)S(1)} %collective-permute-done.12.refs_0_, bf16[256,1024]{1,0:T(8,128)(2,1)S(1)} %collective-permute-done.4.refs_1_, ...), custom_call_target="tpu_custom_call" | custom-call | flops 1879048192 | bytes 1048576 | tf_op jit(solution)/shard_map/pallas_call | solution.py:177
  56.0 1.1 %shard_map.104 = (bf16[256,1024]{1,0:T(8,128)(2,1)S(1)}, bf16[256,1024]{1,0:T(8,128)(2,1)S(1)}, bf16[256,1024]{1,0:T(8,128)(2,1)S(1)}, bf16[256,1024]{1,0:T(8,128)(2,1)S(1)}) custom-call(bf16[256,1024]{1,0:T(8,128)(2,1)S(1)} %collective-permute-done.12.refs_0_, bf16[256,1024]{1,0:T(8,128)(2,1)S(1)} %collective-permute-done.4.refs_1_, ...), custom_call_target="tpu_custom_call" | custom-call | flops 268435456 | bytes 1048576 | tf_op jit(solution)/shard_map/pallas_call | solution.py:208
  57.1 0.8 %shard_map.109 = bf16[256,768]{1,0:T(8,128)(2,1)S(1)} custom-call(bf16[256,1024]{1,0:T(8,128)(2,1)S(1)} %get-tuple-element.52.refs_0_, bf16[128,1024]{1,0:T(8,128)(2,1)S(1)} %copy-done.2, bf16[256,1024]{1,0:T(8,128)(2,1)S(1)} %collective-permute-done.8.refs_5_.refs_2_, bf16[256,1024]{1,0:T(8,128)(2,1)S(1)} %collective-permute-done.13.refs_3_, ...), custom_call_target="tpu_custom_call" | custom-call | flops 402653184 | bytes 6291456 | tf_op jit(solution)/shard_map/pallas_call | solution.py:236
  57.9 0.1 collective-permute-start.17
  58.0 0.8 %shard_map.114 = bf16[256,768]{1,0:T(8,128)(2,1)S(1)} custom-call(bf16[256,1024]{1,0:T(8,128)(2,1)S(1)} %get-tuple-element.50.refs_0_, bf16[128,1024]{1,0:T(8,128)(2,1)S(1)} %copy-done.2, bf16[256,1024]{1,0:T(8,128)(2,1)S(1)} %collective-permute-done.8.refs_5_.refs_2_, bf16[256,1024]{1,0:T(8,128)(2,1)S(1)} %collective-permute-done.13.refs_3_, ...), custom_call_target="tpu_custom_call" | custom-call | flops 402653184 | bytes 6291456 | tf_op jit(solution)/shard_map/pallas_call | solution.py:236
  58.9 0.6 collective-permute-start.20
  59.4 0.8 %shard_map.108.one_ref = bf16[256,768]{1,0:T(8,128)(2,1)S(1)} custom-call(bf16[256,1024]{1,0:T(8,128)(2,1)S(1)} %get-tuple-element.51.refs_0_, bf16[128,1024]{1,0:T(8,128)(2,1)S(1)} %copy-done.2, bf16[256,1024]{1,0:T(8,128)(2,1)S(1)} %collective-permute-done.8.refs_5_.refs_2_, bf16[256,1024]{1,0:T(8,128)(2,1)S(1)} %collective-permute-done.13.refs_3_, ...), custom_call_target="tpu_custom_call" | custom-call | flops 402653184 | bytes 6291456 | tf_op jit(solution)/shard_map/pallas_call | solution.py:236
  60.3 0.1 shard_map.110
  60.4 1.6 %collective-permute-start.21 = (bf16[256,768]{1,0:T(8,128)(2,1)S(1)}, bf16[256,768]{1,0:T(8,128)(2,1)S(1)}, u32[]{:S(2)}, u32[]{:S(2)}) collective-permute-start(bf16[256,768]{1,0:T(8,128)(2,1)S(1)} %shard_map.110), channel_id=1, source_target_pairs={{0,16},{8,24},{16,0},{24,8},{1,17},{9,25},{17,1},{25,9},{2,18},{10... | collective-permute-start | bytes 1179656 | tf_op jit(solution)/shard_map/ppermute | solution.py:25
  62.0 6.0 %collective-permute-done.15.refs_1_ = bf16[256,1024]{1,0:T(8,128)(2,1)S(1)} collective-permute-done((bf16[256,1024]{1,0:T(8,128)(2,1)S(1)}, bf16[256,1024]{1,0:T(8,128)(2,1)S(1)}, u32[]{:S(2)}, u32[]{:S(2)}) %collective-permute-start.15) | collective-permute-done | bytes 524320 | tf_op jit(solution)/shard_map/ppermute | solution.py:20
  68.0 0.3 shard_map.111
  68.4 0.3 shard_map.106
  68.8 0.6 collective-permute-start.16
  69.3 0.3 shard_map.107.one_ref
  69.7 0.1 collective-permute-done.18.two_ref
  69.8 1.6 %collective-permute-start.19 = (bf16[256,256]{1,0:T(8,128)(2,1)S(1)}, bf16[256,256]{1,0:T(8,128)(2,1)S(1)}, u32[]{:S(2)}, u32[]{:S(2)}) collective-permute-start(bf16[256,256]{1,0:T(8,128)(2,1)S(1)} %shard_map.112), channel_id=1, source_target_pairs={{0,16},{8,24},{16,0},{24,8},{1,17},{9,25},{17,1},{25,9},{2,18},{10... | collective-permute-start | bytes 393224 | tf_op jit(solution)/shard_map/ppermute | solution.py:25
  71.4 0.3 shard_map.105.one_ref
  71.7 0.8 %shard_map.113.one_ref = bf16[256,768]{1,0:T(8,128)(2,1)S(1)} custom-call(bf16[256,1024]{1,0:T(8,128)(2,1)S(1)} %get-tuple-element.49.refs_0_, bf16[128,1024]{1,0:T(8,128)(2,1)S(1)} %copy-done.2, bf16[256,1024]{1,0:T(8,128)(2,1)S(1)} %collective-permute-done.8.refs_5_.refs_2_, bf16[256,1024]{1,0:T(8,128)(2,1)S(1)} %collective-permute-done.13.refs_3_, ...), custom_call_target="tpu_custom_call" | custom-call | flops 402653184 | bytes 6291456 | tf_op jit(solution)/shard_map/pallas_call | solution.py:236
  72.6 0.6 copy-done.4
  73.3 1.5 %shard_map.115.refs_0_ = bf16[256,1024]{1,0:T(8,128)(2,1)} custom-call(s32[8]{0:T(128)S(1)} %stack.35.order_ref, bf16[256,1024]{1,0:T(8,128)(2,1)S(1)} %bitcast.16, bf16[256,768]{1,0:T(8,128)(2,1)S(1)} %shard_map.113.one_ref, bf16[256,768]{1,0:T(8,128)(2,1)S(1)} %collective-permute-done.20.two_ref, bf16[256,768]{1,0:T(8,128)(2,1)S(1)} %collective-permute-done.21.far_ref, ...), custom_call_target="tpu_custom_call" | custom-call | tf_op jit(solution)/shard_map/pallas_call | solution.py:288
  74.8 0.6 collective-permute-done.19.far_ref
  75.4 1.3 %shard_map.116 = bf16[256,1024]{1,0:T(8,128)(2,1)} custom-call(s32[8]{0:T(128)S(1)} %stack.35.order_ref, bf16[256,1024]{1,0:T(8,128)(2,1)S(1)} %bitcast.17, bf16[256,256]{1,0:T(8,128)(2,1)S(1)} %shard_map.105.one_ref, bf16[256,256]{1,0:T(8,128)(2,1)S(1)} %collective-permute-done.16.two_ref, ...), custom_call_target="tpu_custom_call", output_to_operand_aliasing={{}: (7, {})} | custom-call | tf_op jit(solution)/shard_map/pallas_call | solution.py:288
  (41 shorter events, 0.3 us)
Async XLA Ops:
  0.0 1.0 %copy-start = (bf16[32,8,1024]{2,1,0:T(8,128)(2,1)S(1)}, bf16[32,8,1024]{2,1,0:T(8,128)(2,1)}, u32[]{:S(2)}) copy-start(bf16[32,8,1024]{2,1,0:T(8,128)(2,1)} %mid_ref.5) | copy-start | bytes 1572868
  1.0 6.5 %copy-start.3 = (bf16[128,1024]{1,0:T(8,128)(2,1)S(1)}, bf16[128,1024]{1,0:T(8,128)(2,1)}, u32[]{:S(2)}) copy-start(bf16[128,1024]{1,0:T(8,128)(2,1)} %refs_4_.1) | copy-start | bytes 786436
  1.5 11.9 %collective-permute-start = (bf16[3,32,1024]{2,1,0:T(8,128)(2,1)S(1)}, bf16[3,32,1024]{2,1,0:T(8,128)(2,1)S(1)}, u32[]{:S(2)}, u32[]{:S(2)}) collective-permute-start(bf16[3,32,1024]{2,1,0:T(8,128)(2,1)S(1)} %get-tuple-element.30), channel_id=1, source_target_pairs={{0,1},{1,2},{2,3},{3,4},{4,5},{5,6},{6,7},{7,0},{8,9},{9,10},{10,1... | collective-permute-start | bytes 589832 | tf_op jit(solution)/shard_map/ppermute | solution.py:343
  4.4 3.8 %copy-start.2 = (bf16[128,1024]{1,0:T(8,128)(2,1)S(1)}, bf16[128,1024]{1,0:T(8,128)(2,1)}, u32[]{:S(2)}) copy-start(bf16[128,1024]{1,0:T(8,128)(2,1)} %refs_1_.7) | copy-start | bytes 786436
  4.4 10.9 %collective-permute-start.1 = (bf16[3,32,1024]{2,1,0:T(8,128)(2,1)S(1)}, bf16[3,32,1024]{2,1,0:T(8,128)(2,1)S(1)}, u32[]{:S(2)}, u32[]{:S(2)}) collective-permute-start(bf16[3,32,1024]{2,1,0:T(8,128)(2,1)S(1)} %get-tuple-element.31), channel_id=1, source_target_pairs={{1,0},{2,1},{3,2},{4,3},{5,4},{6,5},{7,6},{0,7},{9,8},{10,9},{11,1... | collective-permute-start | bytes 589832 | tf_op jit(solution)/shard_map/ppermute | solution.py:344
  7.6 13.4 %collective-permute-start.5 = (bf16[128,1024]{1,0:T(8,128)(2,1)S(1)}, bf16[128,1024]{1,0:T(8,128)(2,1)S(1)}, u32[]{:S(2)}, u32[]{:S(2)}) collective-permute-start(bf16[128,1024]{1,0:T(8,128)(2,1)S(1)} %copy-done.3), channel_id=1, source_target_pairs={{0,2},{1,3},{2,4},{3,5},{4,6},{5,7},{6,0},{7,1},{8,10},{9,11},{10,... | collective-permute-start | bytes 786440 | tf_op jit(solution)/shard_map/ppermute | solution.py:20
  9.0 13.4 %copy-start.1 = (bf16[32,8,1024]{2,1,0:T(8,128)(2,1)S(1)}, bf16[32,8,1024]{2,1,0:T(8,128)(2,1)}, u32[]{:S(2)}) copy-start(bf16[32,8,1024]{2,1,0:T(8,128)(2,1)} %mid_ref.5) | copy-start | bytes 1572868
  9.0 22.1 %collective-permute-start.10 = (bf16[256,1024]{1,0:T(8,128)(2,1)}, bf16[256,1024]{1,0:T(8,128)(2,1)S(1)}, u32[]{:S(2)}, u32[]{:S(2)}) collective-permute-start(bf16[256,1024]{1,0:T(8,128)(2,1)} %constant_dynamic-update-slice_fusion), channel_id=1, source_target_pairs={{0,6},{1,7},{2,0},{3,1},{4,2},{5,3},{6,4},{7,5},{8,14},{9,15},{10,... | collective-permute-start | bytes 1572872 | tf_op jit(solution)/shard_map/ppermute | solution.py:20
  13.4 23.0 %collective-permute-start.8 = (bf16[256,1024]{1,0:T(8,128)(2,1)}, bf16[256,1024]{1,0:T(8,128)(2,1)S(1)}, u32[]{:S(2)}, u32[]{:S(2)}) collective-permute-start(bf16[256,1024]{1,0:T(8,128)(2,1)} %constant_dynamic-update-slice_fusion), channel_id=1, source_target_pairs={{0,1},{1,0},{2,3},{3,2},{4,5},{5,4},{6,7},{7,6},{8,9},{9,8},{10,11... | collective-permute-start | bytes 1572872 | tf_op jit(solution)/shard_map/ppermute | solution.py:25
  15.5 6.7 %copy-start.10 = (bf16[7,7,1024]{2,1,0:T(8,128)(2,1)S(1)}, bf16[7,7,1024]{2,1,0:T(8,128)(2,1)}, u32[]{:S(2)}) copy-start(bf16[7,7,1024]{2,1,0:T(8,128)(2,1)} %param.11) | copy-start | bytes 301060
  15.5 5.4 %collective-permute-start.2 = (bf16[48,1024]{1,0:T(8,128)(2,1)S(1)}, bf16[48,1024]{1,0:T(8,128)(2,1)S(1)}, u32[]{:S(2)}, u32[]{:S(2)}) collective-permute-start(bf16[48,1024]{1,0:T(8,128)(2,1)S(1)} %get-tuple-element.32), channel_id=1, source_target_pairs={{0,8},{8,16},{16,24},{1,9},{9,17},{17,25},{2,10},{10,18},{18,26},{... | collective-permute-start | bytes 294920 | tf_op jit(solution)/shard_map/ppermute | solution.py:346
  17.0 4.9 %collective-permute-start.3 = (bf16[48,1024]{1,0:T(8,128)(2,1)S(1)}, bf16[48,1024]{1,0:T(8,128)(2,1)S(1)}, u32[]{:S(2)}, u32[]{:S(2)}) collective-permute-start(bf16[48,1024]{1,0:T(8,128)(2,1)S(1)} %get-tuple-element.33), channel_id=1, source_target_pairs={{8,0},{16,8},{24,16},{9,1},{17,9},{25,17},{10,2},{18,10},{26,18},{... | collective-permute-start | bytes 294920 | tf_op jit(solution)/shard_map/ppermute | solution.py:347
  21.0 15.4 %collective-permute-start.7 = (bf16[128,1024]{1,0:T(8,128)(2,1)S(1)}, bf16[128,1024]{1,0:T(8,128)(2,1)S(1)}, u32[]{:S(2)}, u32[]{:S(2)}) collective-permute-start(bf16[128,1024]{1,0:T(8,128)(2,1)S(1)} %collective-permute-done.5.refs_6_), channel_id=1, source_target_pairs={{0,2},{1,3},{2,4},{3,5},{4,6},{5,7},{6,0},{7,1},{8,10},{9,11},{10,... | collective-permute-start | bytes 786440 | tf_op jit(solution)/shard_map/ppermute | solution.py:20
  21.9 14.5 %collective-permute-start.6 = (bf16[128,1024]{1,0:T(8,128)(2,1)S(1)}, bf16[128,1024]{1,0:T(8,128)(2,1)}, u32[]{:S(2)}, u32[]{:S(2)}) collective-permute-start(bf16[128,1024]{1,0:T(8,128)(2,1)S(1)} %collective-permute-done.5.refs_6_), channel_id=1, source_target_pairs={{0,1},{1,0},{2,3},{3,2},{4,5},{5,4},{6,7},{7,6},{8,9},{9,8},{10,11... | collective-permute-start | bytes 786440 | tf_op jit(solution)/shard_map/ppermute | solution.py:25
  22.3 0.7 copy-start.8
  22.3 0.7 copy-start.6
  22.3 0.7 copy-start.7
  28.0 15.0 %collective-permute-start.4 = (bf16[256,1024]{1,0:T(8,128)(2,1)S(1)}, bf16[256,1024]{1,0:T(8,128)(2,1)S(1)}, u32[]{:S(2)}, u32[]{:S(2)}) collective-permute-start(bf16[256,1024]{1,0:T(8,128)(2,1)S(1)} %shard_map.102.refs_3_), channel_id=1, source_target_pairs={{0,16},{8,24},{16,0},{24,8},{1,17},{9,25},{17,1},{25,9},{2,18},{10... | collective-permute-start | bytes 1572872 | tf_op jit(solution)/shard_map/ppermute | solution.py:25
  31.1 14.1 %collective-permute-start.11 = (bf16[256,1024]{1,0:T(8,128)(2,1)S(1)}, bf16[256,1024]{1,0:T(8,128)(2,1)S(1)}, u32[]{:S(2)}, u32[]{:S(2)}) collective-permute-start(bf16[256,1024]{1,0:T(8,128)(2,1)S(1)} %collective-permute-done.10.refs_8_.refs_4_), channel_id=1, source_target_pairs={{0,1},{1,0},{2,3},{3,2},{4,5},{5,4},{6,7},{7,6},{8,9},{9,8},{10,11... | collective-permute-start | bytes 1572872 | tf_op jit(solution)/shard_map/ppermute | solution.py:25
  36.4 8.8 %collective-permute-start.9 = (bf16[256,1024]{1,0:T(8,128)(2,1)S(1)}, bf16[256,1024]{1,0:T(8,128)(2,1)S(1)}, u32[]{:S(2)}, u32[]{:S(2)}) collective-permute-start(bf16[256,1024]{1,0:T(8,128)(2,1)S(1)} %shard_map.102.refs_3_), channel_id=1, source_target_pairs={{0,8},{8,0},{16,24},{24,16},{1,9},{9,1},{17,25},{25,17},{2,10},{10... | collective-permute-start | bytes 1572872 | tf_op jit(solution)/shard_map/ppermute | solution.py:25
  36.4 16.2 %copy-start.9 = (f32[1024]{0:T(1024)S(1)}, f32[1024]{0:T(1024)}, u32[]{:S(2)}) copy-start(f32[1024]{0:T(1024)} %param.16) | copy-start | bytes 12292
  36.5 16.2 %collective-permute-start.13 = (bf16[256,1024]{1,0:T(8,128)(2,1)S(1)}, bf16[256,1024]{1,0:T(8,128)(2,1)S(1)}, u32[]{:S(2)}, u32[]{:S(2)}) collective-permute-start(bf16[256,1024]{1,0:T(8,128)(2,1)S(1)} %pad_maximum_fusion), channel_id=1, source_target_pairs={{0,2},{1,3},{2,4},{3,5},{4,6},{5,7},{6,0},{7,1},{8,10},{9,11},{10,... | collective-permute-start | bytes 1572872 | tf_op jit(solution)/shard_map/ppermute | solution.py:20
  45.2 7.4 %collective-permute-start.12 = (bf16[256,1024]{1,0:T(8,128)(2,1)S(1)}, bf16[256,1024]{1,0:T(8,128)(2,1)S(1)}, u32[]{:S(2)}, u32[]{:S(2)}) collective-permute-start(bf16[256,1024]{1,0:T(8,128)(2,1)S(1)} %collective-permute-done.4.refs_1_), channel_id=1, source_target_pairs={{0,8},{8,0},{16,24},{24,16},{1,9},{9,1},{17,25},{25,17},{2,10},{10... | collective-permute-start | bytes 1572872 | tf_op jit(solution)/shard_map/ppermute | solution.py:25
  45.2 10.8 %collective-permute-start.14 = (bf16[128,1024]{1,0:T(8,128)(2,1)S(1)}, bf16[128,1024]{1,0:T(8,128)(2,1)S(1)}, u32[]{:S(2)}, u32[]{:S(2)}) collective-permute-start(bf16[128,1024]{1,0:T(8,128)(2,1)S(1)} %collective-permute-done.7.refs_10_), channel_id=1, source_target_pairs={{0,1},{1,0},{2,3},{3,2},{4,5},{5,4},{6,7},{7,6},{8,9},{9,8},{10,11... | collective-permute-start | bytes 786440 | tf_op jit(solution)/shard_map/ppermute | solution.py:25
  52.7 15.3 %collective-permute-start.15 = (bf16[256,1024]{1,0:T(8,128)(2,1)S(1)}, bf16[256,1024]{1,0:T(8,128)(2,1)S(1)}, u32[]{:S(2)}, u32[]{:S(2)}) collective-permute-start(bf16[256,1024]{1,0:T(8,128)(2,1)S(1)} %collective-permute-done.13.refs_3_), channel_id=1, source_target_pairs={{0,2},{1,3},{2,4},{3,5},{4,6},{5,7},{6,0},{7,1},{8,10},{9,11},{10,... | collective-permute-start | bytes 1572872 | tf_op jit(solution)/shard_map/ppermute | solution.py:20
  57.9 2.3 %collective-permute-start.17 = (bf16[256,768]{1,0:T(8,128)(2,1)S(1)}, bf16[256,768]{1,0:T(8,128)(2,1)S(1)}, u32[]{:S(2)}, u32[]{:S(2)}) collective-permute-start(bf16[256,768]{1,0:T(8,128)(2,1)S(1)} %shard_map.109), channel_id=1, source_target_pairs={{0,8},{8,0},{16,24},{24,16},{1,9},{9,1},{17,25},{25,17},{2,10},{10... | collective-permute-start | bytes 1179656 | tf_op jit(solution)/shard_map/ppermute | solution.py:25
  58.9 13.7 %collective-permute-start.20 = (bf16[256,768]{1,0:T(8,128)(2,1)S(1)}, bf16[256,768]{1,0:T(8,128)(2,1)S(1)}, u32[]{:S(2)}, u32[]{:S(2)}) collective-permute-start(bf16[256,768]{1,0:T(8,128)(2,1)S(1)} %shard_map.114), channel_id=1, source_target_pairs={{0,8},{8,0},{16,24},{24,16},{1,9},{9,1},{17,25},{25,17},{2,10},{10... | collective-permute-start | bytes 1179656 | tf_op jit(solution)/shard_map/ppermute | solution.py:25
  60.4 12.2 %collective-permute-start.21 = (bf16[256,768]{1,0:T(8,128)(2,1)S(1)}, bf16[256,768]{1,0:T(8,128)(2,1)S(1)}, u32[]{:S(2)}, u32[]{:S(2)}) collective-permute-start(bf16[256,768]{1,0:T(8,128)(2,1)S(1)} %shard_map.110), channel_id=1, source_target_pairs={{0,16},{8,24},{16,0},{24,8},{1,17},{9,25},{17,1},{25,9},{2,18},{10... | collective-permute-start | bytes 1179656 | tf_op jit(solution)/shard_map/ppermute | solution.py:25
  68.3 1.4 %collective-permute-start.18 = (bf16[256,256]{1,0:T(8,128)(2,1)S(1)}, bf16[256,256]{1,0:T(8,128)(2,1)S(1)}, u32[]{:S(2)}, u32[]{:S(2)}) collective-permute-start(bf16[256,256]{1,0:T(8,128)(2,1)S(1)} %shard_map.111), channel_id=1, source_target_pairs={{0,8},{8,0},{16,24},{24,16},{1,9},{9,1},{17,25},{25,17},{2,10},{10... | collective-permute-start | bytes 393224 | tf_op jit(solution)/shard_map/ppermute | solution.py:25
  68.8 6.0 %collective-permute-start.16 = (bf16[256,256]{1,0:T(8,128)(2,1)S(1)}, bf16[256,256]{1,0:T(8,128)(2,1)S(1)}, u32[]{:S(2)}, u32[]{:S(2)}) collective-permute-start(bf16[256,256]{1,0:T(8,128)(2,1)S(1)} %shard_map.106), channel_id=1, source_target_pairs={{0,8},{8,0},{16,24},{24,16},{1,9},{9,1},{17,25},{25,17},{2,10},{10... | collective-permute-start | bytes 393224 | tf_op jit(solution)/shard_map/ppermute | solution.py:25
  69.8 5.6 %collective-permute-start.19 = (bf16[256,256]{1,0:T(8,128)(2,1)S(1)}, bf16[256,256]{1,0:T(8,128)(2,1)S(1)}, u32[]{:S(2)}, u32[]{:S(2)}) collective-permute-start(bf16[256,256]{1,0:T(8,128)(2,1)S(1)} %shard_map.112), channel_id=1, source_target_pairs={{0,16},{8,24},{16,0},{24,8},{1,17},{9,25},{17,1},{25,9},{2,18},{10... | collective-permute-start | bytes 393224 | tf_op jit(solution)/shard_map/ppermute | solution.py:25
  71.7 0.9 %copy-start.5 = (f32[1024]{0:T(1024)S(1)}, f32[1024]{0:T(1024)}, u32[]{:S(2)}) copy-start(f32[1024]{0:T(1024)} %param.19) | copy-start | bytes 12292
  72.6 0.7 copy-start.4

commit v6 on v5

--- a/solution.py
+++ b/solution.py
@@ -369,14 +369,14 @@
         arrived_a = swap(far_a, "lat", 2)
         near_bes_a, = down([hid_beside], down_a)
         near_in_a = swap(near_bes_a, "lat", 1)
-        near_own_a, = down([hid_own], down_a)
         down_b = [(dz2, 0, 2 * LANES)]
         far_opp_b, = down([hid_opposite], down_b)
         far_acr_b, = down([hid_across], down_b)
         far_in_b = swap(far_opp_b, "lat", 1)
         far_b = add(after(far_acr_b, far_a), far_in_b)
+        near_own_a, = down([after(hid_own, far_b)], down_a)
         arrived_b = swap(after(far_b, far_opp_a), "lat", 2)
-        near_bes_b, = down([hid_beside], down_b)
+        near_bes_b, = down([after(hid_beside, far_b)], down_b)
         near_in_b = swap(near_bes_b, "lat", 1)
         near_own_b, = down([hid_own], down_b)
         groups = [(near_own_a, near_in_a, arrived_a), (near_own_b, near_in_b, arrived_b)]

time: 77 us -> 77 us (level)
  no operation moved by 1% of the time
where the time goes in v6:
time: 77 us; the launch traced here: 76.7 us
  waiting for transfers between devices  28.3 us (37%)
  starting transfers between devices  26.5 us (34%)
  Pallas kernels  17.6 us (23%)
  local copies, waits for them, and re-layouts  3.92 us (5%)
    ppermute x5, waiting for transfers between devices, shift(): lax.ppermute(value, axis, [(i, (i + step * inner) % count) for i in range...  18 us
    ppermute x13, starting transfers between devices, swap(): return lax.ppermute(value, axis, [(i, i ^ bit) for i in range(count)])  12.7 us
    ppermute x13, waiting for transfers between devices, swap(): return lax.ppermute(value, axis, [(i, i ^ bit) for i in range(count)])  8.82 us
    pallas_call x1, Pallas kernels, conv_norm(): pl.pallas_call(conv_kernel, out_shape=jax.ShapeDtypeStruct((rows * cols,...  4.98 us
    ppermute x5, starting transfers between devices, shift(): lax.ppermute(value, axis, [(i, (i + step * inner) % count) for i in range...  4.97 us
    pallas_call x8, Pallas kernels, down(): pl.pallas_call(functools.partial(down_kernel, len(hidden), spans), out_sh...  4.69 us
    pallas_call x1, Pallas kernels, begin(): pl.pallas_call(functools.partial(begin_kernel, len(pixels), spans), out_s...  3.3 us
    ppermute x1, starting transfers between devices, local(): lax.ppermute(first, 'lon', [((i + 1) % lons, i) for i in range(lons)])  3.11 us
  transfers between devices with their start and end apart: 22, of which 10 were waited for; matrix products, arithmetic and copies ran while one was open for 2% of the time, Pallas kernels for 21%

profile of v6, /device:TPU:0, one launch (start us, length us, event | category | flops | bytes accessed | tf_op | source)
XLA Modules:
  0.0 76.7 jit_solution(9916386657570584764)
XLA Ops:
  0.0 1.0 %copy-done = bf16[32,8,1024]{2,1,0:T(8,128)(2,1)S(1)} copy-done((bf16[32,8,1024]{2,1,0:T(8,128)(2,1)S(1)}, bf16[32,8,1024]{2,1,0:T(8,128)(2,1)}, u32[]{:S(2)}) %copy-start) | copy-done | bytes 524312
  1.0 0.4 shard_map.100
  1.5 3.0 %collective-permute-start = (bf16[3,32,1024]{2,1,0:T(8,128)(2,1)S(1)}, bf16[3,32,1024]{2,1,0:T(8,128)(2,1)S(1)}, u32[]{:S(2)}, u32[]{:S(2)}) collective-permute-start(bf16[3,32,1024]{2,1,0:T(8,128)(2,1)S(1)} %get-tuple-element.32), channel_id=1, source_target_pairs={{0,1},{1,2},{2,3},{3,4},{4,5},{5,6},{6,7},{7,0},{8,9},{9,10},{10,1... | collective-permute-start | bytes 589832 | tf_op jit(solution)/shard_map/ppermute | solution.py:343
  4.4 3.1 %collective-permute-start.1 = (bf16[3,32,1024]{2,1,0:T(8,128)(2,1)S(1)}, bf16[3,32,1024]{2,1,0:T(8,128)(2,1)S(1)}, u32[]{:S(2)}, u32[]{:S(2)}) collective-permute-start(bf16[3,32,1024]{2,1,0:T(8,128)(2,1)S(1)} %get-tuple-element.33), channel_id=1, source_target_pairs={{1,0},{2,1},{3,2},{4,3},{5,4},{6,5},{7,6},{0,7},{9,8},{10,9},{11,1... | collective-permute-start | bytes 589832 | tf_op jit(solution)/shard_map/ppermute | solution.py:344
  7.6 0.7 constant_dynamic-update-slice_fusion.1
  8.3 0.7 constant_dynamic-update-slice_fusion
  9.0 3.8 %collective-permute-start.10 = (bf16[256,1024]{1,0:T(8,128)(2,1)}, bf16[256,1024]{1,0:T(8,128)(2,1)S(1)}, u32[]{:S(2)}, u32[]{:S(2)}) collective-permute-start(bf16[256,1024]{1,0:T(8,128)(2,1)} %constant_dynamic-update-slice_fusion), channel_id=1, source_target_pairs={{0,6},{1,7},{2,0},{3,1},{4,2},{5,3},{6,4},{7,5},{8,14},{9,15},{10,... | collective-permute-start | bytes 1572872 | tf_op jit(solution)/shard_map/ppermute | solution.py:20
  12.8 0.5 collective-permute-done.left_ref
  13.4 1.9 %collective-permute-start.8 = (bf16[256,1024]{1,0:T(8,128)(2,1)}, bf16[256,1024]{1,0:T(8,128)(2,1)S(1)}, u32[]{:S(2)}, u32[]{:S(2)}) collective-permute-start(bf16[256,1024]{1,0:T(8,128)(2,1)} %constant_dynamic-update-slice_fusion), channel_id=1, source_target_pairs={{0,1},{1,0},{2,3},{3,2},{4,5},{5,4},{6,7},{7,6},{8,9},{9,8},{10,11... | collective-permute-start | bytes 1572872 | tf_op jit(solution)/shard_map/ppermute | solution.py:25
  15.3 0.2 shard_map.101
  15.5 1.4 %collective-permute-start.2 = (bf16[48,1024]{1,0:T(8,128)(2,1)S(1)}, bf16[48,1024]{1,0:T(8,128)(2,1)S(1)}, u32[]{:S(2)}, u32[]{:S(2)}) collective-permute-start(bf16[48,1024]{1,0:T(8,128)(2,1)S(1)} %get-tuple-element.34), channel_id=1, source_target_pairs={{0,8},{8,16},{16,24},{1,9},{9,17},{17,25},{2,10},{10,18},{18,26},{... | collective-permute-start | bytes 294920 | tf_op jit(solution)/shard_map/ppermute | solution.py:346
  17.0 1.3 %collective-permute-start.3 = (bf16[48,1024]{1,0:T(8,128)(2,1)S(1)}, bf16[48,1024]{1,0:T(8,128)(2,1)S(1)}, u32[]{:S(2)}, u32[]{:S(2)}) collective-permute-start(bf16[48,1024]{1,0:T(8,128)(2,1)S(1)} %get-tuple-element.35), channel_id=1, source_target_pairs={{8,0},{16,8},{24,16},{9,1},{17,9},{25,17},{10,2},{18,10},{26,18},{... | collective-permute-start | bytes 294920 | tf_op jit(solution)/shard_map/ppermute | solution.py:347
  18.3 2.7 %collective-permute-done.5.refs_6_ = bf16[128,1024]{1,0:T(8,128)(2,1)S(1)} collective-permute-done((bf16[128,1024]{1,0:T(8,128)(2,1)S(1)}, bf16[128,1024]{1,0:T(8,128)(2,1)S(1)}, u32[]{:S(2)}, u32[]{:S(2)}) %collective-permute-start.5) | collective-permute-done | bytes 262176 | tf_op jit(solution)/shard_map/ppermute | solution.py:20
  21.0 0.9 %collective-permute-done.3.high_ref = bf16[48,1024]{1,0:T(8,128)(2,1)S(1)} collective-permute-done((bf16[48,1024]{1,0:T(8,128)(2,1)S(1)}, bf16[48,1024]{1,0:T(8,128)(2,1)S(1)}, u32[]{:S(2)}, u32[]{:S(2)}) %collective-permute-start.3) | collective-permute-done | bytes 98336 | tf_op jit(solution)/shard_map/ppermute | solution.py:347
  21.9 0.3 collective-permute-start.6
  22.3 0.1 stack.35.order_ref
  22.4 0.6 copy-done.8
  23.0 5.0 %shard_map.102.refs_3_ = bf16[256,1024]{1,0:T(8,128)(2,1)S(1)} custom-call(s32[8]{0:T(128)S(1)} %stack.35.order_ref, bf16[32,8,1024]{2,1,0:T(8,128)(2,1)S(1)} %copy-done.1, bf16[48,1024]{1,0:T(8,128)(2,1)S(1)} %collective-permute-done.2.low_ref, bf16[48,1024]{1,0:T(8,128)(2,1)S(1)} %collective-permute-done.3.high_ref, ...), custom_call_target="tpu_custom_call" | custom-call | flops 26214400 | bytes 2097152 | tf_op jit(solution)/shard_map/pallas_call | solution.py:137
  28.0 3.1 %collective-permute-start.4 = (bf16[256,1024]{1,0:T(8,128)(2,1)S(1)}, bf16[256,1024]{1,0:T(8,128)(2,1)S(1)}, u32[]{:S(2)}, u32[]{:S(2)}) collective-permute-start(bf16[256,1024]{1,0:T(8,128)(2,1)S(1)} %shard_map.102.refs_3_), channel_id=1, source_target_pairs={{0,16},{8,24},{16,0},{24,8},{1,17},{9,25},{17,1},{25,9},{2,18},{10... | collective-permute-start | bytes 1572872 | tf_op jit(solution)/shard_map/ppermute | solution.py:25
  31.1 1.7 %collective-permute-start.11 = (bf16[256,1024]{1,0:T(8,128)(2,1)S(1)}, bf16[256,1024]{1,0:T(8,128)(2,1)S(1)}, u32[]{:S(2)}, u32[]{:S(2)}) collective-permute-start(bf16[256,1024]{1,0:T(8,128)(2,1)S(1)} %collective-permute-done.10.refs_8_.refs_4_), channel_id=1, source_target_pairs={{0,1},{1,0},{2,3},{3,2},{4,5},{5,4},{6,7},{7,6},{8,9},{9,8},{10,11... | collective-permute-start | bytes 1572872 | tf_op jit(solution)/shard_map/ppermute | solution.py:25
  32.8 3.6 %collective-permute-done.7.refs_10_ = bf16[128,1024]{1,0:T(8,128)(2,1)S(1)} collective-permute-done((bf16[128,1024]{1,0:T(8,128)(2,1)S(1)}, bf16[128,1024]{1,0:T(8,128)(2,1)S(1)}, u32[]{:S(2)}, u32[]{:S(2)}) %collective-permute-start.7) | collective-permute-done | bytes 262176 | tf_op jit(solution)/shard_map/ppermute | solution.py:20
  36.5 1.1 %collective-permute-start.13 = (bf16[256,1024]{1,0:T(8,128)(2,1)S(1)}, bf16[256,1024]{1,0:T(8,128)(2,1)S(1)}, u32[]{:S(2)}, u32[]{:S(2)}) collective-permute-start(bf16[256,1024]{1,0:T(8,128)(2,1)S(1)} %pad_maximum_fusion), channel_id=1, source_target_pairs={{0,2},{1,3},{2,4},{3,5},{4,6},{5,7},{6,0},{7,1},{8,10},{9,11},{10,... | collective-permute-start | bytes 1572872 | tf_op jit(solution)/shard_map/ppermute | solution.py:20
  37.6 5.3 %collective-permute-done.4.refs_1_ = bf16[256,1024]{1,0:T(8,128)(2,1)S(1)} collective-permute-done((bf16[256,1024]{1,0:T(8,128)(2,1)S(1)}, bf16[256,1024]{1,0:T(8,128)(2,1)S(1)}, u32[]{:S(2)}, u32[]{:S(2)}) %collective-permute-start.4) | collective-permute-done | bytes 524320 | tf_op jit(solution)/shard_map/ppermute | solution.py:25
  42.9 2.3 %collective-permute-done.11.refs_9_.refs_5_ = bf16[256,1024]{1,0:T(8,128)(2,1)S(1)} collective-permute-done((bf16[256,1024]{1,0:T(8,128)(2,1)S(1)}, bf16[256,1024]{1,0:T(8,128)(2,1)S(1)}, u32[]{:S(2)}, u32[]{:S(2)}) %collective-permute-start.11) | collective-permute-done | bytes 524320 | tf_op jit(solution)/shard_map/ppermute | solution.py:25
  45.2 1.7 %collective-permute-start.14 = (bf16[128,1024]{1,0:T(8,128)(2,1)S(1)}, bf16[128,1024]{1,0:T(8,128)(2,1)S(1)}, u32[]{:S(2)}, u32[]{:S(2)}) collective-permute-start(bf16[128,1024]{1,0:T(8,128)(2,1)S(1)} %collective-permute-done.7.refs_10_), channel_id=1, source_target_pairs={{0,1},{1,0},{2,3},{3,2},{4,5},{5,4},{6,7},{7,6},{8,9},{9,8},{10,11... | collective-permute-start | bytes 786440 | tf_op jit(solution)/shard_map/ppermute | solution.py:25
  46.9 5.7 %collective-permute-done.13.refs_3_ = bf16[256,1024]{1,0:T(8,128)(2,1)S(1)} collective-permute-done((bf16[256,1024]{1,0:T(8,128)(2,1)S(1)}, bf16[256,1024]{1,0:T(8,128)(2,1)S(1)}, u32[]{:S(2)}, u32[]{:S(2)}) %collective-permute-start.13) | collective-permute-done | bytes 524320 | tf_op jit(solution)/shard_map/ppermute | solution.py:20
  52.7 3.3 %shard_map.103 = (f32[256,1024]{1,0:T(8,128)S(1)}, f32[256,1024]{1,0:T(8,128)S(1)}, f32[256,1024]{1,0:T(8,128)S(1)}, f32[256,1024]{1,0:T(8,128)S(1)}) custom-call(bf16[256,1024]{1,0:T(8,128)(2,1)S(1)} %collective-permute-done.12.refs_0_, bf16[256,1024]{1,0:T(8,128)(2,1)S(1)} %collective-permute-done.4.refs_1_, ...), custom_call_target="tpu_custom_call" | custom-call | flops 1879048192 | bytes 1048576 | tf_op jit(solution)/shard_map/pallas_call | solution.py:177
  56.0 1.1 %shard_map.104 = (bf16[256,1024]{1,0:T(8,128)(2,1)S(1)}, bf16[256,1024]{1,0:T(8,128)(2,1)S(1)}, bf16[256,1024]{1,0:T(8,128)(2,1)S(1)}, bf16[256,1024]{1,0:T(8,128)(2,1)S(1)}) custom-call(bf16[256,1024]{1,0:T(8,128)(2,1)S(1)} %collective-permute-done.12.refs_0_, bf16[256,1024]{1,0:T(8,128)(2,1)S(1)} %collective-permute-done.4.refs_1_, ...), custom_call_target="tpu_custom_call" | custom-call | flops 268435456 | bytes 1048576 | tf_op jit(solution)/shard_map/pallas_call | solution.py:208
  57.1 0.8 %shard_map.108 = bf16[256,768]{1,0:T(8,128)(2,1)S(1)} custom-call(bf16[256,1024]{1,0:T(8,128)(2,1)S(1)} %get-tuple-element.54.refs_0_, bf16[128,1024]{1,0:T(8,128)(2,1)S(1)} %copy-done.2, bf16[256,1024]{1,0:T(8,128)(2,1)S(1)} %collective-permute-done.8.refs_5_.refs_2_, bf16[256,1024]{1,0:T(8,128)(2,1)S(1)} %collective-permute-done.13.refs_3_, ...), custom_call_target="tpu_custom_call" | custom-call | flops 402653184 | bytes 6291456 | tf_op jit(solution)/shard_map/pallas_call | solution.py:236
  57.9 0.1 collective-permute-start.16
  58.0 0.8 %shard_map.114 = bf16[256,768]{1,0:T(8,128)(2,1)S(1)} custom-call(bf16[256,1024]{1,0:T(8,128)(2,1)S(1)} %get-tuple-element.56.refs_0_, bf16[128,1024]{1,0:T(8,128)(2,1)S(1)} %copy-done.2, bf16[256,1024]{1,0:T(8,128)(2,1)S(1)} %collective-permute-done.8.refs_5_.refs_2_, bf16[256,1024]{1,0:T(8,128)(2,1)S(1)} %collective-permute-done.13.refs_3_, ...), custom_call_target="tpu_custom_call" | custom-call | flops 402653184 | bytes 6291456 | tf_op jit(solution)/shard_map/pallas_call | solution.py:236
  58.9 0.6 collective-permute-start.20
  59.4 0.8 %shard_map.107.one_ref = bf16[256,768]{1,0:T(8,128)(2,1)S(1)} custom-call(bf16[256,1024]{1,0:T(8,128)(2,1)S(1)} %get-tuple-element.53.refs_0_, bf16[128,1024]{1,0:T(8,128)(2,1)S(1)} %copy-done.2, bf16[256,1024]{1,0:T(8,128)(2,1)S(1)} %collective-permute-done.8.refs_5_.refs_2_, bf16[256,1024]{1,0:T(8,128)(2,1)S(1)} %collective-permute-done.13.refs_3_, ...), custom_call_target="tpu_custom_call" | custom-call | flops 402653184 | bytes 6291456 | tf_op jit(solution)/shard_map/pallas_call | solution.py:236
  60.3 0.1 shard_map.109
  60.4 1.6 %collective-permute-start.21 = (bf16[256,768]{1,0:T(8,128)(2,1)S(1)}, bf16[256,768]{1,0:T(8,128)(2,1)S(1)}, u32[]{:S(2)}, u32[]{:S(2)}) collective-permute-start(bf16[256,768]{1,0:T(8,128)(2,1)S(1)} %shard_map.109), channel_id=1, source_target_pairs={{0,16},{8,24},{16,0},{24,8},{1,17},{9,25},{17,1},{25,9},{2,18},{10... | collective-permute-start | bytes 1179656 | tf_op jit(solution)/shard_map/ppermute | solution.py:25
  62.0 6.0 %collective-permute-done.15.refs_1_ = bf16[256,1024]{1,0:T(8,128)(2,1)S(1)} collective-permute-done((bf16[256,1024]{1,0:T(8,128)(2,1)S(1)}, bf16[256,1024]{1,0:T(8,128)(2,1)S(1)}, u32[]{:S(2)}, u32[]{:S(2)}) %collective-permute-start.15) | collective-permute-done | bytes 524320 | tf_op jit(solution)/shard_map/ppermute | solution.py:20
  68.0 0.3 shard_map.110
  68.4 0.3 shard_map.106.one_ref
  68.8 1.0 %collective-permute-done.17.two_ref = bf16[256,256]{1,0:T(8,128)(2,1)S(1)} collective-permute-done((bf16[256,256]{1,0:T(8,128)(2,1)S(1)}, bf16[256,256]{1,0:T(8,128)(2,1)S(1)}, u32[]{:S(2)}, u32[]{:S(2)}) %collective-permute-start.17) | collective-permute-done | bytes 131104 | tf_op jit(solution)/shard_map/ppermute | solution.py:25
  69.8 1.6 %collective-permute-start.19 = (bf16[256,256]{1,0:T(8,128)(2,1)S(1)}, bf16[256,256]{1,0:T(8,128)(2,1)S(1)}, u32[]{:S(2)}, u32[]{:S(2)}) collective-permute-start(bf16[256,256]{1,0:T(8,128)(2,1)S(1)} %shard_map.111), channel_id=1, source_target_pairs={{0,16},{8,24},{16,0},{24,8},{1,17},{9,25},{17,1},{25,9},{2,18},{10... | collective-permute-start | bytes 393224 | tf_op jit(solution)/shard_map/ppermute | solution.py:25
  71.4 0.3 shard_map.112
  71.7 0.1 collective-permute-start.18
  71.8 0.3 shard_map.105.one_ref
  72.1 0.8 %shard_map.113.one_ref = bf16[256,768]{1,0:T(8,128)(2,1)S(1)} custom-call(bf16[256,1024]{1,0:T(8,128)(2,1)S(1)} %get-tuple-element.58.refs_0_, bf16[128,1024]{1,0:T(8,128)(2,1)S(1)} %copy-done.2, bf16[256,1024]{1,0:T(8,128)(2,1)S(1)} %collective-permute-done.8.refs_5_.refs_2_, bf16[256,1024]{1,0:T(8,128)(2,1)S(1)} %collective-permute-done.13.refs_3_, ...), custom_call_target="tpu_custom_call" | custom-call | flops 402653184 | bytes 6291456 | tf_op jit(solution)/shard_map/pallas_call | solution.py:236
  73.0 0.6 copy-done.4
  73.7 1.5 %shard_map.115.refs_0_ = bf16[256,1024]{1,0:T(8,128)(2,1)} custom-call(s32[8]{0:T(128)S(1)} %stack.35.order_ref, bf16[256,1024]{1,0:T(8,128)(2,1)S(1)} %bitcast.16, bf16[256,768]{1,0:T(8,128)(2,1)S(1)} %shard_map.113.one_ref, bf16[256,768]{1,0:T(8,128)(2,1)S(1)} %collective-permute-done.20.two_ref, bf16[256,768]{1,0:T(8,128)(2,1)S(1)} %collective-permute-done.21.far_ref, ...), custom_call_target="tpu_custom_call" | custom-call | tf_op jit(solution)/shard_map/pallas_call | solution.py:288
  75.2 0.2 collective-permute-done.19.far_ref
  75.4 1.3 %shard_map.116 = bf16[256,1024]{1,0:T(8,128)(2,1)} custom-call(s32[8]{0:T(128)S(1)} %stack.35.order_ref, bf16[256,1024]{1,0:T(8,128)(2,1)S(1)} %bitcast.17, bf16[256,256]{1,0:T(8,128)(2,1)S(1)} %shard_map.105.one_ref, bf16[256,256]{1,0:T(8,128)(2,1)S(1)} %collective-permute-done.18.two_ref, ...), custom_call_target="tpu_custom_call", output_to_operand_aliasing={{}: (7, {})} | custom-call | tf_op jit(solution)/shard_map/pallas_call | solution.py:288
  (41 shorter events, 0.3 us)
Async XLA Ops:
  0.0 1.0 %copy-start = (bf16[32,8,1024]{2,1,0:T(8,128)(2,1)S(1)}, bf16[32,8,1024]{2,1,0:T(8,128)(2,1)}, u32[]{:S(2)}) copy-start(bf16[32,8,1024]{2,1,0:T(8,128)(2,1)} %mid_ref.5) | copy-start | bytes 1572868
  1.0 6.5 %copy-start.3 = (bf16[128,1024]{1,0:T(8,128)(2,1)S(1)}, bf16[128,1024]{1,0:T(8,128)(2,1)}, u32[]{:S(2)}) copy-start(bf16[128,1024]{1,0:T(8,128)(2,1)} %refs_4_.1) | copy-start | bytes 786436
  1.5 11.9 %collective-permute-start = (bf16[3,32,1024]{2,1,0:T(8,128)(2,1)S(1)}, bf16[3,32,1024]{2,1,0:T(8,128)(2,1)S(1)}, u32[]{:S(2)}, u32[]{:S(2)}) collective-permute-start(bf16[3,32,1024]{2,1,0:T(8,128)(2,1)S(1)} %get-tuple-element.32), channel_id=1, source_target_pairs={{0,1},{1,2},{2,3},{3,4},{4,5},{5,6},{6,7},{7,0},{8,9},{9,10},{10,1... | collective-permute-start | bytes 589832 | tf_op jit(solution)/shard_map/ppermute | solution.py:343
  4.4 3.8 %copy-start.2 = (bf16[128,1024]{1,0:T(8,128)(2,1)S(1)}, bf16[128,1024]{1,0:T(8,128)(2,1)}, u32[]{:S(2)}) copy-start(bf16[128,1024]{1,0:T(8,128)(2,1)} %refs_1_.7) | copy-start | bytes 786436
  4.4 10.9 %collective-permute-start.1 = (bf16[3,32,1024]{2,1,0:T(8,128)(2,1)S(1)}, bf16[3,32,1024]{2,1,0:T(8,128)(2,1)S(1)}, u32[]{:S(2)}, u32[]{:S(2)}) collective-permute-start(bf16[3,32,1024]{2,1,0:T(8,128)(2,1)S(1)} %get-tuple-element.33), channel_id=1, source_target_pairs={{1,0},{2,1},{3,2},{4,3},{5,4},{6,5},{7,6},{0,7},{9,8},{10,9},{11,1... | collective-permute-start | bytes 589832 | tf_op jit(solution)/shard_map/ppermute | solution.py:344
  7.6 13.4 %collective-permute-start.5 = (bf16[128,1024]{1,0:T(8,128)(2,1)S(1)}, bf16[128,1024]{1,0:T(8,128)(2,1)S(1)}, u32[]{:S(2)}, u32[]{:S(2)}) collective-permute-start(bf16[128,1024]{1,0:T(8,128)(2,1)S(1)} %copy-done.3), channel_id=1, source_target_pairs={{0,2},{1,3},{2,4},{3,5},{4,6},{5,7},{6,0},{7,1},{8,10},{9,11},{10,... | collective-permute-start | bytes 786440 | tf_op jit(solution)/shard_map/ppermute | solution.py:20
  9.0 13.4 %copy-start.1 = (bf16[32,8,1024]{2,1,0:T(8,128)(2,1)S(1)}, bf16[32,8,1024]{2,1,0:T(8,128)(2,1)}, u32[]{:S(2)}) copy-start(bf16[32,8,1024]{2,1,0:T(8,128)(2,1)} %mid_ref.5) | copy-start | bytes 1572868
  9.0 22.1 %collective-permute-start.10 = (bf16[256,1024]{1,0:T(8,128)(2,1)}, bf16[256,1024]{1,0:T(8,128)(2,1)S(1)}, u32[]{:S(2)}, u32[]{:S(2)}) collective-permute-start(bf16[256,1024]{1,0:T(8,128)(2,1)} %constant_dynamic-update-slice_fusion), channel_id=1, source_target_pairs={{0,6},{1,7},{2,0},{3,1},{4,2},{5,3},{6,4},{7,5},{8,14},{9,15},{10,... | collective-permute-start | bytes 1572872 | tf_op jit(solution)/shard_map/ppermute | solution.py:20
  13.4 23.0 %collective-permute-start.8 = (bf16[256,1024]{1,0:T(8,128)(2,1)}, bf16[256,1024]{1,0:T(8,128)(2,1)S(1)}, u32[]{:S(2)}, u32[]{:S(2)}) collective-permute-start(bf16[256,1024]{1,0:T(8,128)(2,1)} %constant_dynamic-update-slice_fusion), channel_id=1, source_target_pairs={{0,1},{1,0},{2,3},{3,2},{4,5},{5,4},{6,7},{7,6},{8,9},{9,8},{10,11... | collective-permute-start | bytes 1572872 | tf_op jit(solution)/shard_map/ppermute | solution.py:25
  15.5 6.7 %copy-start.10 = (bf16[7,7,1024]{2,1,0:T(8,128)(2,1)S(1)}, bf16[7,7,1024]{2,1,0:T(8,128)(2,1)}, u32[]{:S(2)}) copy-start(bf16[7,7,1024]{2,1,0:T(8,128)(2,1)} %param.11) | copy-start | bytes 301060
  15.5 5.4 %collective-permute-start.2 = (bf16[48,1024]{1,0:T(8,128)(2,1)S(1)}, bf16[48,1024]{1,0:T(8,128)(2,1)S(1)}, u32[]{:S(2)}, u32[]{:S(2)}) collective-permute-start(bf16[48,1024]{1,0:T(8,128)(2,1)S(1)} %get-tuple-element.34), channel_id=1, source_target_pairs={{0,8},{8,16},{16,24},{1,9},{9,17},{17,25},{2,10},{10,18},{18,26},{... | collective-permute-start | bytes 294920 | tf_op jit(solution)/shard_map/ppermute | solution.py:346
  17.0 4.9 %collective-permute-start.3 = (bf16[48,1024]{1,0:T(8,128)(2,1)S(1)}, bf16[48,1024]{1,0:T(8,128)(2,1)S(1)}, u32[]{:S(2)}, u32[]{:S(2)}) collective-permute-start(bf16[48,1024]{1,0:T(8,128)(2,1)S(1)} %get-tuple-element.35), channel_id=1, source_target_pairs={{8,0},{16,8},{24,16},{9,1},{17,9},{25,17},{10,2},{18,10},{26,18},{... | collective-permute-start | bytes 294920 | tf_op jit(solution)/shard_map/ppermute | solution.py:347
  21.0 15.4 %collective-permute-start.7 = (bf16[128,1024]{1,0:T(8,128)(2,1)S(1)}, bf16[128,1024]{1,0:T(8,128)(2,1)S(1)}, u32[]{:S(2)}, u32[]{:S(2)}) collective-permute-start(bf16[128,1024]{1,0:T(8,128)(2,1)S(1)} %collective-permute-done.5.refs_6_), channel_id=1, source_target_pairs={{0,2},{1,3},{2,4},{3,5},{4,6},{5,7},{6,0},{7,1},{8,10},{9,11},{10,... | collective-permute-start | bytes 786440 | tf_op jit(solution)/shard_map/ppermute | solution.py:20
  21.9 14.5 %collective-permute-start.6 = (bf16[128,1024]{1,0:T(8,128)(2,1)S(1)}, bf16[128,1024]{1,0:T(8,128)(2,1)}, u32[]{:S(2)}, u32[]{:S(2)}) collective-permute-start(bf16[128,1024]{1,0:T(8,128)(2,1)S(1)} %collective-permute-done.5.refs_6_), channel_id=1, source_target_pairs={{0,1},{1,0},{2,3},{3,2},{4,5},{5,4},{6,7},{7,6},{8,9},{9,8},{10,11... | collective-permute-start | bytes 786440 | tf_op jit(solution)/shard_map/ppermute | solution.py:25
  22.3 0.7 copy-start.8
  22.3 0.7 copy-start.6
  22.3 0.7 copy-start.7
  28.0 15.0 %collective-permute-start.4 = (bf16[256,1024]{1,0:T(8,128)(2,1)S(1)}, bf16[256,1024]{1,0:T(8,128)(2,1)S(1)}, u32[]{:S(2)}, u32[]{:S(2)}) collective-permute-start(bf16[256,1024]{1,0:T(8,128)(2,1)S(1)} %shard_map.102.refs_3_), channel_id=1, source_target_pairs={{0,16},{8,24},{16,0},{24,8},{1,17},{9,25},{17,1},{25,9},{2,18},{10... | collective-permute-start | bytes 1572872 | tf_op jit(solution)/shard_map/ppermute | solution.py:25
  31.1 14.1 %collective-permute-start.11 = (bf16[256,1024]{1,0:T(8,128)(2,1)S(1)}, bf16[256,1024]{1,0:T(8,128)(2,1)S(1)}, u32[]{:S(2)}, u32[]{:S(2)}) collective-permute-start(bf16[256,1024]{1,0:T(8,128)(2,1)S(1)} %collective-permute-done.10.refs_8_.refs_4_), channel_id=1, source_target_pairs={{0,1},{1,0},{2,3},{3,2},{4,5},{5,4},{6,7},{7,6},{8,9},{9,8},{10,11... | collective-permute-start | bytes 1572872 | tf_op jit(solution)/shard_map/ppermute | solution.py:25
  36.4 8.8 %collective-permute-start.9 = (bf16[256,1024]{1,0:T(8,128)(2,1)S(1)}, bf16[256,1024]{1,0:T(8,128)(2,1)S(1)}, u32[]{:S(2)}, u32[]{:S(2)}) collective-permute-start(bf16[256,1024]{1,0:T(8,128)(2,1)S(1)} %shard_map.102.refs_3_), channel_id=1, source_target_pairs={{0,8},{8,0},{16,24},{24,16},{1,9},{9,1},{17,25},{25,17},{2,10},{10... | collective-permute-start | bytes 1572872 | tf_op jit(solution)/shard_map/ppermute | solution.py:25
  36.4 16.2 %copy-start.9 = (f32[1024]{0:T(1024)S(1)}, f32[1024]{0:T(1024)}, u32[]{:S(2)}) copy-start(f32[1024]{0:T(1024)} %param.16) | copy-start | bytes 12292
  36.5 16.2 %collective-permute-start.13 = (bf16[256,1024]{1,0:T(8,128)(2,1)S(1)}, bf16[256,1024]{1,0:T(8,128)(2,1)S(1)}, u32[]{:S(2)}, u32[]{:S(2)}) collective-permute-start(bf16[256,1024]{1,0:T(8,128)(2,1)S(1)} %pad_maximum_fusion), channel_id=1, source_target_pairs={{0,2},{1,3},{2,4},{3,5},{4,6},{5,7},{6,0},{7,1},{8,10},{9,11},{10,... | collective-permute-start | bytes 1572872 | tf_op jit(solution)/shard_map/ppermute | solution.py:20
  45.2 7.4 %collective-permute-start.12 = (bf16[256,1024]{1,0:T(8,128)(2,1)S(1)}, bf16[256,1024]{1,0:T(8,128)(2,1)S(1)}, u32[]{:S(2)}, u32[]{:S(2)}) collective-permute-start(bf16[256,1024]{1,0:T(8,128)(2,1)S(1)} %collective-permute-done.4.refs_1_), channel_id=1, source_target_pairs={{0,8},{8,0},{16,24},{24,16},{1,9},{9,1},{17,25},{25,17},{2,10},{10... | collective-permute-start | bytes 1572872 | tf_op jit(solution)/shard_map/ppermute | solution.py:25
  45.2 10.8 %collective-permute-start.14 = (bf16[128,1024]{1,0:T(8,128)(2,1)S(1)}, bf16[128,1024]{1,0:T(8,128)(2,1)S(1)}, u32[]{:S(2)}, u32[]{:S(2)}) collective-permute-start(bf16[128,1024]{1,0:T(8,128)(2,1)S(1)} %collective-permute-done.7.refs_10_), channel_id=1, source_target_pairs={{0,1},{1,0},{2,3},{3,2},{4,5},{5,4},{6,7},{7,6},{8,9},{9,8},{10,11... | collective-permute-start | bytes 786440 | tf_op jit(solution)/shard_map/ppermute | solution.py:25
  52.7 15.3 %collective-permute-start.15 = (bf16[256,1024]{1,0:T(8,128)(2,1)S(1)}, bf16[256,1024]{1,0:T(8,128)(2,1)S(1)}, u32[]{:S(2)}, u32[]{:S(2)}) collective-permute-start(bf16[256,1024]{1,0:T(8,128)(2,1)S(1)} %collective-permute-done.13.refs_3_), channel_id=1, source_target_pairs={{0,2},{1,3},{2,4},{3,5},{4,6},{5,7},{6,0},{7,1},{8,10},{9,11},{10,... | collective-permute-start | bytes 1572872 | tf_op jit(solution)/shard_map/ppermute | solution.py:20
  57.9 2.3 %collective-permute-start.16 = (bf16[256,768]{1,0:T(8,128)(2,1)S(1)}, bf16[256,768]{1,0:T(8,128)(2,1)S(1)}, u32[]{:S(2)}, u32[]{:S(2)}) collective-permute-start(bf16[256,768]{1,0:T(8,128)(2,1)S(1)} %shard_map.108), channel_id=1, source_target_pairs={{0,8},{8,0},{16,24},{24,16},{1,9},{9,1},{17,25},{25,17},{2,10},{10... | collective-permute-start | bytes 1179656 | tf_op jit(solution)/shard_map/ppermute | solution.py:25
  58.9 14.1 %collective-permute-start.20 = (bf16[256,768]{1,0:T(8,128)(2,1)S(1)}, bf16[256,768]{1,0:T(8,128)(2,1)S(1)}, u32[]{:S(2)}, u32[]{:S(2)}) collective-permute-start(bf16[256,768]{1,0:T(8,128)(2,1)S(1)} %shard_map.114), channel_id=1, source_target_pairs={{0,8},{8,0},{16,24},{24,16},{1,9},{9,1},{17,25},{25,17},{2,10},{10... | collective-permute-start | bytes 1179656 | tf_op jit(solution)/shard_map/ppermute | solution.py:25
  60.4 12.6 %collective-permute-start.21 = (bf16[256,768]{1,0:T(8,128)(2,1)S(1)}, bf16[256,768]{1,0:T(8,128)(2,1)S(1)}, u32[]{:S(2)}, u32[]{:S(2)}) collective-permute-start(bf16[256,768]{1,0:T(8,128)(2,1)S(1)} %shard_map.109), channel_id=1, source_target_pairs={{0,16},{8,24},{16,0},{24,8},{1,17},{9,25},{17,1},{25,9},{2,18},{10... | collective-permute-start | bytes 1179656 | tf_op jit(solution)/shard_map/ppermute | solution.py:25
  68.3 1.4 %collective-permute-start.17 = (bf16[256,256]{1,0:T(8,128)(2,1)S(1)}, bf16[256,256]{1,0:T(8,128)(2,1)S(1)}, u32[]{:S(2)}, u32[]{:S(2)}) collective-permute-start(bf16[256,256]{1,0:T(8,128)(2,1)S(1)} %shard_map.110), channel_id=1, source_target_pairs={{0,8},{8,0},{16,24},{24,16},{1,9},{9,1},{17,25},{25,17},{2,10},{10... | collective-permute-start | bytes 393224 | tf_op jit(solution)/shard_map/ppermute | solution.py:25
  69.8 5.6 %collective-permute-start.19 = (bf16[256,256]{1,0:T(8,128)(2,1)S(1)}, bf16[256,256]{1,0:T(8,128)(2,1)S(1)}, u32[]{:S(2)}, u32[]{:S(2)}) collective-permute-start(bf16[256,256]{1,0:T(8,128)(2,1)S(1)} %shard_map.111), channel_id=1, source_target_pairs={{0,16},{8,24},{16,0},{24,8},{1,17},{9,25},{17,1},{25,9},{2,18},{10... | collective-permute-start | bytes 393224 | tf_op jit(solution)/shard_map/ppermute | solution.py:25
  71.7 3.7 %collective-permute-start.18 = (bf16[256,256]{1,0:T(8,128)(2,1)S(1)}, bf16[256,256]{1,0:T(8,128)(2,1)S(1)}, u32[]{:S(2)}, u32[]{:S(2)}) collective-permute-start(bf16[256,256]{1,0:T(8,128)(2,1)S(1)} %shard_map.112), channel_id=1, source_target_pairs={{0,8},{8,0},{16,24},{24,16},{1,9},{9,1},{17,25},{25,17},{2,10},{10... | collective-permute-start | bytes 393224 | tf_op jit(solution)/shard_map/ppermute | solution.py:25
  72.1 0.9 %copy-start.5 = (f32[1024]{0:T(1024)S(1)}, f32[1024]{0:T(1024)}, u32[]{:S(2)}) copy-start(f32[1024]{0:T(1024)} %param.19) | copy-start | bytes 12292
  73.0 0.7 copy-start.4
